TPU v7x, 128 devices: a whole 4x4x4 slice. The times are simulated.
128 devices in a mesh: section: 8 (over z_hi, y), ep: 16 (over x, z_lo, core).
Axes of the slice: x: 4, y: 4, z: 4 (z_hi: 2, z_lo: 2; z = z_hi * 2 + z_lo), core: 2. Of those that a mesh axis runs over, the one named last changes fastest.
Arguments:
- pending: bfloat16 [8, 2048, 7168], P('section', 'ep'), may hold values from -6 to 6
- expert_ids: int32 [8, 2048, 2], P('section', 'ep'), may hold values from 0 to 3, all different within a row; in each aligned block of 128 rows (0 to 127, 128 to 255, ..., all dimensions but the last counted through in order) at most 72 rows name the same one
- route_weight: float32 [8, 2048, 2], P('section', 'ep'), may hold values from 0.1 to 0.9
- gate_saved: bfloat16 [8, 1152, 4096], P('section', None, 'ep'), may hold values from -8 to 8
- up_saved: bfloat16 [8, 1152, 4096], P('section', None, 'ep'), may hold values from -8 to 8
- w_gate: bfloat16 [8, 7168, 4096], P('section', None, 'ep'), may hold values from -0.0625 to 0.0625
- w_up: bfloat16 [8, 7168, 4096], P('section', None, 'ep'), may hold values from -0.0625 to 0.0625
- w_down: bfloat16 [8, 4096, 7168], P('section', 'ep'), may hold values from -0.1875 to 0.1875
Outputs:
- upstream: bfloat16 [8, 2048, 7168], P('section', 'ep')
- down_grad: float32 [8, 4096, 7168], P('section', 'ep')
Inputs may be any that keep to these rules, and one draw needn't show every extreme that they name: `expert_ids`: each token names 2 different experts. In each aligned block of 128 tokens (the tokens of one device) no expert is named more than 72 times, and in every draw some block names some expert exactly 72 times.
All inputs are finite; a program needn't handle non-finite values.
Results may differ from a plain program's by a relative error of at most 0.006.
Values may be sent and summed in bfloat16 or wider, within the bound.
No kernel may reach another device: no remote copies, remote signals or barrier semaphores. Data moves between devices by JAX's collectives and lax.ppermute only.
A program may use at most 256 MiB of HBM per device.

v0:
```python
import functools

import jax
import jax.numpy as jnp
from jax import lax
from jax.experimental import pallas as pl
from jax.experimental.pallas import tpu as pltpu
from jax.sharding import PartitionSpec as P

NX, NZ, NC, NY = 4, 2, 2, 4
F32, BF16 = jnp.float32, jnp.bfloat16
PARAMS = pltpu.CompilerParams(vmem_limit_bytes=32 << 20)
LIGHT = pl.CostEstimate(flops=1, bytes_accessed=1, transcendentals=0)
EARLY, LATE = (5, 5), (9, 9)
ONCE_TILE = 768
CONTRACT_LAST = (((1,), (1,)), ((), ()))


def section_move(array, flip):
    sections, peers = lax.axis_size("section"), NX * NZ * NC
    pairs = []
    for s in range(sections):
        for q in range(peers):
            to = q ^ NC if flip(s) else q
            pairs.append((s * peers + q, (s - 1) % sections * peers + to))
    return lax.ppermute(array, ("section", "ep"), pairs)


def ep_move(array, dx=0, dz=0, dc=0):
    pairs = []
    for q in range(NX * NZ * NC):
        x, z, c = q // (NZ * NC), q // NC % NZ, q % NC
        pairs.append((q, (x + dx) % NX * NZ * NC + (z ^ dz) * NC + (c ^ dc)))
    return lax.ppermute(array, "ep", pairs)


def x_moves(blocks, sign):
    return [ep_move(blocks[d], dx=sign * d) for d in range(1, NX)]


def x_exchange(array):
    groups = [[x * NZ * NC + i for x in range(NX)] for i in range(NZ * NC)]
    blocks = array.reshape(NX, -1, array.shape[1])
    moved = lax.all_to_all(blocks, "ep", 0, 0, axis_index_groups=groups, tiled=True)
    return moved.reshape(array.shape)


def whole(shape):
    return pl.BlockSpec(shape, lambda *_: (0,) * len(shape))


def in_hbm(array):
    return pltpu.with_memory_space_constraint(array, pltpu.HBM)


def tile_of(columns):
    return max(t for t in range(128, 897, 128) if columns % t == 0)


def release(value, *after):
    return lax.optimization_barrier((value, after))[0]


def at_once(compute, columns, tiled, fixed, scalars, tiled_out, fixed_out, begin=None):
    n_in, n_fix, n_out = len(tiled), len(fixed), len(tiled_out)
    tile = ONCE_TILE if columns % ONCE_TILE == 0 else tile_of(columns)

    def kernel(*refs):
        ins, fixes, outs = refs[:n_in], refs[n_in : n_in + n_fix], refs[n_in + n_fix :]
        if begin is not None:
            begin(fixes, outs[n_out:])

        def step(t):
            here = pl.ds(pl.multiple_of(t * tile, 128), tile)
            values = [
                r[:, here] if axis == 1 else r[here, :] for r, (_, axis, _) in zip(ins, tiled)
            ]
            for ref, value in zip(outs, compute(t, values, fixes, None, outs[n_out:])):
                ref[:, here] = value.astype(ref.dtype)

        pl.loop(0, columns // tile)(step)

    operands, specs = [], []
    for array, axis, start in tiled:
        operands.append(array)
        if array.shape[axis] == columns:
            specs.append(whole(array.shape))
            continue
        shape = list(array.shape)
        shape[axis] = columns
        at = (0, start) if axis == 1 else (start, 0)
        specs.append(pl.BlockSpec(tuple(pl.Element(n) for n in shape), lambda *_, at=at: at))
    for array in fixed:
        operands.append(array)
        specs.append(whole(array.shape))
    shapes = [(shape, dtype) for shape, dtype, *_ in tiled_out] + list(fixed_out)
    return pl.pallas_call(
        kernel,
        in_specs=specs,
        out_specs=[whole(shape) for shape, _ in shapes],
        out_shape=[jax.ShapeDtypeStruct(shape, dtype) for shape, dtype in shapes],
        grid=(1,),
        compiler_params=PARAMS,
        cost_estimate=LIGHT,
    )(*operands)


def over_columns(
    compute, columns, tiled, fixed, scalars, tiled_out, fixed_out, into=None, pin=True,
    pin_out=True, begin=None,
):
    row_windows = [entry[3] if len(entry) > 3 else None for entry in tiled]
    tiled = [entry[:3] for entry in tiled]
    tile = tile_of(columns)
    steps = columns // tile
    n_in, n_fix, n_out = len(tiled), len(fixed), len(tiled_out)

    def kernel(*refs):
        refs = list(refs)
        take = lambda n: [refs.pop(0) for _ in range(n)]
        ins, fixes = take(n_in), take(n_fix)
        scalar = take(1)[0] if scalars is not None else None
        if into is not None:
            take(1)
        outs, fix_outs = take(n_out), take(len(fixed_out))
        in_bufs, out_bufs, fix_bufs = take(n_in), take(n_out), take(n_fix)
        in_sems, out_sems, fix_sems = take(3)

        def window(ref, axis, start, t, rows=None):
            here = pl.ds(pl.multiple_of(start + t * tile, 128), tile)
            if rows is not None:
                return ref.at[pl.ds(*rows), here]
            return ref.at[:, here] if axis == 1 else ref.at[here, :]

        def loads(t):
            return [
                pltpu.make_async_copy(
                    window(ins[i], axis, start, t, row_windows[i]),
                    window(in_bufs[i], axis, 0, t),
                    in_sems.at[i * steps + t],
                )
                for i, (_, axis, start) in enumerate(tiled)
            ]

        def stores(t):
            return [
                pltpu.make_async_copy(
                    window(out_bufs[i], 1, 0, t),
                    window(outs[i], 1, tiled_out[i][2], t),
                    out_sems.at[i * steps + t],
                )
                for i in range(n_out)
            ]

        whole_loads = [
            pltpu.make_async_copy(fixes[i], fix_bufs[i], fix_sems.at[i]) for i in range(n_fix)
        ]
        for copy in whole_loads:
            copy.start()
        for t in range(steps):
            for copy in loads(t):
                copy.start()
        for copy in whole_loads:
            copy.wait()

        def step(t):
            for copy in loads(t):
                copy.wait()
            values = [
                window(in_bufs[i], axis, 0, t)[...] for i, (_, axis, _) in enumerate(tiled)
            ]
            results = compute(t, values, fix_bufs, scalar, fix_outs)
            for i, value in enumerate(results):
                window(out_bufs[i], 1, 0, t)[...] = value.astype(out_bufs[i].dtype)
            for copy in stores(t):
                copy.start()

        if begin is not None:
            begin(fix_bufs, fix_outs)
        pl.loop(0, steps)(step)
        for t in range(steps):
            for copy in stores(t):
                copy.wait()

    hbm = pl.BlockSpec(memory_space=pl.ANY)
    operands = [in_hbm(a) if pin else a for a in [a for a, _, _ in tiled] + list(fixed)]
    specs = [hbm] * (n_in + n_fix)
    if scalars is not None:
        operands.append(scalars)
        specs.append(pl.BlockSpec(memory_space=pltpu.SMEM))
    aliases = {}
    if into is not None:
        aliases[len(operands)] = 0
        operands.append(in_hbm(into))
        specs.append(hbm)
    buffers = [
        pltpu.VMEM(
            (r[1] if r else a.shape[0], columns) if axis == 1 else (columns, a.shape[1]), a.dtype
        )
        for (a, axis, _), r in zip(tiled, row_windows)
    ] + [pltpu.VMEM((shape[0], columns), dtype) for shape, dtype, _ in tiled_out]
    buffers += [pltpu.VMEM(a.shape, a.dtype) for a in fixed]
    return pl.pallas_call(
        kernel,
        in_specs=specs,
        out_specs=[hbm] * n_out + [pl.BlockSpec(memory_space=pltpu.VMEM)] * len(fixed_out),
        out_shape=[
            (pltpu.HBM if pin_out else jax.ShapeDtypeStruct)(shape, dtype)
            for shape, dtype, _ in tiled_out
        ]
        + [jax.ShapeDtypeStruct(shape, dtype) for shape, dtype in fixed_out],
        scratch_shapes=buffers
        + [
            pltpu.SemaphoreType.DMA((max(1, n_in * steps),)),
            pltpu.SemaphoreType.DMA((max(1, n_out * steps),)),
            pltpu.SemaphoreType.DMA((max(1, n_fix),)),
        ],
        input_output_aliases=aliases,
        compiler_params=PARAMS,
        cost_estimate=LIGHT,
    )(*operands)


def tables_of(cap, info_ref, first_x):
    tokens = info_ref.shape[1]
    row = lax.broadcasted_iota(jnp.int32, (tokens, tokens), 0)
    col = lax.broadcasted_iota(jnp.int32, (tokens, tokens), 1)
    before = (row < col).astype(F32).astype(BF16)
    slot_of = lax.broadcasted_iota(jnp.int32, (cap, tokens), 0).astype(F32)
    places, weights = [], []
    for d in range(NX):
        expert = lax.rem(first_x + d, NX).astype(F32)
        first = info_ref[0:1, :] == expert
        second = info_ref[1:2, :] == expert
        named = jnp.where(first | second, 1.0, 0.0)
        prob = jnp.where(first, info_ref[2:3, :], jnp.where(second, info_ref[3:4, :], 0.0))
        rank = jnp.dot(
            jnp.broadcast_to(named, (8, tokens)).astype(BF16), before, preferred_element_type=F32
        )[0:1]
        placed = jnp.where((slot_of == rank) & (named > 0.0), 1.0, 0.0)
        places.append(placed)
        weights.append(
            jnp.broadcast_to(jnp.sum(placed * prob, axis=1, keepdims=True), (cap, 128))
        )
    return places, weights


def transposed(block):
    tokens = block.shape[1]
    row = lax.broadcasted_iota(jnp.int32, (tokens, tokens), 0)
    col = lax.broadcasted_iota(jnp.int32, (tokens, tokens), 1)
    eye = (row == col).astype(F32).astype(BF16)
    return lax.dot_general(eye, block.astype(BF16), CONTRACT_LAST, preferred_element_type=F32)


def route_kernel(
    cap, at_ref, info0_ref, info1_ref, pa_ref, pat_ref, wa_ref, p0_ref, w0_ref, p1_ref, w1_ref,
    keep_ref, send_ref,
):
    x, last = at_ref[0], at_ref[4].astype(F32)
    places, weights = tables_of(cap, info0_ref, jnp.int32(0))
    pa_ref[...] = jnp.concatenate(places, axis=0).astype(BF16)
    pat_ref[...] = transposed(jnp.concatenate(places, axis=0)).astype(BF16)
    wa_ref[...] = jnp.concatenate(weights, axis=0)
    places0, weights0 = tables_of(cap, info0_ref, x)
    places1, weights1 = tables_of(cap, info1_ref, x)
    p0_ref[...] = jnp.concatenate(places0, axis=0).astype(BF16)
    w0_ref[...] = jnp.concatenate(weights0, axis=0)
    p1_ref[...] = jnp.concatenate(places1, axis=0).astype(BF16)
    w1_ref[...] = jnp.concatenate(weights1, axis=0)
    for d in range(NX):
        keep = jnp.concatenate([places0[d] * (1.0 - last), places1[d] * last], axis=0)
        send = jnp.concatenate([places0[d] * last, places1[d] * (1.0 - last)], axis=0)
        keep_ref[d] = transposed(keep).astype(BF16)
        send_ref[d] = transposed(send).astype(BF16)


def route(at, info0, info1, cap):
    tokens = info0.shape[1]
    slots = NX * cap
    place, weight = (slots, tokens), (slots, 128)
    back = (NX, tokens, NZ * cap)
    shapes = [(place, BF16), ((tokens, slots), BF16), (weight, F32), (place, BF16), (weight, F32)]
    shapes += [(place, BF16), (weight, F32), (back, BF16), (back, BF16)]
    return pl.pallas_call(
        functools.partial(route_kernel, cap),
        in_specs=[pl.BlockSpec(memory_space=pltpu.SMEM), whole(info0.shape), whole(info1.shape)],
        out_specs=[whole(s) for s, _ in shapes],
        out_shape=[pltpu.HBM(s, t) for s, t in shapes],
        grid=(1,),
        compiler_params=PARAMS,
        cost_estimate=LIGHT,
    )(at, info0, info1)


def saved_kernel(cap, at_ref, gate_ref, up_ref, f1_ref, f2_ref, ha_ref, hb_ref, g3, u3, h3, k3):
    g3[...] = gate_ref[...].astype(F32).reshape(g3.shape)
    u3[...] = up_ref[...].astype(F32).reshape(u3.shape)
    z, c = at_ref[1], at_ref[2]
    for cr in range(NC):
        for zr in range(NZ):
            for xs in range(NX):
                j = (cr * NZ + zr) * NX + xs
                zs = z if zr == 0 else 1 - z
                cs = c if cr == 0 else 1 - c
                q = xs * (NZ * NC) + zs * NC + cs
                gate, upval = g3[q], u3[q]
                sig = jax.nn.sigmoid(gate)
                f1_ref[pl.ds(j * cap, cap), :] = upval * sig * (1.0 + gate * (1.0 - sig))
                f2_ref[pl.ds(j * cap, cap), :] = gate * sig
                h3[j] = gate * sig * upval
    ha_ref[...] = h3[...].reshape(ha_ref.shape).astype(BF16)
    a_to_b(at_ref[0], h3, k3)
    hb_ref[...] = k3[...].reshape(hb_ref.shape).astype(BF16)


def pairs_of_blocks(x):
    for cr in range(NC):
        for zr in range(NZ):
            for d in range(NX):
                yield (cr * NZ + zr) * NX + lax.rem(x + NX - d, NX), (cr * NX + d) * NZ + zr


def a_to_b(x, a3, b3):
    for ja, jb in pairs_of_blocks(x):
        b3[jb] = a3[ja]


def saved(at, gate, up, cap):
    rows, hid = gate.shape
    blocks = rows // cap
    return pl.pallas_call(
        functools.partial(saved_kernel, cap),
        in_specs=[pl.BlockSpec(memory_space=pltpu.SMEM), whole(gate.shape), whole(up.shape)],
        out_specs=[whole((rows, hid))] * 4,
        out_shape=[jax.ShapeDtypeStruct((rows, hid), t) for t in (F32, F32, BF16, BF16)],
        scratch_shapes=[pltpu.VMEM((blocks, cap, hid), F32)] * 4,
        grid=(1,),
        compiler_params=PARAMS,
        cost_estimate=LIGHT,
    )(at, gate, up)


def pack_a(place, weight, tok, start, columns):
    def compute(t, values, fixed, scalar, outs):
        rows = jnp.dot(fixed[0][...], values[0], preferred_element_type=F32)
        return [rows * fixed[1][:, 0:1]]

    out = ((place.shape[0], columns), BF16, 0)
    return over_columns(
        compute, columns, [(tok, 1, start)], [place, weight], None, [out], [], pin_out=False
    )[0]


def pack_b(place0, weight0, place1, weight1, tok0, start, tok1, cap):
    columns = tok1.shape[1]

    def compute(t, values, fixed, scalar, outs):
        rows0 = jnp.dot(fixed[0][...], values[0], preferred_element_type=F32) * fixed[1][:, 0:1]
        rows1 = jnp.dot(fixed[2][...], values[1], preferred_element_type=F32) * fixed[3][:, 0:1]
        cut = [slice(d * cap, (d + 1) * cap) for d in range(NX)]
        return [jnp.concatenate([rows0[i], rows1[i]], axis=0) for i in cut]

    out = ((NZ * cap, columns), BF16, 0)
    return over_columns(
        compute, columns, [(tok0, 1, start), (tok1, 1, 0)], [place0, weight0, place1, weight1],
        None, [out] * NX, [], pin_out=False,
    )


def use_rows(groups, w_down, hid_t, dh, grad, start, want_sum, want_grad, kernel=over_columns):
    hid, width = w_down.shape
    groups = [[e if isinstance(e, tuple) else (e, None) for e in g] for g in groups]
    columns = groups[0][0][0].shape[1]
    lengths = [sum(r[1] if r else a.shape[0] for a, r in g) for g in groups]
    rows = sum(lengths)
    tiled = [(a, 1, 0, r) if r else (a, 1, 0) for g in groups for a, r in g]
    fixed = []
    if want_sum:
        tiled.append((w_down, 1, start))
        if dh is not None:
            fixed.append(dh)
    if want_grad:
        fixed.append(hid_t)

    def compute(t, values, fixed_refs, scalar, outs):
        values, refs = list(values), list(fixed_refs)
        blocks = []
        for g in groups:
            parts = [values.pop(0) for _ in g]
            blocks.append(parts[0] if len(parts) == 1 else jnp.concatenate(parts, axis=0))
        if want_sum:
            if dh is not None:
                refs.pop(0)
            low = 0
            for block, many in zip(blocks, lengths):
                here = pl.ds(low, many)
                more = lax.dot_general(block, values[0], CONTRACT_LAST, preferred_element_type=F32)
                outs[0][here, :] += more
                low += many
        if not want_grad:
            return []
        total = None
        for i, block in enumerate(blocks):
            more = jnp.dot(refs[0][i], block, preferred_element_type=F32)
            total = more if total is None else total + more
        return [total]

    def begin(fixed_refs, outs):
        outs[0][...] = fixed_refs[0][...] if dh is not None else jnp.zeros((rows, hid), F32)

    begin = begin if want_sum else None
    sums = [((rows, hid), F32)] if want_sum else []
    if not want_grad:
        return kernel(compute, columns, tiled, fixed, None, [], sums, begin=begin)[0]
    done = over_columns(
        compute, columns, tiled, fixed, None, [((hid, width), F32, start)], sums, grad, begin=begin
    )
    return (done[1], done[0]) if want_sum else done[0]


def join(blocks):
    rows, columns = sum(b.shape[0] for b in blocks), blocks[0].shape[1]

    def compute(t, values, fixed, scalar, outs):
        return [jnp.concatenate(values, axis=0)]

    out = ((rows, columns), blocks[0].dtype, 0)
    return over_columns(compute, columns, [(b, 1, 0) for b in blocks], [], None, [out], [])[0]


def act_kernel(
    at_ref, near_ref, far0_ref, far1_ref, b0_ref, b1_ref, f1_ref, f2_ref,
    ga_ref, ua_ref, gb_ref, ub_ref, one, two,
):
    x = at_ref[0]
    half = two.shape[0] // NC
    two[pl.ds(0, half)] = b0_ref[...].reshape((half,) + two.shape[1:])
    two[pl.ds(half, half)] = b1_ref[...].reshape((half,) + two.shape[1:])
    for ja, jb in pairs_of_blocks(x):
        one[ja] = two[jb]
    many = far0_ref.shape[0]
    dh = jnp.concatenate(
        [near_ref[pl.ds(0, many), :], far0_ref[...], near_ref[pl.ds(many, many), :], far1_ref[...]],
        axis=0,
    ) + one[...].reshape(f1_ref.shape)
    dgate = dh * f1_ref[...]
    dup = dh * f2_ref[...]
    ga_ref[...] = dgate.astype(BF16)
    ua_ref[...] = dup.astype(BF16)
    for value, out_ref in ((dgate, gb_ref), (dup, ub_ref)):
        one[...] = value.reshape(one.shape)
        a_to_b(x, one, two)
        out_ref[...] = two[...].reshape(out_ref.shape).astype(BF16)


def activations(at, dhs, f1, f2, cap):
    rows, hid = f1.shape
    operands = list(dhs) + [f1, f2]
    return pl.pallas_call(
        act_kernel,
        in_specs=[pl.BlockSpec(memory_space=pltpu.SMEM)] + [whole(a.shape) for a in operands],
        out_specs=[whole((rows, hid))] * 4,
        out_shape=[jax.ShapeDtypeStruct((rows, hid), BF16)] * 4,
        scratch_shapes=[pltpu.VMEM((rows // cap, cap, hid), F32)] * 2,
        grid=(1,),
        compiler_params=PARAMS,
        cost_estimate=LIGHT,
    )(at, *operands)


def unpinned(*args):
    return over_columns(*args, pin_out=False)


def parts_of(dg, du, wg, wu, start, columns, half, other, pieces, kernel):
    many = dg.shape[0] // NC
    each = many // pieces
    tiled = [(wg, 0, start), (wu, 0, start)]
    if other is not None:
        tiled.append((other, 1, 0))

    def compute(t, values, fixed, scalar, outs):
        here = pl.ds(half * many, many)
        total = lax.dot_general(
            fixed[0][here, :], values[0], CONTRACT_LAST, preferred_element_type=F32
        )
        total += lax.dot_general(
            fixed[1][here, :], values[1], CONTRACT_LAST, preferred_element_type=F32
        )
        if other is not None:
            total += values[2].astype(F32)
        return [total[i * each : (i + 1) * each] for i in range(pieces)]

    out = ((each, columns), BF16, 0)
    return kernel(compute, columns, tiled, [dg, du], None, [out] * pieces, [])


def sum_z(a, b):
    def compute(t, values, fixed, scalar, outs):
        return [values[0].astype(F32) + values[1].astype(F32)]

    return over_columns(
        compute, a.shape[1], [(a, 1, 0), (b, 1, 0)], [], None, [(a.shape, BF16, 0)], []
    )[0]


def finish_a(place_t, tok, start, rows):
    def compute(t, values, fixed, scalar, outs):
        branch = jnp.dot(fixed[0][...], values[1], preferred_element_type=F32).astype(BF16)
        return [values[0].astype(F32) + branch.astype(F32)]

    out = ((tok.shape[0], rows.shape[1]), BF16, 0)
    return over_columns(
        compute, rows.shape[1], [(tok, 1, start), (rows, 1, 0)], [place_t], None, [out], []
    )[0]


def combine_b(keep, send, blocks):
    columns = blocks[0].shape[1]
    tokens = keep.shape[1]

    def compute(t, values, fixed, scalar, outs):
        totals = []
        for ref in fixed:
            total = None
            for d in range(NX):
                more = jnp.dot(ref[d], values[d], preferred_element_type=F32)
                total = more if total is None else total + more
            totals.append(total)
        return totals

    outs = [((tokens, columns), F32, 0), ((tokens, columns), BF16, 0)]
    return over_columns(compute, columns, [(b, 1, 0) for b in blocks], [keep, send], None, outs, [])


def finish_b(at, own, other, tok0, start, tok1):
    columns = own.shape[1]

    def compute(t, values, fixed, scalar, outs):
        branch = (values[0] + values[1].astype(F32)).astype(BF16)
        tok = jnp.where(scalar[4] == 0, values[2].astype(F32), values[3].astype(F32))
        return [tok + branch.astype(F32)]

    tiled = [(own, 1, 0), (other, 1, 0), (tok0, 1, start), (tok1, 1, 0)]
    return over_columns(compute, columns, tiled, [], at, [(own.shape, BF16, 0)], [])[0]


def place_chunk(piece, width, start, into):
    def compute(t, values, fixed, scalar, outs):
        return values

    columns = piece.shape[1]
    out = ((piece.shape[0], width), piece.dtype, start)
    return over_columns(compute, columns, [(piece, 1, 0)], [], None, [out], [], into, False)[0]


def body(pending, expert_ids, route_weight, gate_saved, up_saved, w_gate, w_up, w_down):
    own = pending[0]
    width = own.shape[1]
    rows, hid = gate_saved.shape[1:]
    cap = rows // (NX * NZ * NC)
    w_gate, w_up, w_down = w_gate[0], w_up[0], w_down[0]
    unit = width // 28
    a0, b0, a1, b1 = EARLY[0] * unit, EARLY[1] * unit, LATE[0] * unit, LATE[1] * unit
    early = a0 + b0
    at_a0, at_b0, at_a1, at_b1 = 0, a0, early, early + a1
    tie = lax.optimization_barrier

    def crossing(s):
        return s % NY == 0

    def swapped(s):
        return s % NY == NY - 1

    tok_a0 = section_move(own[:, :a0], crossing)
    own_b0 = own[:, a0:early]
    next_b0 = ep_move(own_b0, dz=1)
    info = jnp.concatenate([expert_ids[0].astype(F32), route_weight[0]], axis=1).T
    info_far = ep_move(info, dz=1)
    tok_b0 = section_move(release(own_b0, tok_a0), crossing)
    far_tok0 = section_move(next_b0, crossing)
    own_late = release(own, tok_b0)
    tok_a1 = section_move(own_late[:, early : early + a1], crossing)
    tok_b1 = section_move(release(own_late, tok_a1)[:, early + a1 :], crossing)
    section = lax.axis_index("section").astype(jnp.int32)
    position = lax.axis_index("ep").astype(jnp.int32)
    turned = (section % NY == NY - 1).astype(jnp.int32)
    last = jnp.maximum(turned, (section % NY == 0).astype(jnp.int32))
    z = (position >> 1) & 1
    at = jnp.stack([position >> 2, jnp.where(turned == 1, 1 - z, z), position & 1, turned, last])
    info0 = jnp.where(turned == 1, info_far, info)
    info1 = jnp.where(turned == 1, info, info_far)
    place, place_t, weight, place0, weight0, place1, weight1, keep_t, send_t = route(
        at, info0, info1, cap
    )

    near_a0 = x_exchange(pack_a(place, weight, tok_a0, 0, a0))
    near_a0, tok_b0, far_tok0, at_later = tie((near_a0, tok_b0, far_tok0, at))
    far_a0 = ep_move(near_a0, dz=1)
    sent_b0 = pack_b(place0, weight0, place1, weight1, tok_b0, 0, far_tok0, cap)
    got_b0 = x_moves(sent_b0, 1)
    f1, f2, hid_a, hid_b = saved(release(at_later, sent_b0), gate_saved[0], up_saved[0], cap)
    hid_at = hid_a.reshape(NC * NZ, -1, hid).transpose(0, 2, 1)
    hid_bt = hid_b.reshape(NC, -1, hid).transpose(0, 2, 1)
    hid_near = jnp.stack([hid_at[0], hid_at[2], hid_at[1], hid_at[3]])
    packed_a1 = pack_a(place, weight, tok_a1, 0, a1)
    far_a0, got_b0, packed_a1, f1, f2, hid_at, hid_bt, hid_near = tie(
        (far_a0, got_b0, packed_a1, f1, f2, hid_at, hid_bt, hid_near)
    )
    near_a1 = x_exchange(packed_a1)
    far_tok1 = ep_move(tok_b1, dz=1)
    mine0 = join([near_a0, far_a0, sent_b0[0]] + got_b0)
    near_a1, far_tok1, mine0 = tie((near_a1, far_tok1, mine0))
    far_a1 = ep_move(near_a1, dz=1)
    sent_b1 = pack_b(place0, weight0, place1, weight1, tok_b1, 0, far_tok1, cap)
    got_b1 = x_moves(sent_b1, 1)
    many = NX * cap
    theirs0 = ep_move(mine0, dc=1)
    rows_a0 = [(mine0, (0, many)), (theirs0, (0, many)), (mine0, (many, many)), (theirs0, (many, many))]
    rows_b0 = [(mine0, (2 * many, 2 * many)), (theirs0, (2 * many, 2 * many))]
    dh_a, grad = use_rows([[g] for g in rows_a0], w_down, hid_near, None, None, at_a0, True, True)
    dh_b, grad = use_rows([[g] for g in rows_b0], w_down, hid_bt, None, grad, at_b0, True, True)
    dh_near, dh_far0, dh_far1 = dh_a[: 2 * many], dh_a[2 * many : 3 * many], dh_a[3 * many :]
    dh_b0, dh_b1 = dh_b[: 2 * many], dh_b[2 * many :]

    def more_dh(groups, dh, start):
        return use_rows(groups, w_down, None, dh, None, start, True, False, at_once)

    far_a1, got_b1, dh_near, dh_far0, dh_far1, dh_b0, dh_b1, grad = tie(
        (far_a1, got_b1, dh_near, dh_far0, dh_far1, dh_b0, dh_b1, grad)
    )
    near_a1_other, far_a1_other = ep_move(near_a1, dc=1), ep_move(far_a1, dc=1)
    mine_b1 = [sent_b1[0]] + got_b1
    theirs_b1 = [ep_move(piece, dc=1) for piece in mine_b1]
    dh_b0 = more_dh([mine_b1], dh_b0, at_b1)
    dh_far0 = more_dh([[far_a1]], dh_far0, at_a1)
    dh_near = more_dh([[near_a1], [near_a1_other]], dh_near, at_a1)
    dh_b1 = more_dh([theirs_b1], dh_b1, at_b1)
    dh_far1 = more_dh([[far_a1_other]], dh_far1, at_a1)
    rows_a1 = [[near_a1], [far_a1], [near_a1_other], [far_a1_other]]
    rows_b1 = [mine_b1, theirs_b1]

    grads = activations(at, [dh_near, dh_far0, dh_far1, dh_b0, dh_b1], f1, f2, cap)

    def parts(kind, low, n, other, pieces, kernel, grads):
        dg, du = grads[:2] if kind == "A" else grads[2:]
        half = 1 if other is None else 0
        return parts_of(dg, du, w_gate, w_up, low, n, half, other, pieces, kernel)

    core_b1 = ep_move(parts("B", at_b1, b1, None, 1, at_once, grads)[0], dc=1)
    core_a1 = ep_move(parts("A", at_a1, a1, None, 1, at_once, grads)[0], dc=1)
    part_b1 = parts("B", at_b1, b1, core_b1, NX, at_once, grads)
    back_b1 = x_moves(part_b1, -1)
    keep_a1, send_a1 = parts("A", at_a1, a1, core_a1, NZ, at_once, grads)
    back_a1 = ep_move(send_a1, dz=1)
    core_b0 = ep_move(parts("B", at_b0, b0, None, 1, at_once, grads)[0], dc=1)
    core_a0 = ep_move(parts("A", at_a0, a0, None, 1, at_once, grads)[0], dc=1)
    grads = release(grads, part_b1, send_a1)
    part_b0 = parts("B", at_b0, b0, core_b0, NX, unpinned, grads)
    keep_a0, send_a0 = parts("A", at_a0, a0, core_a0, NZ, over_columns, grads)
    grad = use_rows(rows_a1, w_down, hid_at, None, release(grad, grads), at_a1, False, True)
    grad = use_rows(rows_b1, w_down, hid_bt, None, grad, at_b1, False, True)
    back_b1, back_a1, part_b0, keep_a0, send_a0, grad = tie(
        (back_b1, back_a1, part_b0, keep_a0, send_a0, grad)
    )
    back_b0 = x_moves(part_b0, -1)
    back_a0 = ep_move(send_a0, dz=1)
    keep_b1, send_b1 = combine_b(keep_t, send_t, [part_b1[0]] + back_b1)
    cross_b1 = ep_move(send_b1, dz=1)
    keep_b0, send_b0 = combine_b(keep_t, send_t, [part_b0[0]] + back_b0)
    sum_a1 = sum_z(keep_a1, back_a1)
    cross_b1, send_b0, back_a0, sum_a1 = tie((cross_b1, send_b0, back_a0, sum_a1))
    own_a1 = x_exchange(sum_a1)
    up_b1 = section_move(finish_b(at, keep_b1, cross_b1, tok_b1, 0, far_tok1), crossing)
    cross_b0 = ep_move(send_b0, dz=1)
    sum_a0 = sum_z(keep_a0, back_a0)
    done_a1 = finish_a(place_t, tok_a1, 0, own_a1)
    done_a1, cross_b0, sum_a0, up_b1 = tie((done_a1, cross_b0, sum_a0, up_b1))
    up_a1 = section_move(done_a1, swapped)
    own_a0 = x_exchange(sum_a0)
    up_b0 = section_move(finish_b(at, keep_b0, cross_b0, tok_b0, 0, far_tok0), crossing)
    up_a0 = section_move(finish_a(place_t, tok_a0, 0, own_a0), swapped)
    out = place_chunk(up_b1, width, at_b1, None)
    out = place_chunk(up_a1, width, at_a1, out)
    out = place_chunk(up_b0, width, at_b0, out)
    out = place_chunk(up_a0, width, at_a0, out)
    return (out[None], grad[None])


def solution(mesh):
    placed = (
        P("section", "ep", None),
        P("section", "ep", None),
        P("section", "ep", None),
        P("section", None, "ep"),
        P("section", None, "ep"),
        P("section", None, "ep"),
        P("section", None, "ep"),
        P("section", "ep", None),
    )
    return jax.shard_map(
        body,
        mesh=mesh,
        in_specs=placed,
        out_specs=(P("section", "ep", None), P("section", "ep", None)),
        check_vma=False,
    )
```

profile of v0, /device:TPU:0, one launch (start us, length us, event | category | flops | bytes accessed | tf_op | source)
XLA Modules:
  0.0 272.0 jit_solution(16135743463405694118)
XLA Ops:
  1.8 6.6 %collective-permute-start = (bf16[128,1280]{1,0:T(8,128)(2,1)S(1)}, bf16[128,1280]{1,0:T(8,128)(2,1)S(1)}, u32[]{:S(2)}, u32[]{:S(2)}) collective-permute-start(bf16[128,1280]{1,0:T(8,128)(2,1)S(1)} %get-tuple-element.203), channel_id=1, source_target_pairs={{0,114},{1,115},{2,112},{3,113},{4,118},{5,119},{6,116},{7,117},{8... | collective-permute-start | bytes 983048 | tf_op jit(solution)/shard_map/ppermute | solution.py:26
  9.8 2.0 collective-permute-start.4
  11.9 3.5 %collective-permute-done.refs_0_ = bf16[128,1280]{1,0:T(8,128)(2,1)S(1)} collective-permute-done((bf16[128,1280]{1,0:T(8,128)(2,1)S(1)}, bf16[128,1280]{1,0:T(8,128)(2,1)S(1)}, u32[]{:S(2)}, u32[]{:S(2)}) %collective-permute-start) | collective-permute-done | bytes 327712 | tf_op jit(solution)/shard_map/ppermute | solution.py:26
  15.4 5.8 %collective-permute-start.1 = (bf16[128,1280]{1,0:T(8,128)(2,1)S(1)}, bf16[128,1280]{1,0:T(8,128)(2,1)S(1)}, u32[]{:S(2)}, u32[]{:S(2)}) collective-permute-start(bf16[128,1280]{1,0:T(8,128)(2,1)S(1)} %get-tuple-element.102), channel_id=1, source_target_pairs={{0,114},{1,115},{2,112},{3,113},{4,118},{5,119},{6,116},{7,117},{8... | collective-permute-start | bytes 983048 | tf_op jit(solution)/shard_map/ppermute | solution.py:26
  21.9 2.0 shard_map.95
  23.9 2.3 shard_map.96
  26.2 4.3 %all-to-all-start = ((bf16[4,72,1280]{2,1,0:T(8,128)(2,1)}), bf16[4,72,1280]{2,1,0:T(8,128)(2,1)}, u32[]{:S(2)}, u32[]{:S(2)}) async-start(bf16[4,72,1280]{2,1,0:T(8,128)(2,1)} %bitcast.11), calls=%async_computation | async-start | bytes 1474560 | tf_op jit(solution)/shard_map/all_to_all | solution.py:44
  30.6 2.1 slice.41
  32.7 2.4 collective-permute-start.2
  35.1 6.1 %collective-permute-done.5.refs_1_.refs_3_ = bf16[128,1280]{1,0:T(8,128)(2,1)S(1)} collective-permute-done((bf16[128,1280]{1,0:T(8,128)(2,1)S(1)}, bf16[128,1280]{1,0:T(8,128)(2,1)S(1)}, u32[]{:S(2)}, u32[]{:S(2)}) %collective-permute-start.5) | collective-permute-done | bytes 327712 | tf_op jit(solution)/shard_map/ppermute | solution.py:26
  41.9 2.9 %shard_map.97 = (bf16[144,1280]{1,0:T(8,128)(2,1)S(1)}, bf16[144,1280]{1,0:T(8,128)(2,1)}, bf16[144,1280]{1,0:T(8,128)(2,1)}, bf16[144,1280]{1,0:T(8,128)(2,1)S(1)}) custom-call(bf16[128,1280]{1,0:T(8,128)(2,1)} %copy-done.37, bf16[128,1280]{1,0:T(8,128)(2,1)} %copy-done.38, bf16[288,128]{1,0:T(8,128)(2,1)} %get-tuple-element.109.refs_2_, ...), custom_call_target="tpu_custom_call" | custom-call | flops 1 | bytes 1 | tf_op jit(solution)/shard_map/pallas_call | solution.py:203
  45.7 2.0 collective-permute-start.7
  47.7 2.7 collective-permute-start.8
  50.4 1.5 collective-permute-start.9
  55.0 1.4 copy.16
  56.4 2.2 slice.46
  58.6 3.4 %collective-permute-start.10 = (bf16[128,2304]{1,0:T(8,128)(2,1)}, bf16[128,2304]{1,0:T(8,128)(2,1)}, u32[]{:S(2)}, u32[]{:S(2)}) collective-permute-start(bf16[128,2304]{1,0:T(8,128)(2,1)} %slice.46), channel_id=1, source_target_pairs={{0,114},{1,115},{2,112},{3,113},{4,118},{5,119},{6,116},{7,117},{8... | collective-permute-start | bytes 1769480 | tf_op jit(solution)/shard_map/ppermute | solution.py:26
  63.9 2.0 pad_maximum_fusion.refs_5_
  65.9 2.8 %shard_map.98 = bf16[288,2304]{1,0:T(8,128)(2,1)} custom-call(bf16[128,2304]{1,0:T(8,128)(2,1)} %collective-permute-done.2.refs_0_, bf16[288,128]{1,0:T(8,128)(2,1)} %get-tuple-element.104.refs_1_, f32[288,128]{1,0:T(8,128)} %get-tuple-element.105.refs_2_), custom_call_target="tpu_custom_call" | custom-call | flops 1 | bytes 1 | tf_op jit(solution)/shard_map/pallas_call | solution.py:203
  68.7 3.6 %all-to-all-start.1 = ((bf16[4,72,2304]{2,1,0:T(8,128)(2,1)}), bf16[4,72,2304]{2,1,0:T(8,128)(2,1)S(1)}, u32[]{:S(2)}, u32[]{:S(2)}) async-start(bf16[4,72,2304]{2,1,0:T(8,128)(2,1)} %bitcast.19), calls=%async_computation.1 | async-start | bytes 2654208 | tf_op jit(solution)/shard_map/all_to_all | solution.py:44
  73.1 3.2 %shard_map.100.refs_0_.refs_2_ = bf16[1152,1280]{1,0:T(8,128)(2,1)} custom-call(bf16[288,1280]{1,0:T(8,128)(2,1)} %bitcast.12.refs_0_, bf16[288,1280]{1,0:T(8,128)(2,1)} %collective-permute-done.6.refs_1_, bf16[144,1280]{1,0:T(8,128)(2,1)} %copy-done.26, bf16[144,1280]{1,0:T(8,128)(2,1)} %collective-permute-done.7.refs_3_, ...), custom_call_target="tpu_custom_call" | custom-call | flops 1 | bytes 1 | tf_op jit(solution)/shard_map/pallas_call | solution.py:203
  76.3 6.1 %collective-permute-done.11.refs_1_.refs_3_ = bf16[128,2304]{1,0:T(8,128)(2,1)S(1)} collective-permute-done((bf16[128,2304]{1,0:T(8,128)(2,1)}, bf16[128,2304]{1,0:T(8,128)(2,1)S(1)}, u32[]{:S(2)}, u32[]{:S(2)}) %collective-permute-start.11) | collective-permute-done | bytes 589856 | tf_op jit(solution)/shard_map/ppermute | solution.py:34
  82.4 2.3 all-to-all-done.1
  85.3 3.0 %shard_map.101 = (bf16[144,2304]{1,0:T(8,128)(2,1)S(1)}, bf16[144,2304]{1,0:T(8,128)(2,1)S(1)}, bf16[144,2304]{1,0:T(8,128)(2,1)S(1)}, bf16[144,2304]{1,0:T(8,128)(2,1)S(1)}) custom-call(bf16[128,2304]{1,0:T(8,128)(2,1)} %collective-permute-done.10.refs_0_.refs_2_, bf16[128,2304]{1,0:T(8,128)(2,1)} %copy-done.32, ...), custom_call_target="tpu_custom_call" | custom-call | flops 1 | bytes 1 | tf_op jit(solution)/shard_map/pallas_call | solution.py:203
  89.0 2.1 collective-permute-start.15
  91.0 1.4 collective-permute-start.16
  92.5 1.5 copy-done.28
  94.0 6.0 %shard_map.102 = (f32[256,7168]{1,0:T(8,128)}, f32[1152,256]{1,0:T(8,128)S(1)}) custom-call(bf16[1152,1280]{1,0:T(8,128)(2,1)} %shard_map.100.refs_0_.refs_2_, bf16[1152,1280]{1,0:T(8,128)(2,1)} %copy-done.28, bf16[1152,1280]{1,0:T(8,128)(2,1)} %shard_map.100.refs_0_.refs_2_, bf16[1152,1280]{1,0:T(8,128)(2,1)} %copy-done.28, bf16[256,7168]{1,0:T(8,128)(2,1)} %bitcast.50, ...), custom_call_target="tpu_custom_call" | custom-call | flops 1 | bytes 1 | tf_op jit(solution)/shard_map/pallas_call | solution.py:203
  100.0 5.6 %shard_map.103 = (f32[256,7168]{1,0:T(8,128)}, f32[1152,256]{1,0:T(8,128)S(1)}) custom-call(bf16[1152,1280]{1,0:T(8,128)(2,1)} %shard_map.100.refs_0_.refs_2_, bf16[1152,1280]{1,0:T(8,128)(2,1)} %copy-done.28, bf16[256,7168]{1,0:T(8,128)(2,1)} %bitcast.51, bf16[2,256,576]{2,1,0:T(8,128)(2,1)} %bitcast.69, ...), custom_call_target="tpu_custom_call", output_to_operand_aliasing={{0}: (4, {})} | custom-call | flops 1 | bytes 1 | tf_op jit(solution)/shard_map/pallas_call | solution.py:203
  105.9 15.0 %collective-permute-done.14.refs_1_ = bf16[144,2304]{1,0:T(8,128)(2,1)S(1)} collective-permute-done((bf16[144,2304]{1,0:T(8,128)(2,1)S(1)}, bf16[144,2304]{1,0:T(8,128)(2,1)S(1)}, u32[]{:S(2)}, u32[]{:S(2)}) %collective-permute-start.14) | collective-permute-done | bytes 663584 | tf_op jit(solution)/shard_map/ppermute | solution.py:34
  125.2 1.4 shard_map.104.near_ref
  128.4 1.4 shard_map.108.b1_ref
  131.7 1.4 shard_map.109
  134.1 2.0 shard_map.112
  136.3 2.0 shard_map.110
  142.1 2.0 shard_map.113
  144.1 1.6 collective-permute-start.28
  145.7 2.0 shard_map.111
  147.8 2.7 collective-permute-start.24
  151.4 6.5 %shard_map.118.refs_9_ = f32[256,7168]{1,0:T(8,128)} custom-call(bf16[288,2304]{1,0:T(8,128)(2,1)} %bitcast.60, bf16[288,2304]{1,0:T(8,128)(2,1)} %copy-done.9, bf16[288,2304]{1,0:T(8,128)(2,1)} %copy-done.8, bf16[288,2304]{1,0:T(8,128)(2,1)} %copy-done.10, bf16[4,256,288]{2,1,0:T(8,128)(2,1)} %bitcast.68, ...), custom_call_target="tpu_custom_call", output_to_operand_aliasing={{}: (5, {})} | custom-call | flops 1 | bytes 1 | tf_op jit(solution)/shard_map/pallas_call | solution.py:203
  158.0 6.3 %shard_map.119 = f32[256,7168]{1,0:T(8,128)} custom-call(bf16[144,2304]{1,0:T(8,128)(2,1)} %copy-done.11, bf16[144,2304]{1,0:T(8,128)(2,1)} %copy-done.12, bf16[144,2304]{1,0:T(8,128)(2,1)} %copy-done.13, bf16[144,2304]{1,0:T(8,128)(2,1)} %copy-done.14, bf16[144,2304]{1,0:T(8,128)(2,1)} %copy-done.15, ...), custom_call_target="tpu_custom_call", output_to_operand_aliasing={{}: (9, {})} | custom-call | flops 1 | bytes 1 | tf_op jit(solution)/shard_map/pallas_call | solution.py:203
  164.2 4.2 %shard_map.117 = (bf16[288,1280]{1,0:T(8,128)(2,1)}, bf16[288,1280]{1,0:T(8,128)(2,1)}) custom-call(bf16[7168,256]{1,0:T(8,128)(2,1)} %bitcast.34, bf16[7168,256]{1,0:T(8,128)(2,1)} %bitcast.42, bf16[576,1280]{1,0:T(8,128)(2,1)} %copy-done.34, bf16[1152,256]{1,0:T(8,128)(2,1)} %copy-done.6, bf16[1152,256]{1,0:T(8,128)(2,1)} %copy-done.7), custom_call_target="tpu_custom_call" | custom-call | flops 1 | bytes 1 | tf_op jit(solution)/shard_map/pallas_call | solution.py:203
  169.5 3.5 %shard_map.115 = (bf16[144,1280]{1,0:T(8,128)(2,1)S(1)}, bf16[144,1280]{1,0:T(8,128)(2,1)S(1)}, bf16[144,1280]{1,0:T(8,128)(2,1)S(1)}, bf16[144,1280]{1,0:T(8,128)(2,1)S(1)}) custom-call(bf16[7168,256]{1,0:T(8,128)(2,1)} %bitcast.35, bf16[7168,256]{1,0:T(8,128)(2,1)} %bitcast.43, bf16[576,1280]{1,0:T(8,128)(2,1)} %copy-done.33, bf16[1152,256]{1,0:T(8,128)(2,1)} %copy-done.4, ...), custom_call_target="tpu_custom_call" | custom-call | flops 1 | bytes 1 | tf_op jit(solution)/shard_map/pallas_call | solution.py:203
  173.0 5.8 %collective-permute-done.24.refs_1_ = bf16[144,2304]{1,0:T(8,128)(2,1)S(1)} collective-permute-done((bf16[144,2304]{1,0:T(8,128)(2,1)S(1)}, bf16[144,2304]{1,0:T(8,128)(2,1)S(1)}, u32[]{:S(2)}, u32[]{:S(2)}) %collective-permute-start.24) | collective-permute-done | bytes 663584 | tf_op jit(solution)/shard_map/ppermute | solution.py:34
  178.9 3.7 %collective-permute-done.26.refs_3_ = bf16[144,2304]{1,0:T(8,128)(2,1)S(1)} collective-permute-done((bf16[144,2304]{1,0:T(8,128)(2,1)S(1)}, bf16[144,2304]{1,0:T(8,128)(2,1)S(1)}, u32[]{:S(2)}, u32[]{:S(2)}) %collective-permute-start.26) | collective-permute-done | bytes 663584 | tf_op jit(solution)/shard_map/ppermute | solution.py:34
  183.7 4.6 %shard_map.120 = (f32[128,2304]{1,0:T(8,128)}, bf16[128,2304]{1,0:T(8,128)(2,1)}) custom-call(bf16[144,2304]{1,0:T(8,128)(2,1)} %copy-done.22, bf16[144,2304]{1,0:T(8,128)(2,1)} %copy-done.40, bf16[144,2304]{1,0:T(8,128)(2,1)} %copy-done.41, bf16[144,2304]{1,0:T(8,128)(2,1)} %copy-done.42, bf16[4,128,144]{2,1,0:T(8,128)(2,1)} %get-tuple-element.178.refs_4_, ...), custom_call_target="tpu_custom_call" | custom-call | flops 1 | bytes 1 | tf_op jit(solution)/shard_map/pallas_call | solution.py:203
  191.5 2.7 shard_map.122
  194.2 6.8 %collective-permute-done.32.refs_1_ = bf16[144,1280]{1,0:T(8,128)(2,1)S(1)} collective-permute-done((bf16[144,1280]{1,0:T(8,128)(2,1)S(1)}, bf16[144,1280]{1,0:T(8,128)(2,1)S(1)}, u32[]{:S(2)}, u32[]{:S(2)}) %collective-permute-start.32) | collective-permute-done | bytes 368672 | tf_op jit(solution)/shard_map/ppermute | solution.py:34
  200.9 2.2 collective-permute-done.33.refs_2_
  203.1 5.8 %collective-permute-done.34.refs_3_ = bf16[144,1280]{1,0:T(8,128)(2,1)S(1)} collective-permute-done((bf16[144,1280]{1,0:T(8,128)(2,1)S(1)}, bf16[144,1280]{1,0:T(8,128)(2,1)S(1)}, u32[]{:S(2)}, u32[]{:S(2)}) %collective-permute-start.34) | collective-permute-done | bytes 368672 | tf_op jit(solution)/shard_map/ppermute | solution.py:34
  209.6 3.6 %shard_map.121 = (f32[128,1280]{1,0:T(8,128)}, bf16[128,1280]{1,0:T(8,128)(2,1)}) custom-call(bf16[144,1280]{1,0:T(8,128)(2,1)} %copy-done.27, bf16[144,1280]{1,0:T(8,128)(2,1)} %copy-done.45, bf16[144,1280]{1,0:T(8,128)(2,1)} %copy-done.46, bf16[144,1280]{1,0:T(8,128)(2,1)} %copy-done.47, bf16[4,128,144]{2,1,0:T(8,128)(2,1)} %get-tuple-element.178.refs_4_, ...), custom_call_target="tpu_custom_call" | custom-call | flops 1 | bytes 1 | tf_op jit(solution)/shard_map/pallas_call | solution.py:203
  213.7 3.5 %all-to-all-start.2 = ((bf16[4,72,2304]{2,1,0:T(8,128)(2,1)}), bf16[4,72,2304]{2,1,0:T(8,128)(2,1)S(1)}, u32[]{:S(2)}, u32[]{:S(2)}) async-start(bf16[4,72,2304]{2,1,0:T(8,128)(2,1)} %bitcast.22), calls=%async_computation.2 | async-start | bytes 2654208 | tf_op jit(solution)/shard_map/all_to_all | solution.py:44
  217.3 3.3 %shard_map.125 = bf16[128,2304]{1,0:T(8,128)(2,1)} custom-call(f32[128,2304]{1,0:T(8,128)} %get-tuple-element.194.refs_0_, bf16[128,2304]{1,0:T(8,128)(2,1)} %copy-done.44, bf16[128,2304]{1,0:T(8,128)(2,1)} %collective-permute-done.10.refs_0_.refs_2_, bf16[128,2304]{1,0:T(8,128)(2,1)} %copy-done.32, s32[5]{0:T(128)S(1)} %stack.26.at_ref.refs_4_), custom_call_target="tpu_custom_call" | custom-call | flops 1 | bytes 1 | tf_op jit(solution)/shard_map/pallas_call | solution.py:203
  222.0 2.2 shard_map.124
  224.2 11.1 %all-to-all-done.2 = bf16[4,72,2304]{2,1,0:T(8,128)(2,1)S(1)} async-done(((bf16[4,72,2304]{2,1,0:T(8,128)(2,1)}), bf16[4,72,2304]{2,1,0:T(8,128)(2,1)S(1)}, u32[]{:S(2)}, u32[]{:S(2)}) %all-to-all-start.2) | async-done | bytes 1327136 | tf_op jit(solution)/shard_map/all_to_all | solution.py:44
  236.4 3.0 %shard_map.123 = bf16[128,2304]{1,0:T(8,128)(2,1)} custom-call(bf16[128,2304]{1,0:T(8,128)(2,1)} %collective-permute-done.2.refs_0_, bf16[288,2304]{1,0:T(8,128)(2,1)} %bitcast.71, bf16[128,288]{1,0:T(8,128)(2,1)} %get-tuple-element.190.refs_2_), custom_call_target="tpu_custom_call" | custom-call | flops 1 | bytes 1 | tf_op jit(solution)/shard_map/pallas_call | solution.py:203
  239.4 3.6 %all-to-all-start.3 = ((bf16[4,72,1280]{2,1,0:T(8,128)(2,1)}), bf16[4,72,1280]{2,1,0:T(8,128)(2,1)S(1)}, u32[]{:S(2)}, u32[]{:S(2)}) async-start(bf16[4,72,1280]{2,1,0:T(8,128)(2,1)} %bitcast.24), calls=%async_computation.3 | async-start | bytes 1474560 | tf_op jit(solution)/shard_map/all_to_all | solution.py:44
  243.0 1.4 collective-permute-start.40
  244.5 2.8 %shard_map.127 = bf16[128,1280]{1,0:T(8,128)(2,1)} custom-call(f32[128,1280]{1,0:T(8,128)} %get-tuple-element.197.refs_0_, bf16[128,1280]{1,0:T(8,128)(2,1)} %copy-done.48, bf16[128,1280]{1,0:T(8,128)(2,1)} %copy-done.37, bf16[128,1280]{1,0:T(8,128)(2,1)} %copy-done.38, s32[5]{0:T(128)S(1)} %stack.26.at_ref.refs_4_), custom_call_target="tpu_custom_call" | custom-call | flops 1 | bytes 1 | tf_op jit(solution)/shard_map/pallas_call | solution.py:203
  247.4 6.4 %all-to-all-done.3 = bf16[4,72,1280]{2,1,0:T(8,128)(2,1)S(1)} async-done(((bf16[4,72,1280]{2,1,0:T(8,128)(2,1)}), bf16[4,72,1280]{2,1,0:T(8,128)(2,1)S(1)}, u32[]{:S(2)}, u32[]{:S(2)}) %all-to-all-start.3) | async-done | bytes 737312 | tf_op jit(solution)/shard_map/all_to_all | solution.py:44
  254.7 2.4 shard_map.126
  257.1 1.4 collective-permute-start.38
  260.4 6.0 %collective-permute-done.39.refs_0_ = bf16[128,1280]{1,0:T(8,128)(2,1)S(1)} collective-permute-done((bf16[128,1280]{1,0:T(8,128)(2,1)}, bf16[128,1280]{1,0:T(8,128)(2,1)S(1)}, u32[]{:S(2)}, u32[]{:S(2)}) %collective-permute-start.39) | collective-permute-done | bytes 327712 | tf_op jit(solution)/shard_map/ppermute | solution.py:26
  267.2 3.8 %collective-permute-done.38.refs_0_ = bf16[128,1280]{1,0:T(8,128)(2,1)S(1)} collective-permute-done((bf16[128,1280]{1,0:T(8,128)(2,1)}, bf16[128,1280]{1,0:T(8,128)(2,1)S(1)}, u32[]{:S(2)}, u32[]{:S(2)}) %collective-permute-start.38) | collective-permute-done | bytes 327712 | tf_op jit(solution)/shard_map/ppermute | solution.py:26
  (179 shorter events, 39.2 us)
Async XLA Ops:
  1.8 13.6 %collective-permute-start = (bf16[128,1280]{1,0:T(8,128)(2,1)S(1)}, bf16[128,1280]{1,0:T(8,128)(2,1)S(1)}, u32[]{:S(2)}, u32[]{:S(2)}) collective-permute-start(bf16[128,1280]{1,0:T(8,128)(2,1)S(1)} %get-tuple-element.203), channel_id=1, source_target_pairs={{0,114},{1,115},{2,112},{3,113},{4,118},{5,119},{6,116},{7,117},{8... | collective-permute-start | bytes 983048 | tf_op jit(solution)/shard_map/ppermute | solution.py:26
  9.8 11.4 %collective-permute-start.3 = (f32[4,128]{1,0:T(4,128)S(1)}, f32[4,128]{1,0:T(4,128)S(1)}, u32[]{:S(2)}, u32[]{:S(2)}) collective-permute-start(f32[4,128]{1,0:T(4,128)S(1)} %maximum_bitcast_fusion), channel_id=1, source_target_pairs={{0,2},{1,3},{2,0},{3,1},{4,6},{5,7},{6,4},{7,5},{8,10},{9,11},{10,... | collective-permute-start | bytes 6152 | tf_op jit(solution)/shard_map/ppermute | solution.py:34
  9.8 20.7 %collective-permute-start.4 = (bf16[128,1280]{1,0:T(8,128)(2,1)S(1)}, bf16[128,1280]{1,0:T(8,128)(2,1)S(1)}, u32[]{:S(2)}, u32[]{:S(2)}) collective-permute-start(bf16[128,1280]{1,0:T(8,128)(2,1)S(1)} %get-tuple-element.102), channel_id=1, source_target_pairs={{0,2},{1,3},{2,0},{3,1},{4,6},{5,7},{6,4},{7,5},{8,10},{9,11},{10,... | collective-permute-start | bytes 983048 | tf_op jit(solution)/shard_map/ppermute | solution.py:34
  15.4 8.5 %copy-start.36 = (bf16[128,1280]{1,0:T(8,128)(2,1)}, bf16[128,1280]{1,0:T(8,128)(2,1)S(1)}, u32[]{:S(2)}) copy-start(bf16[128,1280]{1,0:T(8,128)(2,1)S(1)} %collective-permute-done.refs_0_) | copy-start | bytes 983044
  15.4 15.3 %collective-permute-start.1 = (bf16[128,1280]{1,0:T(8,128)(2,1)S(1)}, bf16[128,1280]{1,0:T(8,128)(2,1)S(1)}, u32[]{:S(2)}, u32[]{:S(2)}) collective-permute-start(bf16[128,1280]{1,0:T(8,128)(2,1)S(1)} %get-tuple-element.102), channel_id=1, source_target_pairs={{0,114},{1,115},{2,112},{3,113},{4,118},{5,119},{6,116},{7,117},{8... | collective-permute-start | bytes 983048 | tf_op jit(solution)/shard_map/ppermute | solution.py:26
  26.2 15.2 %all-to-all-start = ((bf16[4,72,1280]{2,1,0:T(8,128)(2,1)}), bf16[4,72,1280]{2,1,0:T(8,128)(2,1)}, u32[]{:S(2)}, u32[]{:S(2)}) async-start(bf16[4,72,1280]{2,1,0:T(8,128)(2,1)} %bitcast.11), calls=%async_computation | async-start | bytes 1474560 | tf_op jit(solution)/shard_map/all_to_all | solution.py:44
  30.5 21.3 %copy-start.23 = (bf16[1,1152,256]{2,1,0:T(8,128)(2,1)S(1)}, bf16[1,1152,256]{2,1,0:T(8,128)(2,1)}, u32[]{:S(2)}) copy-start(bf16[1,1152,256]{2,1,0:T(8,128)(2,1)} %param.11) | copy-start | bytes 1769476
  30.5 21.3 %copy-start.24 = (bf16[1,1152,256]{2,1,0:T(8,128)(2,1)S(1)}, bf16[1,1152,256]{2,1,0:T(8,128)(2,1)}, u32[]{:S(2)}) copy-start(bf16[1,1152,256]{2,1,0:T(8,128)(2,1)} %param.12) | copy-start | bytes 1769476
  30.5 10.7 %collective-permute-start.5 = (bf16[128,1280]{1,0:T(8,128)(2,1)S(1)}, bf16[128,1280]{1,0:T(8,128)(2,1)S(1)}, u32[]{:S(2)}, u32[]{:S(2)}) collective-permute-start(bf16[128,1280]{1,0:T(8,128)(2,1)S(1)} %collective-permute-done.4), channel_id=1, source_target_pairs={{0,114},{1,115},{2,112},{3,113},{4,118},{5,119},{6,116},{7,117},{8... | collective-permute-start | bytes 983048 | tf_op jit(solution)/shard_map/ppermute | solution.py:26
  30.6 10.7 %copy-start.37 = (bf16[128,1280]{1,0:T(8,128)(2,1)}, bf16[128,1280]{1,0:T(8,128)(2,1)S(1)}, u32[]{:S(2)}) copy-start(bf16[128,1280]{1,0:T(8,128)(2,1)S(1)} %collective-permute-done.1.refs_0_.refs_2_) | copy-start | bytes 983044
  32.7 23.7 %collective-permute-start.2 = (bf16[128,2304]{1,0:T(8,128)(2,1)}, bf16[128,2304]{1,0:T(8,128)(2,1)}, u32[]{:S(2)}, u32[]{:S(2)}) collective-permute-start(bf16[128,2304]{1,0:T(8,128)(2,1)} %slice.41), channel_id=1, source_target_pairs={{0,114},{1,115},{2,112},{3,113},{4,118},{5,119},{6,116},{7,117},{8... | collective-permute-start | bytes 1769480 | tf_op jit(solution)/shard_map/ppermute | solution.py:26
  41.3 27.3 %collective-permute-start.6 = (bf16[288,1280]{1,0:T(8,128)(2,1)}, bf16[288,1280]{1,0:T(8,128)(2,1)}, u32[]{:S(2)}, u32[]{:S(2)}) collective-permute-start(bf16[288,1280]{1,0:T(8,128)(2,1)} %bitcast.12.refs_0_), channel_id=1, source_target_pairs={{0,2},{1,3},{2,0},{3,1},{4,6},{5,7},{6,4},{7,5},{8,10},{9,11},{10,... | collective-permute-start | bytes 2211848 | tf_op jit(solution)/shard_map/ppermute | solution.py:34
  45.7 23.0 %collective-permute-start.7 = (bf16[144,1280]{1,0:T(8,128)(2,1)}, bf16[144,1280]{1,0:T(8,128)(2,1)}, u32[]{:S(2)}, u32[]{:S(2)}) collective-permute-start(bf16[144,1280]{1,0:T(8,128)(2,1)} %get-tuple-element.113), channel_id=1, source_target_pairs={{0,4},{1,5},{2,6},{3,7},{4,8},{5,9},{6,10},{7,11},{8,12},{9,13},{1... | collective-permute-start | bytes 1105928 | tf_op jit(solution)/shard_map/ppermute | solution.py:34
  47.7 21.0 %collective-permute-start.8 = (bf16[144,1280]{1,0:T(8,128)(2,1)}, bf16[144,1280]{1,0:T(8,128)(2,1)}, u32[]{:S(2)}, u32[]{:S(2)}) collective-permute-start(bf16[144,1280]{1,0:T(8,128)(2,1)} %get-tuple-element.114), channel_id=1, source_target_pairs={{0,8},{1,9},{2,10},{3,11},{4,12},{5,13},{6,14},{7,15},{8,0},{9,1},... | collective-permute-start | bytes 1105928 | tf_op jit(solution)/shard_map/ppermute | solution.py:34
  50.4 18.3 %collective-permute-start.9 = (bf16[144,1280]{1,0:T(8,128)(2,1)S(1)}, bf16[144,1280]{1,0:T(8,128)(2,1)}, u32[]{:S(2)}, u32[]{:S(2)}) collective-permute-start(bf16[144,1280]{1,0:T(8,128)(2,1)S(1)} %get-tuple-element.115), channel_id=1, source_target_pairs={{0,12},{1,13},{2,14},{3,15},{4,0},{5,1},{6,2},{7,3},{8,4},{9,5},{1... | collective-permute-start | bytes 1105928 | tf_op jit(solution)/shard_map/ppermute | solution.py:34
  56.4 7.5 %copy-start.29 = (bf16[4,288,256]{1,2,0:T(8,128)(2,1)}, bf16[4,288,256]{1,2,0:T(8,128)(2,1)S(1)}, u32[]{:S(2)}) copy-start(bf16[4,288,256]{1,2,0:T(8,128)(2,1)S(1)} %copy.16) | copy-start | bytes 1769476
  58.6 13.6 %collective-permute-start.10 = (bf16[128,2304]{1,0:T(8,128)(2,1)}, bf16[128,2304]{1,0:T(8,128)(2,1)}, u32[]{:S(2)}, u32[]{:S(2)}) collective-permute-start(bf16[128,2304]{1,0:T(8,128)(2,1)} %slice.46), channel_id=1, source_target_pairs={{0,114},{1,115},{2,112},{3,113},{4,118},{5,119},{6,116},{7,117},{8... | collective-permute-start | bytes 1769480 | tf_op jit(solution)/shard_map/ppermute | solution.py:26
  68.7 16.1 %all-to-all-start.1 = ((bf16[4,72,2304]{2,1,0:T(8,128)(2,1)}), bf16[4,72,2304]{2,1,0:T(8,128)(2,1)S(1)}, u32[]{:S(2)}, u32[]{:S(2)}) async-start(bf16[4,72,2304]{2,1,0:T(8,128)(2,1)} %bitcast.19), calls=%async_computation.1 | async-start | bytes 2654208 | tf_op jit(solution)/shard_map/all_to_all | solution.py:44
  72.3 10.2 %collective-permute-start.11 = (bf16[128,2304]{1,0:T(8,128)(2,1)}, bf16[128,2304]{1,0:T(8,128)(2,1)S(1)}, u32[]{:S(2)}, u32[]{:S(2)}) collective-permute-start(bf16[128,2304]{1,0:T(8,128)(2,1)} %collective-permute-done.10.refs_0_.refs_2_), channel_id=1, source_target_pairs={{0,2},{1,3},{2,0},{3,1},{4,6},{5,7},{6,4},{7,5},{8,10},{9,11},{10,... | collective-permute-start | bytes 1769480 | tf_op jit(solution)/shard_map/ppermute | solution.py:34
  84.8 40.4 %copy-start.3 = (bf16[4,72,2304]{2,1,0:T(8,128)(2,1)}, bf16[4,72,2304]{2,1,0:T(8,128)(2,1)S(1)}, u32[]{:S(2)}) copy-start(bf16[4,72,2304]{2,1,0:T(8,128)(2,1)S(1)} %all-to-all-done.1) | copy-start | bytes 3981316
  84.8 7.7 %collective-permute-start.17 = (bf16[1152,1280]{1,0:T(8,128)(2,1)}, bf16[1152,1280]{1,0:T(8,128)(2,1)S(1)}, u32[]{:S(2)}, u32[]{:S(2)}) collective-permute-start(bf16[1152,1280]{1,0:T(8,128)(2,1)} %shard_map.100.refs_0_.refs_2_), channel_id=1, source_target_pairs={{0,1},{1,0},{2,3},{3,2},{4,5},{5,4},{6,7},{7,6},{8,9},{9,8},{10,11... | collective-permute-start | bytes 8847368 | tf_op jit(solution)/shard_map/ppermute | solution.py:34
  84.8 36.7 %collective-permute-start.13 = (bf16[288,2304]{1,0:T(8,128)(2,1)S(1)}, bf16[288,2304]{1,0:T(8,128)(2,1)S(1)}, u32[]{:S(2)}, u32[]{:S(2)}) collective-permute-start(bf16[288,2304]{1,0:T(8,128)(2,1)S(1)} %bitcast.57), channel_id=1, source_target_pairs={{0,2},{1,3},{2,0},{3,1},{4,6},{5,7},{6,4},{7,5},{8,10},{9,11},{10,... | collective-permute-start | bytes 3981320 | tf_op jit(solution)/shard_map/ppermute | solution.py:34
  88.3 34.4 %copy-start.11 = (bf16[144,2304]{1,0:T(8,128)(2,1)}, bf16[144,2304]{1,0:T(8,128)(2,1)S(1)}, u32[]{:S(2)}) copy-start(bf16[144,2304]{1,0:T(8,128)(2,1)S(1)} %get-tuple-element.145.refs_0_) | copy-start | bytes 1990660
  88.3 32.5 %collective-permute-start.14 = (bf16[144,2304]{1,0:T(8,128)(2,1)S(1)}, bf16[144,2304]{1,0:T(8,128)(2,1)S(1)}, u32[]{:S(2)}, u32[]{:S(2)}) collective-permute-start(bf16[144,2304]{1,0:T(8,128)(2,1)S(1)} %get-tuple-element.131), channel_id=1, source_target_pairs={{0,4},{1,5},{2,6},{3,7},{4,8},{5,9},{6,10},{7,11},{8,12},{9,13},{1... | collective-permute-start | bytes 1990664 | tf_op jit(solution)/shard_map/ppermute | solution.py:34
  89.0 31.9 %collective-permute-start.15 = (bf16[144,2304]{1,0:T(8,128)(2,1)S(1)}, bf16[144,2304]{1,0:T(8,128)(2,1)S(1)}, u32[]{:S(2)}, u32[]{:S(2)}) collective-permute-start(bf16[144,2304]{1,0:T(8,128)(2,1)S(1)} %get-tuple-element.132), channel_id=1, source_target_pairs={{0,8},{1,9},{2,10},{3,11},{4,12},{5,13},{6,14},{7,15},{8,0},{9,1},... | collective-permute-start | bytes 1990664 | tf_op jit(solution)/shard_map/ppermute | solution.py:34
  91.0 30.5 %collective-permute-start.16 = (bf16[144,2304]{1,0:T(8,128)(2,1)S(1)}, bf16[144,2304]{1,0:T(8,128)(2,1)S(1)}, u32[]{:S(2)}, u32[]{:S(2)}) collective-permute-start(bf16[144,2304]{1,0:T(8,128)(2,1)S(1)} %get-tuple-element.133), channel_id=1, source_target_pairs={{0,12},{1,13},{2,14},{3,15},{4,0},{5,1},{6,2},{7,3},{8,4},{9,5},{1... | collective-permute-start | bytes 1990664 | tf_op jit(solution)/shard_map/ppermute | solution.py:34
  92.5 30.2 %collective-permute-start.12 = (bf16[288,2304]{1,0:T(8,128)(2,1)S(1)}, bf16[288,2304]{1,0:T(8,128)(2,1)S(1)}, u32[]{:S(2)}, u32[]{:S(2)}) collective-permute-start(bf16[288,2304]{1,0:T(8,128)(2,1)S(1)} %bitcast.58), channel_id=1, source_target_pairs={{0,1},{1,0},{2,3},{3,2},{4,5},{5,4},{6,7},{7,6},{8,9},{9,8},{10,11... | collective-permute-start | bytes 3981320 | tf_op jit(solution)/shard_map/ppermute | solution.py:34
  105.7 17.0 %copy-start.2 = (bf16[1,256,7168]{2,1,0:T(8,128)(2,1)S(1)}, bf16[1,256,7168]{2,1,0:T(8,128)(2,1)}, u32[]{:S(2)}) copy-start(bf16[1,256,7168]{2,1,0:T(8,128)(2,1)} %param.15) | copy-start | bytes 11010052
  121.5 8.4 %collective-permute-start.18 = (bf16[288,2304]{1,0:T(8,128)(2,1)S(1)}, bf16[288,2304]{1,0:T(8,128)(2,1)S(1)}, u32[]{:S(2)}, u32[]{:S(2)}) collective-permute-start(bf16[288,2304]{1,0:T(8,128)(2,1)S(1)} %collective-permute-done.13.refs_0_.refs_1_), channel_id=1, source_target_pairs={{0,1},{1,0},{2,3},{3,2},{4,5},{5,4},{6,7},{7,6},{8,9},{9,8},{10,11... | collective-permute-start | bytes 3981320 | tf_op jit(solution)/shard_map/ppermute | solution.py:34
  121.6 5.1 %collective-permute-start.19 = (bf16[144,2304]{1,0:T(8,128)(2,1)S(1)}, bf16[144,2304]{1,0:T(8,128)(2,1)S(1)}, u32[]{:S(2)}, u32[]{:S(2)}) collective-permute-start(bf16[144,2304]{1,0:T(8,128)(2,1)S(1)} %get-tuple-element.145.refs_0_), channel_id=1, source_target_pairs={{0,1},{1,0},{2,3},{3,2},{4,5},{5,4},{6,7},{7,6},{8,9},{9,8},{10,11... | collective-permute-start | bytes 1990664 | tf_op jit(solution)/shard_map/ppermute | solution.py:34
  122.1 4.6 %collective-permute-start.20 = (bf16[144,2304]{1,0:T(8,128)(2,1)S(1)}, bf16[144,2304]{1,0:T(8,128)(2,1)S(1)}, u32[]{:S(2)}, u32[]{:S(2)}) collective-permute-start(bf16[144,2304]{1,0:T(8,128)(2,1)S(1)} %collective-permute-done.14.refs_1_), channel_id=1, source_target_pairs={{0,1},{1,0},{2,3},{3,2},{4,5},{5,4},{6,7},{7,6},{8,9},{9,8},{10,11... | collective-permute-start | bytes 1990664 | tf_op jit(solution)/shard_map/ppermute | solution.py:34
  122.2 5.3 %collective-permute-start.21 = (bf16[144,2304]{1,0:T(8,128)(2,1)S(1)}, bf16[144,2304]{1,0:T(8,128)(2,1)S(1)}, u32[]{:S(2)}, u32[]{:S(2)}) collective-permute-start(bf16[144,2304]{1,0:T(8,128)(2,1)S(1)} %collective-permute-done.15.refs_2_), channel_id=1, source_target_pairs={{0,1},{1,0},{2,3},{3,2},{4,5},{5,4},{6,7},{7,6},{8,9},{9,8},{10,11... | collective-permute-start | bytes 1990664 | tf_op jit(solution)/shard_map/ppermute | solution.py:34
  122.6 5.8 %collective-permute-start.22 = (bf16[144,2304]{1,0:T(8,128)(2,1)S(1)}, bf16[144,2304]{1,0:T(8,128)(2,1)S(1)}, u32[]{:S(2)}, u32[]{:S(2)}) collective-permute-start(bf16[144,2304]{1,0:T(8,128)(2,1)S(1)} %collective-permute-done.16.refs_3_), channel_id=1, source_target_pairs={{0,1},{1,0},{2,3},{3,2},{4,5},{5,4},{6,7},{7,6},{8,9},{9,8},{10,11... | collective-permute-start | bytes 1990664 | tf_op jit(solution)/shard_map/ppermute | solution.py:34
  133.1 9.0 %copy-start.6 = (bf16[1152,256]{1,0:T(8,128)(2,1)}, bf16[1152,256]{1,0:T(8,128)(2,1)S(1)}, u32[]{:S(2)}) copy-start(bf16[1152,256]{1,0:T(8,128)(2,1)S(1)} %get-tuple-element.168.refs_2_.refs_3_) | copy-start | bytes 1769476
  133.1 9.0 %copy-start.7 = (bf16[1152,256]{1,0:T(8,128)(2,1)}, bf16[1152,256]{1,0:T(8,128)(2,1)S(1)}, u32[]{:S(2)}) copy-start(bf16[1152,256]{1,0:T(8,128)(2,1)S(1)} %get-tuple-element.169.refs_3_.refs_4_) | copy-start | bytes 1769476
  133.1 12.6 %copy-start.4 = (bf16[1152,256]{1,0:T(8,128)(2,1)}, bf16[1152,256]{1,0:T(8,128)(2,1)S(1)}, u32[]{:S(2)}) copy-start(bf16[1152,256]{1,0:T(8,128)(2,1)S(1)} %get-tuple-element.162.refs_2_.refs_3_) | copy-start | bytes 1769476
  133.1 12.6 %copy-start.5 = (bf16[1152,256]{1,0:T(8,128)(2,1)}, bf16[1152,256]{1,0:T(8,128)(2,1)S(1)}, u32[]{:S(2)}) copy-start(bf16[1152,256]{1,0:T(8,128)(2,1)S(1)} %get-tuple-element.163.refs_3_.refs_4_) | copy-start | bytes 1769476
  136.1 6.0 %collective-permute-start.27 = (bf16[576,2304]{1,0:T(8,128)(2,1)S(1)}, bf16[576,2304]{1,0:T(8,128)(2,1)S(1)}, u32[]{:S(2)}, u32[]{:S(2)}) collective-permute-start(bf16[576,2304]{1,0:T(8,128)(2,1)S(1)} %shard_map.112), channel_id=1, source_target_pairs={{0,1},{1,0},{2,3},{3,2},{4,5},{5,4},{6,7},{7,6},{8,9},{9,8},{10,11... | collective-permute-start | bytes 7962632 | tf_op jit(solution)/shard_map/ppermute | solution.py:34
  138.3 7.4 %collective-permute-start.23 = (bf16[576,2304]{1,0:T(8,128)(2,1)S(1)}, bf16[576,2304]{1,0:T(8,128)(2,1)S(1)}, u32[]{:S(2)}, u32[]{:S(2)}) collective-permute-start(bf16[576,2304]{1,0:T(8,128)(2,1)S(1)} %shard_map.110), channel_id=1, source_target_pairs={{0,1},{1,0},{2,3},{3,2},{4,5},{5,4},{6,7},{7,6},{8,9},{9,8},{10,11... | collective-permute-start | bytes 7962632 | tf_op jit(solution)/shard_map/ppermute | solution.py:34
  140.1 10.3 %collective-permute-start.30 = (bf16[576,1280]{1,0:T(8,128)(2,1)S(1)}, bf16[576,1280]{1,0:T(8,128)(2,1)S(1)}, u32[]{:S(2)}, u32[]{:S(2)}) collective-permute-start(bf16[576,1280]{1,0:T(8,128)(2,1)S(1)} %shard_map.116), channel_id=1, source_target_pairs={{0,1},{1,0},{2,3},{3,2},{4,5},{5,4},{6,7},{7,6},{8,9},{9,8},{10,11... | collective-permute-start | bytes 4423688 | tf_op jit(solution)/shard_map/ppermute | solution.py:34
  141.6 26.8 %collective-permute-start.29 = (bf16[576,1280]{1,0:T(8,128)(2,1)S(1)}, bf16[576,1280]{1,0:T(8,128)(2,1)S(1)}, u32[]{:S(2)}, u32[]{:S(2)}) collective-permute-start(bf16[576,1280]{1,0:T(8,128)(2,1)S(1)} %shard_map.114), channel_id=1, source_target_pairs={{0,1},{1,0},{2,3},{3,2},{4,5},{5,4},{6,7},{7,6},{8,9},{9,8},{10,11... | collective-permute-start | bytes 4423688 | tf_op jit(solution)/shard_map/ppermute | solution.py:34
  144.1 38.4 %collective-permute-start.28 = (bf16[288,2304]{1,0:T(8,128)(2,1)S(1)}, bf16[288,2304]{1,0:T(8,128)(2,1)S(1)}, u32[]{:S(2)}, u32[]{:S(2)}) collective-permute-start(bf16[288,2304]{1,0:T(8,128)(2,1)S(1)} %get-tuple-element.161), channel_id=1, source_target_pairs={{0,2},{1,3},{2,0},{3,1},{4,6},{5,7},{6,4},{7,5},{8,10},{9,11},{10,... | collective-permute-start | bytes 3981320 | tf_op jit(solution)/shard_map/ppermute | solution.py:34
  147.7 10.2 %copy-start.22 = (bf16[144,2304]{1,0:T(8,128)(2,1)}, bf16[144,2304]{1,0:T(8,128)(2,1)S(1)}, u32[]{:S(2)}) copy-start(bf16[144,2304]{1,0:T(8,128)(2,1)S(1)} %get-tuple-element.155.refs_0_) | copy-start | bytes 1990660
  147.8 31.1 %collective-permute-start.24 = (bf16[144,2304]{1,0:T(8,128)(2,1)S(1)}, bf16[144,2304]{1,0:T(8,128)(2,1)S(1)}, u32[]{:S(2)}, u32[]{:S(2)}) collective-permute-start(bf16[144,2304]{1,0:T(8,128)(2,1)S(1)} %get-tuple-element.156), channel_id=1, source_target_pairs={{0,12},{1,13},{2,14},{3,15},{4,0},{5,1},{6,2},{7,3},{8,4},{9,5},{1... | collective-permute-start | bytes 1990664 | tf_op jit(solution)/shard_map/ppermute | solution.py:34
  150.4 28.4 %collective-permute-start.25 = (bf16[144,2304]{1,0:T(8,128)(2,1)S(1)}, bf16[144,2304]{1,0:T(8,128)(2,1)S(1)}, u32[]{:S(2)}, u32[]{:S(2)}) collective-permute-start(bf16[144,2304]{1,0:T(8,128)(2,1)S(1)} %get-tuple-element.157), channel_id=1, source_target_pairs={{0,8},{1,9},{2,10},{3,11},{4,12},{5,13},{6,14},{7,15},{8,0},{9,1},... | collective-permute-start | bytes 1990664 | tf_op jit(solution)/shard_map/ppermute | solution.py:34
  150.4 7.5 %copy-start.34 = (bf16[576,1280]{1,0:T(8,128)(2,1)}, bf16[576,1280]{1,0:T(8,128)(2,1)S(1)}, u32[]{:S(2)}) copy-start(bf16[576,1280]{1,0:T(8,128)(2,1)S(1)} %collective-permute-done.30.refs_2_) | copy-start | bytes 4423684
  150.5 32.1 %collective-permute-start.26 = (bf16[144,2304]{1,0:T(8,128)(2,1)S(1)}, bf16[144,2304]{1,0:T(8,128)(2,1)S(1)}, u32[]{:S(2)}, u32[]{:S(2)}) collective-permute-start(bf16[144,2304]{1,0:T(8,128)(2,1)S(1)} %get-tuple-element.158), channel_id=1, source_target_pairs={{0,4},{1,5},{2,6},{3,7},{4,8},{5,9},{6,10},{7,11},{8,12},{9,13},{1... | collective-permute-start | bytes 1990664 | tf_op jit(solution)/shard_map/ppermute | solution.py:34
  168.4 14.2 %copy-start.49 = (bf16[288,1280]{1,0:T(8,128)(2,1)S(1)}, bf16[288,1280]{1,0:T(8,128)(2,1)}, u32[]{:S(2)}) copy-start(bf16[288,1280]{1,0:T(8,128)(2,1)} %get-tuple-element.186) | copy-start | bytes 2211844
  173.0 15.3 %copy-start.27 = (bf16[144,1280]{1,0:T(8,128)(2,1)}, bf16[144,1280]{1,0:T(8,128)(2,1)S(1)}, u32[]{:S(2)}) copy-start(bf16[144,1280]{1,0:T(8,128)(2,1)S(1)} %get-tuple-element.181.refs_0_) | copy-start | bytes 1105924
  182.6 31.1 %collective-permute-start.35 = (bf16[288,1280]{1,0:T(8,128)(2,1)S(1)}, bf16[288,1280]{1,0:T(8,128)(2,1)S(1)}, u32[]{:S(2)}, u32[]{:S(2)}) collective-permute-start(bf16[288,1280]{1,0:T(8,128)(2,1)S(1)} %copy-done.49), channel_id=1, source_target_pairs={{0,2},{1,3},{2,0},{3,1},{4,6},{5,7},{6,4},{7,5},{8,10},{9,11},{10,... | collective-permute-start | bytes 2211848 | tf_op jit(solution)/shard_map/ppermute | solution.py:34
  188.3 25.4 %collective-permute-start.31 = (bf16[128,2304]{1,0:T(8,128)(2,1)}, bf16[128,2304]{1,0:T(8,128)(2,1)S(1)}, u32[]{:S(2)}, u32[]{:S(2)}) collective-permute-start(bf16[128,2304]{1,0:T(8,128)(2,1)} %get-tuple-element.180), channel_id=1, source_target_pairs={{0,2},{1,3},{2,0},{3,1},{4,6},{5,7},{6,4},{7,5},{8,10},{9,11},{10,... | collective-permute-start | bytes 1769480 | tf_op jit(solution)/shard_map/ppermute | solution.py:34
  189.4 11.5 %collective-permute-start.32 = (bf16[144,1280]{1,0:T(8,128)(2,1)S(1)}, bf16[144,1280]{1,0:T(8,128)(2,1)S(1)}, u32[]{:S(2)}, u32[]{:S(2)}) collective-permute-start(bf16[144,1280]{1,0:T(8,128)(2,1)S(1)} %get-tuple-element.182), channel_id=1, source_target_pairs={{0,12},{1,13},{2,14},{3,15},{4,0},{5,1},{6,2},{7,3},{8,4},{9,5},{1... | collective-permute-start | bytes 1105928 | tf_op jit(solution)/shard_map/ppermute | solution.py:34
  190.0 13.1 %collective-permute-start.33 = (bf16[144,1280]{1,0:T(8,128)(2,1)S(1)}, bf16[144,1280]{1,0:T(8,128)(2,1)S(1)}, u32[]{:S(2)}, u32[]{:S(2)}) collective-permute-start(bf16[144,1280]{1,0:T(8,128)(2,1)S(1)} %get-tuple-element.183), channel_id=1, source_target_pairs={{0,8},{1,9},{2,10},{3,11},{4,12},{5,13},{6,14},{7,15},{8,0},{9,1},... | collective-permute-start | bytes 1105928 | tf_op jit(solution)/shard_map/ppermute | solution.py:34
  190.3 18.6 %collective-permute-start.34 = (bf16[144,1280]{1,0:T(8,128)(2,1)S(1)}, bf16[144,1280]{1,0:T(8,128)(2,1)S(1)}, u32[]{:S(2)}, u32[]{:S(2)}) collective-permute-start(bf16[144,1280]{1,0:T(8,128)(2,1)S(1)} %get-tuple-element.184), channel_id=1, source_target_pairs={{0,4},{1,5},{2,6},{3,7},{4,8},{5,9},{6,10},{7,11},{8,12},{9,13},{1... | collective-permute-start | bytes 1105928 | tf_op jit(solution)/shard_map/ppermute | solution.py:34
  200.9 7.9 %copy-start.45 = (bf16[144,1280]{1,0:T(8,128)(2,1)}, bf16[144,1280]{1,0:T(8,128)(2,1)S(1)}, u32[]{:S(2)}) copy-start(bf16[144,1280]{1,0:T(8,128)(2,1)S(1)} %collective-permute-done.32.refs_1_) | copy-start | bytes 1105924
  203.1 5.8 %copy-start.46 = (bf16[144,1280]{1,0:T(8,128)(2,1)}, bf16[144,1280]{1,0:T(8,128)(2,1)S(1)}, u32[]{:S(2)}) copy-start(bf16[144,1280]{1,0:T(8,128)(2,1)S(1)} %collective-permute-done.33.refs_2_) | copy-start | bytes 1105924
  213.7 6.9 %copy-start.39 = (bf16[288,1280]{1,0:T(8,128)(2,1)}, bf16[288,1280]{1,0:T(8,128)(2,1)S(1)}, u32[]{:S(2)}) copy-start(bf16[288,1280]{1,0:T(8,128)(2,1)S(1)} %collective-permute-done.35.refs_1_) | copy-start | bytes 2211844
  213.7 21.6 %all-to-all-start.2 = ((bf16[4,72,2304]{2,1,0:T(8,128)(2,1)}), bf16[4,72,2304]{2,1,0:T(8,128)(2,1)S(1)}, u32[]{:S(2)}, u32[]{:S(2)}) async-start(bf16[4,72,2304]{2,1,0:T(8,128)(2,1)} %bitcast.22), calls=%async_computation.2 | async-start | bytes 2654208 | tf_op jit(solution)/shard_map/all_to_all | solution.py:44
  220.6 18.8 %collective-permute-start.37 = (bf16[128,2304]{1,0:T(8,128)(2,1)}, bf16[128,2304]{1,0:T(8,128)(2,1)S(1)}, u32[]{:S(2)}, u32[]{:S(2)}) collective-permute-start(bf16[128,2304]{1,0:T(8,128)(2,1)} %shard_map.125), channel_id=1, source_target_pairs={{0,114},{1,115},{2,112},{3,113},{4,118},{5,119},{6,116},{7,117},{8... | collective-permute-start | bytes 1769480 | tf_op jit(solution)/shard_map/ppermute | solution.py:26
  221.6 17.8 %collective-permute-start.36 = (bf16[128,1280]{1,0:T(8,128)(2,1)S(1)}, bf16[128,1280]{1,0:T(8,128)(2,1)S(1)}, u32[]{:S(2)}, u32[]{:S(2)}) collective-permute-start(bf16[128,1280]{1,0:T(8,128)(2,1)S(1)} %copy-done.50), channel_id=1, source_target_pairs={{0,2},{1,3},{2,0},{3,1},{4,6},{5,7},{6,4},{7,5},{8,10},{9,11},{10,... | collective-permute-start | bytes 983048 | tf_op jit(solution)/shard_map/ppermute | solution.py:34
  239.4 14.5 %all-to-all-start.3 = ((bf16[4,72,1280]{2,1,0:T(8,128)(2,1)}), bf16[4,72,1280]{2,1,0:T(8,128)(2,1)S(1)}, u32[]{:S(2)}, u32[]{:S(2)}) async-start(bf16[4,72,1280]{2,1,0:T(8,128)(2,1)} %bitcast.24), calls=%async_computation.3 | async-start | bytes 1474560 | tf_op jit(solution)/shard_map/all_to_all | solution.py:44
  243.0 16.4 %collective-permute-start.40 = (bf16[128,2304]{1,0:T(8,128)(2,1)S(1)}, bf16[128,2304]{1,0:T(8,128)(2,1)S(1)}, u32[]{:S(2)}, u32[]{:S(2)}) collective-permute-start(bf16[128,2304]{1,0:T(8,128)(2,1)S(1)} %copy-done.43), channel_id=1, source_target_pairs={{0,112},{1,113},{2,114},{3,115},{4,116},{5,117},{6,118},{7,119},{8... | collective-permute-start | bytes 1769480 | tf_op jit(solution)/shard_map/ppermute | solution.py:26
  247.3 19.1 %collective-permute-start.39 = (bf16[128,1280]{1,0:T(8,128)(2,1)}, bf16[128,1280]{1,0:T(8,128)(2,1)S(1)}, u32[]{:S(2)}, u32[]{:S(2)}) collective-permute-start(bf16[128,1280]{1,0:T(8,128)(2,1)} %shard_map.127), channel_id=1, source_target_pairs={{0,114},{1,115},{2,112},{3,113},{4,118},{5,119},{6,116},{7,117},{8... | collective-permute-start | bytes 983048 | tf_op jit(solution)/shard_map/ppermute | solution.py:26
  257.1 13.9 %collective-permute-start.38 = (bf16[128,1280]{1,0:T(8,128)(2,1)}, bf16[128,1280]{1,0:T(8,128)(2,1)S(1)}, u32[]{:S(2)}, u32[]{:S(2)}) collective-permute-start(bf16[128,1280]{1,0:T(8,128)(2,1)} %shard_map.126), channel_id=1, source_target_pairs={{0,112},{1,113},{2,114},{3,115},{4,116},{5,117},{6,118},{7,119},{8... | collective-permute-start | bytes 983048 | tf_op jit(solution)/shard_map/ppermute | solution.py:26
  (32 other events, 81.4 us)
where the time goes:
time: 273 us; the launch traced here: 272 us
  Pallas kernels  96.1 us (35%)
  waiting for transfers between devices  87.6 us (32%)
  starting transfers between devices  63.3 us (23%)
  local copies, waits for them, and re-layouts  19.2 us (7%)
  other arithmetic  4.06 us (1%)
    pallas_call x23, Pallas kernels, over_columns(): pl.pallas_call(kernel, in_specs=specs, out_specs=[hbm] * n_out + [pl.Bloc...  74.5 us
    ppermute x32, waiting for transfers between devices, ep_move(): return lax.ppermute(array, 'ep', pairs)  48.3 us
    ppermute x32, starting transfers between devices, ep_move(): return lax.ppermute(array, 'ep', pairs)  26 us
    ppermute x9, starting transfers between devices, section_move(): return lax.ppermute(array, ('section', 'ep'), pairs)  22.3 us
    all_to_all x4, waiting for transfers between devices, x_exchange(): lax.all_to_all(blocks, 'ep', 0, 0, axis_index_groups=groups, tiled=True)  20 us
    ppermute x9, waiting for transfers between devices, section_move(): return lax.ppermute(array, ('section', 'ep'), pairs)  19.4 us
    pallas_call x11, Pallas kernels, at_once(): pl.pallas_call(kernel, in_specs=specs, out_specs=[whole(shape) for shape,...  16.9 us
    all_to_all x4, starting transfers between devices, x_exchange(): lax.all_to_all(blocks, 'ep', 0, 0, axis_index_groups=groups, tiled=True)  15 us
  transfers between devices with their start and end apart: 45, of which 19 were waited for; matrix products, arithmetic and copies ran while one was open for 4% of the time, Pallas kernels for 33%

commit v1 on v0

--- a/solution.py
+++ b/solution.py
@@ -574,15 +574,10 @@
         return s % NY == NY - 1
 
     tok_a0 = section_move(own[:, :a0], crossing)
-    own_b0 = own[:, a0:early]
-    next_b0 = ep_move(own_b0, dz=1)
     info = jnp.concatenate([expert_ids[0].astype(F32), route_weight[0]], axis=1).T
     info_far = ep_move(info, dz=1)
-    tok_b0 = section_move(release(own_b0, tok_a0), crossing)
-    far_tok0 = section_move(next_b0, crossing)
-    own_late = release(own, tok_b0)
-    tok_a1 = section_move(own_late[:, early : early + a1], crossing)
-    tok_b1 = section_move(release(own_late, tok_a1)[:, early + a1 :], crossing)
+    tok_b0 = section_move(own[:, a0:early], crossing)
+    tok1 = section_move(release(own, tok_b0)[:, early:], crossing)
     section = lax.axis_index("section").astype(jnp.int32)
     position = lax.axis_index("ep").astype(jnp.int32)
     turned = (section % NY == NY - 1).astype(jnp.int32)
@@ -596,7 +591,7 @@
     )
 
     near_a0 = x_exchange(pack_a(place, weight, tok_a0, 0, a0))
-    near_a0, tok_b0, far_tok0, at_later = tie((near_a0, tok_b0, far_tok0, at))
+    near_a0, far_tok0, at_later = tie((near_a0, ep_move(tok_b0, dz=1), at))
     far_a0 = ep_move(near_a0, dz=1)
     sent_b0 = pack_b(place0, weight0, place1, weight1, tok_b0, 0, far_tok0, cap)
     got_b0 = x_moves(sent_b0, 1)
@@ -604,9 +599,9 @@
     hid_at = hid_a.reshape(NC * NZ, -1, hid).transpose(0, 2, 1)
     hid_bt = hid_b.reshape(NC, -1, hid).transpose(0, 2, 1)
     hid_near = jnp.stack([hid_at[0], hid_at[2], hid_at[1], hid_at[3]])
-    packed_a1 = pack_a(place, weight, tok_a1, 0, a1)
-    far_a0, got_b0, packed_a1, f1, f2, hid_at, hid_bt, hid_near = tie(
-        (far_a0, got_b0, packed_a1, f1, f2, hid_at, hid_bt, hid_near)
+    packed_a1, tok_b1 = pack_a(place, weight, tok1, 0, a1), tok1[:, a1:]
+    far_a0, got_b0, packed_a1, tok_b1, f1, f2, hid_at, hid_bt, hid_near = tie(
+        (far_a0, got_b0, packed_a1, tok_b1, f1, f2, hid_at, hid_bt, hid_near)
     )
     near_a1 = x_exchange(packed_a1)
     far_tok1 = ep_move(tok_b1, dz=1)
@@ -668,22 +663,22 @@
     back_a0 = ep_move(send_a0, dz=1)
     keep_b1, send_b1 = combine_b(keep_t, send_t, [part_b1[0]] + back_b1)
     cross_b1 = ep_move(send_b1, dz=1)
-    keep_b0, send_b0 = combine_b(keep_t, send_t, [part_b0[0]] + back_b0)
     sum_a1 = sum_z(keep_a1, back_a1)
-    cross_b1, send_b0, back_a0, sum_a1 = tie((cross_b1, send_b0, back_a0, sum_a1))
+    cross_b1, back_b0, back_a0, sum_a1 = tie((cross_b1, back_b0, back_a0, sum_a1))
     own_a1 = x_exchange(sum_a1)
     up_b1 = section_move(finish_b(at, keep_b1, cross_b1, tok_b1, 0, far_tok1), crossing)
+    keep_b0, send_b0 = combine_b(keep_t, send_t, [part_b0[0]] + back_b0)
     cross_b0 = ep_move(send_b0, dz=1)
     sum_a0 = sum_z(keep_a0, back_a0)
-    done_a1 = finish_a(place_t, tok_a1, 0, own_a1)
-    done_a1, cross_b0, sum_a0, up_b1 = tie((done_a1, cross_b0, sum_a0, up_b1))
-    up_a1 = section_move(done_a1, swapped)
+    done_b0 = finish_b(at, keep_b0, cross_b0, tok_b0, 0, far_tok0)
+    done_b0, sum_a0, up_b1 = tie((done_b0, sum_a0, up_b1))
+    up_b0 = section_move(done_b0, crossing)
+    up_a1 = section_move(release(finish_a(place_t, tok1, 0, own_a1), up_b0), swapped)
     own_a0 = x_exchange(sum_a0)
-    up_b0 = section_move(finish_b(at, keep_b0, cross_b0, tok_b0, 0, far_tok0), crossing)
     up_a0 = section_move(finish_a(place_t, tok_a0, 0, own_a0), swapped)
     out = place_chunk(up_b1, width, at_b1, None)
+    out = place_chunk(up_b0, width, at_b0, out)
     out = place_chunk(up_a1, width, at_a1, out)
-    out = place_chunk(up_b0, width, at_b0, out)
     out = place_chunk(up_a0, width, at_a0, out)
     return (out[None], grad[None])
 

time: 273 us -> 268 us (0.982)
    ppermute x32, waiting for transfers between devices: 48.3 us -> 70 us  [ep_move(): return lax.ppermute(array, 'ep', pairs)]
    all_to_all x4, waiting for transfers between devices: 20 us -> 7.85 us  [x_exchange(): lax.all_to_all(blocks, 'ep', 0, 0, axis_index_groups=groups, tiled=True)]
    ppermute x9 -> x7, waiting for transfers between devices: 19.4 us -> 7.77 us  [section_move(): return lax.ppermute(array, ('section', 'ep'), pairs)]
    ppermute x9 -> x7, starting transfers between devices: 22.3 us -> 21.4 us  [section_move(): return lax.ppermute(array, ('section', 'ep'), pairs)]
    unnamed x102 -> x98, local copies, waits for them, and re-layouts: 10.3 us -> 10.1 us
  transfers between devices with their start and end apart: 45 -> 43, of which waited for: 19 -> 21; matrix products, arithmetic and copies ran while one was open for 4% -> 4% of each run, Pallas kernels for 33% -> 34%
where the time goes in v1:
time: 268 us; the launch traced here: 267 us
  Pallas kernels  96.2 us (36%)
  waiting for transfers between devices  85.6 us (32%)
  starting transfers between devices  62.4 us (23%)
  local copies, waits for them, and re-layouts  17.7 us (7%)
  other arithmetic  3.12 us (1%)
    pallas_call x23, Pallas kernels, over_columns(): pl.pallas_call(kernel, in_specs=specs, out_specs=[hbm] * n_out + [pl.Bloc...  74.5 us
    ppermute x32, waiting for transfers between devices, ep_move(): return lax.ppermute(array, 'ep', pairs)  70 us
    ppermute x32, starting transfers between devices, ep_move(): return lax.ppermute(array, 'ep', pairs)  24.6 us
    ppermute x7, starting transfers between devices, section_move(): return lax.ppermute(array, ('section', 'ep'), pairs)  21.4 us
    pallas_call x11, Pallas kernels, at_once(): pl.pallas_call(kernel, in_specs=specs, out_specs=[whole(shape) for shape,...  16.9 us
    all_to_all x4, starting transfers between devices, x_exchange(): lax.all_to_all(blocks, 'ep', 0, 0, axis_index_groups=groups, tiled=True)  16.3 us
    unnamed x98, local copies, waits for them, and re-layouts  10.1 us
    all_to_all x4, waiting for transfers between devices, x_exchange(): lax.all_to_all(blocks, 'ep', 0, 0, axis_index_groups=groups, tiled=True)  7.85 us
  transfers between devices with their start and end apart: 43, of which 21 were waited for; matrix products, arithmetic and copies ran while one was open for 4% of the time, Pallas kernels for 34%

profile of v1, /device:TPU:0, one launch (start us, length us, event | category | flops | bytes accessed | tf_op | source)
XLA Modules:
  0.0 266.6 jit_solution(11993817808011058123)
XLA Ops:
  1.8 6.6 %collective-permute-start = (bf16[128,1280]{1,0:T(8,128)(2,1)S(1)}, bf16[128,1280]{1,0:T(8,128)(2,1)S(1)}, u32[]{:S(2)}, u32[]{:S(2)}) collective-permute-start(bf16[128,1280]{1,0:T(8,128)(2,1)S(1)} %get-tuple-element.203), channel_id=1, source_target_pairs={{0,114},{1,115},{2,112},{3,113},{4,118},{5,119},{6,116},{7,117},{8... | collective-permute-start | bytes 983048 | tf_op jit(solution)/shard_map/ppermute | solution.py:26
  11.0 2.4 collective-permute-done.1
  14.0 2.0 shard_map.95
  17.2 2.3 shard_map.96
  19.6 4.3 %all-to-all-start = ((bf16[4,72,1280]{2,1,0:T(8,128)(2,1)}), bf16[4,72,1280]{2,1,0:T(8,128)(2,1)}, u32[]{:S(2)}, u32[]{:S(2)}) async-start(bf16[4,72,1280]{2,1,0:T(8,128)(2,1)} %bitcast.11), calls=%async_computation | async-start | bytes 1474560 | tf_op jit(solution)/shard_map/all_to_all | solution.py:44
  23.9 2.5 slice.41
  26.4 5.8 %collective-permute-start.8 = (bf16[128,4608]{1,0:T(8,128)(2,1)}, bf16[128,4608]{1,0:T(8,128)(2,1)}, u32[]{:S(2)}, u32[]{:S(2)}) collective-permute-start(bf16[128,4608]{1,0:T(8,128)(2,1)} %slice.41), channel_id=1, source_target_pairs={{0,114},{1,115},{2,112},{3,113},{4,118},{5,119},{6,116},{7,117},{8... | collective-permute-start | bytes 3538952 | tf_op jit(solution)/shard_map/ppermute | solution.py:26
  32.2 7.5 %collective-permute-done.3.refs_1_.refs_3_ = bf16[128,1280]{1,0:T(8,128)(2,1)S(1)} collective-permute-done((bf16[128,1280]{1,0:T(8,128)(2,1)S(1)}, bf16[128,1280]{1,0:T(8,128)(2,1)S(1)}, u32[]{:S(2)}, u32[]{:S(2)}) %collective-permute-start.3) | collective-permute-done | bytes 327712 | tf_op jit(solution)/shard_map/ppermute | solution.py:34
  40.4 2.9 %shard_map.97 = (bf16[144,1280]{1,0:T(8,128)(2,1)S(1)}, bf16[144,1280]{1,0:T(8,128)(2,1)}, bf16[144,1280]{1,0:T(8,128)(2,1)}, bf16[144,1280]{1,0:T(8,128)(2,1)S(1)}) custom-call(bf16[128,1280]{1,0:T(8,128)(2,1)} %copy-done.37, bf16[128,1280]{1,0:T(8,128)(2,1)} %copy-done.38, bf16[288,128]{1,0:T(8,128)(2,1)} %get-tuple-element.106.refs_2_, ...), custom_call_target="tpu_custom_call" | custom-call | flops 1 | bytes 1 | tf_op jit(solution)/shard_map/pallas_call | solution.py:203
  44.1 2.4 collective-permute-start.5
  46.5 2.7 %collective-permute-start.6 = (bf16[144,1280]{1,0:T(8,128)(2,1)}, bf16[144,1280]{1,0:T(8,128)(2,1)}, u32[]{:S(2)}, u32[]{:S(2)}) collective-permute-start(bf16[144,1280]{1,0:T(8,128)(2,1)} %get-tuple-element.111), channel_id=1, source_target_pairs={{0,8},{1,9},{2,10},{3,11},{4,12},{5,13},{6,14},{7,15},{8,0},{9,1},... | collective-permute-start | bytes 1105928 | tf_op jit(solution)/shard_map/ppermute | solution.py:34
  49.2 1.5 collective-permute-start.7
  50.6 1.3 shard_map.99
  53.8 1.4 copy.16
  57.5 2.8 %shard_map.98 = bf16[288,2304]{1,0:T(8,128)(2,1)} custom-call(bf16[128,4608]{1,0:T(8,128)(2,1)} %collective-permute-done.8.refs_0_, bf16[288,128]{1,0:T(8,128)(2,1)} %get-tuple-element.102.refs_1_, f32[288,128]{1,0:T(8,128)} %get-tuple-element.103.refs_2_), custom_call_target="tpu_custom_call" | custom-call | flops 1 | bytes 1 | tf_op jit(solution)/shard_map/pallas_call | solution.py:203
  61.5 4.0 %all-to-all-start.1 = ((bf16[4,72,2304]{2,1,0:T(8,128)(2,1)}), bf16[4,72,2304]{2,1,0:T(8,128)(2,1)S(1)}, u32[]{:S(2)}, u32[]{:S(2)}) async-start(bf16[4,72,2304]{2,1,0:T(8,128)(2,1)} %bitcast.19), calls=%async_computation.1 | async-start | bytes 2654208 | tf_op jit(solution)/shard_map/all_to_all | solution.py:44
  66.5 3.2 %shard_map.100.refs_0_.refs_2_ = bf16[1152,1280]{1,0:T(8,128)(2,1)} custom-call(bf16[288,1280]{1,0:T(8,128)(2,1)} %bitcast.12.refs_0_, bf16[288,1280]{1,0:T(8,128)(2,1)} %collective-permute-done.4.refs_1_, bf16[144,1280]{1,0:T(8,128)(2,1)} %copy-done.26, bf16[144,1280]{1,0:T(8,128)(2,1)} %collective-permute-done.5.refs_3_, ...), custom_call_target="tpu_custom_call" | custom-call | flops 1 | bytes 1 | tf_op jit(solution)/shard_map/pallas_call | solution.py:203
  69.7 7.7 %collective-permute-done.9.refs_1_.refs_3_ = bf16[128,2304]{1,0:T(8,128)(2,1)} collective-permute-done((bf16[128,2304]{1,0:T(8,128)(2,1)S(1)}, bf16[128,2304]{1,0:T(8,128)(2,1)}, u32[]{:S(2)}, u32[]{:S(2)}) %collective-permute-start.9) | collective-permute-done | bytes 589856 | tf_op jit(solution)/shard_map/ppermute | solution.py:34
  77.4 3.2 %all-to-all-done.1 = bf16[4,72,2304]{2,1,0:T(8,128)(2,1)S(1)} async-done(((bf16[4,72,2304]{2,1,0:T(8,128)(2,1)}), bf16[4,72,2304]{2,1,0:T(8,128)(2,1)S(1)}, u32[]{:S(2)}, u32[]{:S(2)}) %all-to-all-start.1) | async-done | bytes 1327136 | tf_op jit(solution)/shard_map/all_to_all | solution.py:44
  81.3 3.0 %shard_map.101 = (bf16[144,2304]{1,0:T(8,128)(2,1)S(1)}, bf16[144,2304]{1,0:T(8,128)(2,1)S(1)}, bf16[144,2304]{1,0:T(8,128)(2,1)S(1)}, bf16[144,2304]{1,0:T(8,128)(2,1)S(1)}) custom-call(bf16[128,2304]{1,0:T(8,128)(2,1)} %copy-done.31, bf16[128,2304]{1,0:T(8,128)(2,1)} %collective-permute-done.9.refs_1_.refs_3_, ...), custom_call_target="tpu_custom_call" | custom-call | flops 1 | bytes 1 | tf_op jit(solution)/shard_map/pallas_call | solution.py:203
  85.0 2.7 %collective-permute-start.13 = (bf16[144,2304]{1,0:T(8,128)(2,1)S(1)}, bf16[144,2304]{1,0:T(8,128)(2,1)S(1)}, u32[]{:S(2)}, u32[]{:S(2)}) collective-permute-start(bf16[144,2304]{1,0:T(8,128)(2,1)S(1)} %get-tuple-element.130), channel_id=1, source_target_pairs={{0,8},{1,9},{2,10},{3,11},{4,12},{5,13},{6,14},{7,15},{8,0},{9,1},... | collective-permute-start | bytes 1990664 | tf_op jit(solution)/shard_map/ppermute | solution.py:34
  88.2 1.6 copy-done.28
  89.8 6.0 %shard_map.102 = (f32[256,7168]{1,0:T(8,128)}, f32[1152,256]{1,0:T(8,128)S(1)}) custom-call(bf16[1152,1280]{1,0:T(8,128)(2,1)} %shard_map.100.refs_0_.refs_2_, bf16[1152,1280]{1,0:T(8,128)(2,1)} %copy-done.28, bf16[1152,1280]{1,0:T(8,128)(2,1)} %shard_map.100.refs_0_.refs_2_, bf16[1152,1280]{1,0:T(8,128)(2,1)} %copy-done.28, bf16[256,7168]{1,0:T(8,128)(2,1)} %bitcast.50, ...), custom_call_target="tpu_custom_call" | custom-call | flops 1 | bytes 1 | tf_op jit(solution)/shard_map/pallas_call | solution.py:203
  95.9 5.6 %shard_map.103 = (f32[256,7168]{1,0:T(8,128)}, f32[1152,256]{1,0:T(8,128)S(1)}) custom-call(bf16[1152,1280]{1,0:T(8,128)(2,1)} %shard_map.100.refs_0_.refs_2_, bf16[1152,1280]{1,0:T(8,128)(2,1)} %copy-done.28, bf16[256,7168]{1,0:T(8,128)(2,1)} %bitcast.51, bf16[2,256,576]{2,1,0:T(8,128)(2,1)} %bitcast.69, ...), custom_call_target="tpu_custom_call", output_to_operand_aliasing={{0}: (4, {})} | custom-call | flops 1 | bytes 1 | tf_op jit(solution)/shard_map/pallas_call | solution.py:203
  101.7 1.7 collective-permute-done.12.refs_1_
  103.3 13.5 %collective-permute-done.13.refs_2_ = bf16[144,2304]{1,0:T(8,128)(2,1)S(1)} collective-permute-done((bf16[144,2304]{1,0:T(8,128)(2,1)S(1)}, bf16[144,2304]{1,0:T(8,128)(2,1)S(1)}, u32[]{:S(2)}, u32[]{:S(2)}) %collective-permute-start.13) | collective-permute-done | bytes 663584 | tf_op jit(solution)/shard_map/ppermute | solution.py:34
  118.9 1.4 shard_map.107.b0_ref
  121.4 1.4 shard_map.104.near_ref
  124.4 1.4 shard_map.108.b1_ref
  127.6 1.4 shard_map.109
  130.1 2.0 shard_map.112
  132.3 2.0 shard_map.110
  136.3 1.3 shard_map.114
  138.1 2.0 shard_map.113
  140.1 1.4 collective-permute-start.26
  141.5 2.0 shard_map.111
  143.5 2.7 %collective-permute-start.22 = (bf16[144,2304]{1,0:T(8,128)(2,1)S(1)}, bf16[144,2304]{1,0:T(8,128)(2,1)S(1)}, u32[]{:S(2)}, u32[]{:S(2)}) collective-permute-start(bf16[144,2304]{1,0:T(8,128)(2,1)S(1)} %get-tuple-element.153), channel_id=1, source_target_pairs={{0,12},{1,13},{2,14},{3,15},{4,0},{5,1},{6,2},{7,3},{8,4},{9,5},{1... | collective-permute-start | bytes 1990664 | tf_op jit(solution)/shard_map/ppermute | solution.py:34
  147.2 6.5 %shard_map.118.refs_9_ = f32[256,7168]{1,0:T(8,128)} custom-call(bf16[288,2304]{1,0:T(8,128)(2,1)} %bitcast.60, bf16[288,2304]{1,0:T(8,128)(2,1)} %copy-done.9, bf16[288,2304]{1,0:T(8,128)(2,1)} %copy-done.8, bf16[288,2304]{1,0:T(8,128)(2,1)} %copy-done.10, bf16[4,256,288]{2,1,0:T(8,128)(2,1)} %bitcast.68, ...), custom_call_target="tpu_custom_call", output_to_operand_aliasing={{}: (5, {})} | custom-call | flops 1 | bytes 1 | tf_op jit(solution)/shard_map/pallas_call | solution.py:203
  153.8 6.3 %shard_map.119 = f32[256,7168]{1,0:T(8,128)} custom-call(bf16[144,2304]{1,0:T(8,128)(2,1)} %copy-done.11, bf16[144,2304]{1,0:T(8,128)(2,1)} %copy-done.12, bf16[144,2304]{1,0:T(8,128)(2,1)} %copy-done.13, bf16[144,2304]{1,0:T(8,128)(2,1)} %copy-done.14, bf16[144,2304]{1,0:T(8,128)(2,1)} %copy-done.15, ...), custom_call_target="tpu_custom_call", output_to_operand_aliasing={{}: (9, {})} | custom-call | flops 1 | bytes 1 | tf_op jit(solution)/shard_map/pallas_call | solution.py:203
  160.0 4.2 %shard_map.117 = (bf16[288,1280]{1,0:T(8,128)(2,1)}, bf16[288,1280]{1,0:T(8,128)(2,1)}) custom-call(bf16[7168,256]{1,0:T(8,128)(2,1)} %bitcast.34, bf16[7168,256]{1,0:T(8,128)(2,1)} %bitcast.42, bf16[576,1280]{1,0:T(8,128)(2,1)} %copy-done.34, bf16[1152,256]{1,0:T(8,128)(2,1)} %copy-done.6, bf16[1152,256]{1,0:T(8,128)(2,1)} %copy-done.7), custom_call_target="tpu_custom_call" | custom-call | flops 1 | bytes 1 | tf_op jit(solution)/shard_map/pallas_call | solution.py:203
  165.3 3.5 %shard_map.115 = (bf16[144,1280]{1,0:T(8,128)(2,1)S(1)}, bf16[144,1280]{1,0:T(8,128)(2,1)S(1)}, bf16[144,1280]{1,0:T(8,128)(2,1)S(1)}, bf16[144,1280]{1,0:T(8,128)(2,1)S(1)}) custom-call(bf16[7168,256]{1,0:T(8,128)(2,1)} %bitcast.35, bf16[7168,256]{1,0:T(8,128)(2,1)} %bitcast.43, bf16[576,1280]{1,0:T(8,128)(2,1)} %copy-done.33, bf16[1152,256]{1,0:T(8,128)(2,1)} %copy-done.4, ...), custom_call_target="tpu_custom_call" | custom-call | flops 1 | bytes 1 | tf_op jit(solution)/shard_map/pallas_call | solution.py:203
  168.9 5.8 %collective-permute-done.22.refs_1_ = bf16[144,2304]{1,0:T(8,128)(2,1)S(1)} collective-permute-done((bf16[144,2304]{1,0:T(8,128)(2,1)S(1)}, bf16[144,2304]{1,0:T(8,128)(2,1)S(1)}, u32[]{:S(2)}, u32[]{:S(2)}) %collective-permute-start.22) | collective-permute-done | bytes 663584 | tf_op jit(solution)/shard_map/ppermute | solution.py:34
  174.7 3.7 %collective-permute-done.24.refs_3_ = bf16[144,2304]{1,0:T(8,128)(2,1)S(1)} collective-permute-done((bf16[144,2304]{1,0:T(8,128)(2,1)S(1)}, bf16[144,2304]{1,0:T(8,128)(2,1)S(1)}, u32[]{:S(2)}, u32[]{:S(2)}) %collective-permute-start.24) | collective-permute-done | bytes 663584 | tf_op jit(solution)/shard_map/ppermute | solution.py:34
  179.5 4.7 %shard_map.120 = (f32[128,2304]{1,0:T(8,128)}, bf16[128,2304]{1,0:T(8,128)(2,1)}) custom-call(bf16[144,2304]{1,0:T(8,128)(2,1)} %copy-done.22, bf16[144,2304]{1,0:T(8,128)(2,1)} %copy-done.40, bf16[144,2304]{1,0:T(8,128)(2,1)} %copy-done.41, bf16[144,2304]{1,0:T(8,128)(2,1)} %copy-done.42, bf16[4,128,144]{2,1,0:T(8,128)(2,1)} %get-tuple-element.177.refs_4_, ...), custom_call_target="tpu_custom_call" | custom-call | flops 1 | bytes 1 | tf_op jit(solution)/shard_map/pallas_call | solution.py:203
  187.3 2.7 %shard_map.121 = bf16[288,2304]{1,0:T(8,128)(2,1)} custom-call(bf16[288,2304]{1,0:T(8,128)(2,1)} %copy-done.19, bf16[288,2304]{1,0:T(8,128)(2,1)} %copy-done.35), custom_call_target="tpu_custom_call" | custom-call | flops 1 | bytes 1 | tf_op jit(solution)/shard_map/pallas_call | solution.py:203
  190.0 6.8 %collective-permute-done.30.refs_1_ = bf16[144,1280]{1,0:T(8,128)(2,1)S(1)} collective-permute-done((bf16[144,1280]{1,0:T(8,128)(2,1)S(1)}, bf16[144,1280]{1,0:T(8,128)(2,1)S(1)}, u32[]{:S(2)}, u32[]{:S(2)}) %collective-permute-start.30) | collective-permute-done | bytes 368672 | tf_op jit(solution)/shard_map/ppermute | solution.py:34
  196.8 2.2 collective-permute-done.31.refs_2_
  198.9 5.7 %collective-permute-done.32.refs_3_ = bf16[144,1280]{1,0:T(8,128)(2,1)S(1)} collective-permute-done((bf16[144,1280]{1,0:T(8,128)(2,1)S(1)}, bf16[144,1280]{1,0:T(8,128)(2,1)S(1)}, u32[]{:S(2)}, u32[]{:S(2)}) %collective-permute-start.32) | collective-permute-done | bytes 368672 | tf_op jit(solution)/shard_map/ppermute | solution.py:34
  204.6 4.9 %collective-permute-done.29.refs_1_ = bf16[128,2304]{1,0:T(8,128)(2,1)S(1)} collective-permute-done((bf16[128,2304]{1,0:T(8,128)(2,1)}, bf16[128,2304]{1,0:T(8,128)(2,1)S(1)}, u32[]{:S(2)}, u32[]{:S(2)}) %collective-permute-start.29) | collective-permute-done | bytes 589856 | tf_op jit(solution)/shard_map/ppermute | solution.py:34
  209.5 3.6 %all-to-all-start.3 = ((bf16[4,72,2304]{2,1,0:T(8,128)(2,1)}), bf16[4,72,2304]{2,1,0:T(8,128)(2,1)S(1)}, u32[]{:S(2)}, u32[]{:S(2)}) async-start(bf16[4,72,2304]{2,1,0:T(8,128)(2,1)} %bitcast.71), calls=%async_computation.3 | async-start | bytes 2654208 | tf_op jit(solution)/shard_map/all_to_all | solution.py:44
  213.1 3.3 %shard_map.125 = bf16[128,2304]{1,0:T(8,128)(2,1)} custom-call(f32[128,2304]{1,0:T(8,128)} %get-tuple-element.193.refs_0_, bf16[128,2304]{1,0:T(8,128)(2,1)} %copy-done.43, bf16[128,2304]{1,0:T(8,128)(2,1)} %copy-done.31, bf16[128,2304]{1,0:T(8,128)(2,1)} %collective-permute-done.9.refs_1_.refs_3_, s32[5]{0:T(128)S(1)} %stack.26.at_ref.refs_4_), custom_call_target="tpu_custom_call" | custom-call | flops 1 | bytes 1 | tf_op jit(solution)/shard_map/pallas_call | solution.py:203
  216.4 3.9 %collective-permute-start.35 = (bf16[128,2304]{1,0:T(8,128)(2,1)}, bf16[128,2304]{1,0:T(8,128)(2,1)S(1)}, u32[]{:S(2)}, u32[]{:S(2)}) collective-permute-start(bf16[128,2304]{1,0:T(8,128)(2,1)} %shard_map.125), channel_id=1, source_target_pairs={{0,114},{1,115},{2,112},{3,113},{4,118},{5,119},{6,116},{7,117},{8... | collective-permute-start | bytes 1769480 | tf_op jit(solution)/shard_map/ppermute | solution.py:26
  220.3 3.6 %shard_map.122 = (f32[128,1280]{1,0:T(8,128)}, bf16[128,1280]{1,0:T(8,128)(2,1)}) custom-call(bf16[144,1280]{1,0:T(8,128)(2,1)} %copy-done.27, bf16[144,1280]{1,0:T(8,128)(2,1)} %copy-done.44, bf16[144,1280]{1,0:T(8,128)(2,1)} %copy-done.45, bf16[144,1280]{1,0:T(8,128)(2,1)} %copy-done.46, bf16[4,128,144]{2,1,0:T(8,128)(2,1)} %get-tuple-element.177.refs_4_, ...), custom_call_target="tpu_custom_call" | custom-call | flops 1 | bytes 1 | tf_op jit(solution)/shard_map/pallas_call | solution.py:203
  224.4 2.2 shard_map.124
  226.6 6.1 %collective-permute-done.34.refs_1_ = bf16[128,1280]{1,0:T(8,128)(2,1)S(1)} collective-permute-done((bf16[128,1280]{1,0:T(8,128)(2,1)}, bf16[128,1280]{1,0:T(8,128)(2,1)S(1)}, u32[]{:S(2)}, u32[]{:S(2)}) %collective-permute-start.34) | collective-permute-done | bytes 327712 | tf_op jit(solution)/shard_map/ppermute | solution.py:34
  233.4 2.8 %shard_map.123 = bf16[128,1280]{1,0:T(8,128)(2,1)} custom-call(f32[128,1280]{1,0:T(8,128)} %get-tuple-element.189.refs_0_, bf16[128,1280]{1,0:T(8,128)(2,1)} %copy-done.47, bf16[128,1280]{1,0:T(8,128)(2,1)} %copy-done.37, bf16[128,1280]{1,0:T(8,128)(2,1)} %copy-done.38, s32[5]{0:T(128)S(1)} %stack.26.at_ref.refs_4_), custom_call_target="tpu_custom_call" | custom-call | flops 1 | bytes 1 | tf_op jit(solution)/shard_map/pallas_call | solution.py:203
  236.3 1.9 collective-permute-start.37
  238.2 4.5 %all-to-all-start.2 = ((bf16[4,72,1280]{2,1,0:T(8,128)(2,1)}), bf16[4,72,1280]{2,1,0:T(8,128)(2,1)S(1)}, u32[]{:S(2)}, u32[]{:S(2)}) async-start(bf16[4,72,1280]{2,1,0:T(8,128)(2,1)} %bitcast.22), calls=%async_computation.2 | async-start | bytes 1474560 | tf_op jit(solution)/shard_map/all_to_all | solution.py:44
  242.7 3.0 %shard_map.127 = bf16[128,2304]{1,0:T(8,128)(2,1)} custom-call(bf16[128,4608]{1,0:T(8,128)(2,1)} %collective-permute-done.8.refs_0_, bf16[288,2304]{1,0:T(8,128)(2,1)} %bitcast.72, bf16[128,288]{1,0:T(8,128)(2,1)} %get-tuple-element.196.refs_2_), custom_call_target="tpu_custom_call" | custom-call | flops 1 | bytes 1 | tf_op jit(solution)/shard_map/pallas_call | solution.py:203
  245.7 2.0 collective-permute-start.38
  247.6 4.7 %all-to-all-done.2 = bf16[4,72,1280]{2,1,0:T(8,128)(2,1)S(1)} async-done(((bf16[4,72,1280]{2,1,0:T(8,128)(2,1)}), bf16[4,72,1280]{2,1,0:T(8,128)(2,1)S(1)}, u32[]{:S(2)}, u32[]{:S(2)}) %all-to-all-start.2) | async-done | bytes 737312 | tf_op jit(solution)/shard_map/all_to_all | solution.py:44
  253.2 2.4 shard_map.126
  257.4 4.7 %collective-permute-done.38.refs_0_ = bf16[128,2304]{1,0:T(8,128)(2,1)S(1)} collective-permute-done((bf16[128,2304]{1,0:T(8,128)(2,1)}, bf16[128,2304]{1,0:T(8,128)(2,1)S(1)}, u32[]{:S(2)}, u32[]{:S(2)}) %collective-permute-start.38) | collective-permute-done | bytes 589856 | tf_op jit(solution)/shard_map/ppermute | solution.py:26
  263.0 2.6 collective-permute-done.36.refs_0_
  (171 shorter events, 37.5 us)
Async XLA Ops:
  1.8 14.8 %collective-permute-start = (bf16[128,1280]{1,0:T(8,128)(2,1)S(1)}, bf16[128,1280]{1,0:T(8,128)(2,1)S(1)}, u32[]{:S(2)}, u32[]{:S(2)}) collective-permute-start(bf16[128,1280]{1,0:T(8,128)(2,1)S(1)} %get-tuple-element.203), channel_id=1, source_target_pairs={{0,114},{1,115},{2,112},{3,113},{4,118},{5,119},{6,116},{7,117},{8... | collective-permute-start | bytes 983048 | tf_op jit(solution)/shard_map/ppermute | solution.py:26
  9.8 3.6 %collective-permute-start.1 = (f32[4,128]{1,0:T(4,128)S(1)}, f32[4,128]{1,0:T(4,128)S(1)}, u32[]{:S(2)}, u32[]{:S(2)}) collective-permute-start(f32[4,128]{1,0:T(4,128)S(1)} %maximum_bitcast_fusion), channel_id=1, source_target_pairs={{0,2},{1,3},{2,0},{3,1},{4,6},{5,7},{6,4},{7,5},{8,10},{9,11},{10,... | collective-permute-start | bytes 6152 | tf_op jit(solution)/shard_map/ppermute | solution.py:34
  9.8 14.1 %collective-permute-start.2 = (bf16[128,1280]{1,0:T(8,128)(2,1)S(1)}, bf16[128,1280]{1,0:T(8,128)(2,1)S(1)}, u32[]{:S(2)}, u32[]{:S(2)}) collective-permute-start(bf16[128,1280]{1,0:T(8,128)(2,1)S(1)} %get-tuple-element.202), channel_id=1, source_target_pairs={{0,114},{1,115},{2,112},{3,113},{4,118},{5,119},{6,116},{7,117},{8... | collective-permute-start | bytes 983048 | tf_op jit(solution)/shard_map/ppermute | solution.py:26
  19.6 20.1 %all-to-all-start = ((bf16[4,72,1280]{2,1,0:T(8,128)(2,1)}), bf16[4,72,1280]{2,1,0:T(8,128)(2,1)}, u32[]{:S(2)}, u32[]{:S(2)}) async-start(bf16[4,72,1280]{2,1,0:T(8,128)(2,1)} %bitcast.11), calls=%async_computation | async-start | bytes 1474560 | tf_op jit(solution)/shard_map/all_to_all | solution.py:44
  23.9 26.8 %copy-start.23 = (bf16[1,1152,256]{2,1,0:T(8,128)(2,1)S(1)}, bf16[1,1152,256]{2,1,0:T(8,128)(2,1)}, u32[]{:S(2)}) copy-start(bf16[1,1152,256]{2,1,0:T(8,128)(2,1)} %param.11) | copy-start | bytes 1769476
  23.9 26.8 %copy-start.24 = (bf16[1,1152,256]{2,1,0:T(8,128)(2,1)S(1)}, bf16[1,1152,256]{2,1,0:T(8,128)(2,1)}, u32[]{:S(2)}) copy-start(bf16[1,1152,256]{2,1,0:T(8,128)(2,1)} %param.12) | copy-start | bytes 1769476
  23.9 15.9 %copy-start.37 = (bf16[128,1280]{1,0:T(8,128)(2,1)}, bf16[128,1280]{1,0:T(8,128)(2,1)S(1)}, u32[]{:S(2)}) copy-start(bf16[128,1280]{1,0:T(8,128)(2,1)S(1)} %collective-permute-done.2.refs_0_.refs_2_) | copy-start | bytes 983044
  26.4 31.1 %collective-permute-start.8 = (bf16[128,4608]{1,0:T(8,128)(2,1)}, bf16[128,4608]{1,0:T(8,128)(2,1)}, u32[]{:S(2)}, u32[]{:S(2)}) collective-permute-start(bf16[128,4608]{1,0:T(8,128)(2,1)} %slice.41), channel_id=1, source_target_pairs={{0,114},{1,115},{2,112},{3,113},{4,118},{5,119},{6,116},{7,117},{8... | collective-permute-start | bytes 3538952 | tf_op jit(solution)/shard_map/ppermute | solution.py:26
  32.2 7.5 %collective-permute-start.3 = (bf16[128,1280]{1,0:T(8,128)(2,1)S(1)}, bf16[128,1280]{1,0:T(8,128)(2,1)S(1)}, u32[]{:S(2)}, u32[]{:S(2)}) collective-permute-start(bf16[128,1280]{1,0:T(8,128)(2,1)S(1)} %collective-permute-done.2.refs_0_.refs_2_), channel_id=1, source_target_pairs={{0,2},{1,3},{2,0},{3,1},{4,6},{5,7},{6,4},{7,5},{8,10},{9,11},{10,... | collective-permute-start | bytes 983048 | tf_op jit(solution)/shard_map/ppermute | solution.py:34
  39.7 21.8 %collective-permute-start.4 = (bf16[288,1280]{1,0:T(8,128)(2,1)}, bf16[288,1280]{1,0:T(8,128)(2,1)}, u32[]{:S(2)}, u32[]{:S(2)}) collective-permute-start(bf16[288,1280]{1,0:T(8,128)(2,1)} %bitcast.12.refs_0_), channel_id=1, source_target_pairs={{0,2},{1,3},{2,0},{3,1},{4,6},{5,7},{6,4},{7,5},{8,10},{9,11},{10,... | collective-permute-start | bytes 2211848 | tf_op jit(solution)/shard_map/ppermute | solution.py:34
  44.1 17.3 %collective-permute-start.5 = (bf16[144,1280]{1,0:T(8,128)(2,1)}, bf16[144,1280]{1,0:T(8,128)(2,1)}, u32[]{:S(2)}, u32[]{:S(2)}) collective-permute-start(bf16[144,1280]{1,0:T(8,128)(2,1)} %get-tuple-element.110), channel_id=1, source_target_pairs={{0,4},{1,5},{2,6},{3,7},{4,8},{5,9},{6,10},{7,11},{8,12},{9,13},{1... | collective-permute-start | bytes 1105928 | tf_op jit(solution)/shard_map/ppermute | solution.py:34
  46.5 15.0 %collective-permute-start.6 = (bf16[144,1280]{1,0:T(8,128)(2,1)}, bf16[144,1280]{1,0:T(8,128)(2,1)}, u32[]{:S(2)}, u32[]{:S(2)}) collective-permute-start(bf16[144,1280]{1,0:T(8,128)(2,1)} %get-tuple-element.111), channel_id=1, source_target_pairs={{0,8},{1,9},{2,10},{3,11},{4,12},{5,13},{6,14},{7,15},{8,0},{9,1},... | collective-permute-start | bytes 1105928 | tf_op jit(solution)/shard_map/ppermute | solution.py:34
  49.2 12.3 %collective-permute-start.7 = (bf16[144,1280]{1,0:T(8,128)(2,1)S(1)}, bf16[144,1280]{1,0:T(8,128)(2,1)}, u32[]{:S(2)}, u32[]{:S(2)}) collective-permute-start(bf16[144,1280]{1,0:T(8,128)(2,1)S(1)} %get-tuple-element.112), channel_id=1, source_target_pairs={{0,12},{1,13},{2,14},{3,15},{4,0},{5,1},{6,2},{7,3},{8,4},{9,5},{1... | collective-permute-start | bytes 1105928 | tf_op jit(solution)/shard_map/ppermute | solution.py:34
  61.4 8.3 %copy-start.31 = (bf16[128,2304]{1,0:T(8,128)(2,1)}, bf16[128,2304]{1,0:T(8,128)(2,1)S(1)}, u32[]{:S(2)}) copy-start(bf16[128,2304]{1,0:T(8,128)(2,1)S(1)} %slice.54.refs_0_.refs_2_) | copy-start | bytes 1769476
  61.5 19.1 %all-to-all-start.1 = ((bf16[4,72,2304]{2,1,0:T(8,128)(2,1)}), bf16[4,72,2304]{2,1,0:T(8,128)(2,1)S(1)}, u32[]{:S(2)}, u32[]{:S(2)}) async-start(bf16[4,72,2304]{2,1,0:T(8,128)(2,1)} %bitcast.19), calls=%async_computation.1 | async-start | bytes 2654208 | tf_op jit(solution)/shard_map/all_to_all | solution.py:44
  65.4 11.9 %collective-permute-start.9 = (bf16[128,2304]{1,0:T(8,128)(2,1)S(1)}, bf16[128,2304]{1,0:T(8,128)(2,1)}, u32[]{:S(2)}, u32[]{:S(2)}) collective-permute-start(bf16[128,2304]{1,0:T(8,128)(2,1)S(1)} %slice.54.refs_0_.refs_2_), channel_id=1, source_target_pairs={{0,2},{1,3},{2,0},{3,1},{4,6},{5,7},{6,4},{7,5},{8,10},{9,11},{10,... | collective-permute-start | bytes 1769480 | tf_op jit(solution)/shard_map/ppermute | solution.py:34
  80.5 40.8 %copy-start.3 = (bf16[4,72,2304]{2,1,0:T(8,128)(2,1)}, bf16[4,72,2304]{2,1,0:T(8,128)(2,1)S(1)}, u32[]{:S(2)}) copy-start(bf16[4,72,2304]{2,1,0:T(8,128)(2,1)S(1)} %all-to-all-done.1) | copy-start | bytes 3981316
  80.6 7.7 %collective-permute-start.15 = (bf16[1152,1280]{1,0:T(8,128)(2,1)}, bf16[1152,1280]{1,0:T(8,128)(2,1)S(1)}, u32[]{:S(2)}, u32[]{:S(2)}) collective-permute-start(bf16[1152,1280]{1,0:T(8,128)(2,1)} %shard_map.100.refs_0_.refs_2_), channel_id=1, source_target_pairs={{0,1},{1,0},{2,3},{3,2},{4,5},{5,4},{6,7},{7,6},{8,9},{9,8},{10,11... | collective-permute-start | bytes 8847368 | tf_op jit(solution)/shard_map/ppermute | solution.py:34
  80.6 36.9 %collective-permute-start.11 = (bf16[288,2304]{1,0:T(8,128)(2,1)S(1)}, bf16[288,2304]{1,0:T(8,128)(2,1)S(1)}, u32[]{:S(2)}, u32[]{:S(2)}) collective-permute-start(bf16[288,2304]{1,0:T(8,128)(2,1)S(1)} %bitcast.57), channel_id=1, source_target_pairs={{0,2},{1,3},{2,0},{3,1},{4,6},{5,7},{6,4},{7,5},{8,10},{9,11},{10,... | collective-permute-start | bytes 3981320 | tf_op jit(solution)/shard_map/ppermute | solution.py:34
  84.3 34.6 %copy-start.11 = (bf16[144,2304]{1,0:T(8,128)(2,1)}, bf16[144,2304]{1,0:T(8,128)(2,1)S(1)}, u32[]{:S(2)}) copy-start(bf16[144,2304]{1,0:T(8,128)(2,1)S(1)} %get-tuple-element.143.refs_0_) | copy-start | bytes 1990660
  84.3 19.0 %collective-permute-start.12 = (bf16[144,2304]{1,0:T(8,128)(2,1)S(1)}, bf16[144,2304]{1,0:T(8,128)(2,1)S(1)}, u32[]{:S(2)}, u32[]{:S(2)}) collective-permute-start(bf16[144,2304]{1,0:T(8,128)(2,1)S(1)} %get-tuple-element.129), channel_id=1, source_target_pairs={{0,4},{1,5},{2,6},{3,7},{4,8},{5,9},{6,10},{7,11},{8,12},{9,13},{1... | collective-permute-start | bytes 1990664 | tf_op jit(solution)/shard_map/ppermute | solution.py:34
  85.0 31.9 %collective-permute-start.13 = (bf16[144,2304]{1,0:T(8,128)(2,1)S(1)}, bf16[144,2304]{1,0:T(8,128)(2,1)S(1)}, u32[]{:S(2)}, u32[]{:S(2)}) collective-permute-start(bf16[144,2304]{1,0:T(8,128)(2,1)S(1)} %get-tuple-element.130), channel_id=1, source_target_pairs={{0,8},{1,9},{2,10},{3,11},{4,12},{5,13},{6,14},{7,15},{8,0},{9,1},... | collective-permute-start | bytes 1990664 | tf_op jit(solution)/shard_map/ppermute | solution.py:34
  87.6 29.8 %collective-permute-start.14 = (bf16[144,2304]{1,0:T(8,128)(2,1)S(1)}, bf16[144,2304]{1,0:T(8,128)(2,1)S(1)}, u32[]{:S(2)}, u32[]{:S(2)}) collective-permute-start(bf16[144,2304]{1,0:T(8,128)(2,1)S(1)} %get-tuple-element.131), channel_id=1, source_target_pairs={{0,12},{1,13},{2,14},{3,15},{4,0},{5,1},{6,2},{7,3},{8,4},{9,5},{1... | collective-permute-start | bytes 1990664 | tf_op jit(solution)/shard_map/ppermute | solution.py:34
  88.2 30.4 %collective-permute-start.10 = (bf16[288,2304]{1,0:T(8,128)(2,1)S(1)}, bf16[288,2304]{1,0:T(8,128)(2,1)S(1)}, u32[]{:S(2)}, u32[]{:S(2)}) collective-permute-start(bf16[288,2304]{1,0:T(8,128)(2,1)S(1)} %bitcast.58), channel_id=1, source_target_pairs={{0,1},{1,0},{2,3},{3,2},{4,5},{5,4},{6,7},{7,6},{8,9},{9,8},{10,11... | collective-permute-start | bytes 3981320 | tf_op jit(solution)/shard_map/ppermute | solution.py:34
  101.5 17.4 %copy-start.2 = (bf16[1,256,7168]{2,1,0:T(8,128)(2,1)S(1)}, bf16[1,256,7168]{2,1,0:T(8,128)(2,1)}, u32[]{:S(2)}) copy-start(bf16[1,256,7168]{2,1,0:T(8,128)(2,1)} %param.15) | copy-start | bytes 11010052
  103.3 16.9 %copy-start.12 = (bf16[144,2304]{1,0:T(8,128)(2,1)}, bf16[144,2304]{1,0:T(8,128)(2,1)S(1)}, u32[]{:S(2)}) copy-start(bf16[144,2304]{1,0:T(8,128)(2,1)S(1)} %collective-permute-done.12.refs_1_) | copy-start | bytes 1990660
  117.5 8.4 %collective-permute-start.16 = (bf16[288,2304]{1,0:T(8,128)(2,1)S(1)}, bf16[288,2304]{1,0:T(8,128)(2,1)S(1)}, u32[]{:S(2)}, u32[]{:S(2)}) collective-permute-start(bf16[288,2304]{1,0:T(8,128)(2,1)S(1)} %collective-permute-done.11.refs_0_.refs_1_), channel_id=1, source_target_pairs={{0,1},{1,0},{2,3},{3,2},{4,5},{5,4},{6,7},{7,6},{8,9},{9,8},{10,11... | collective-permute-start | bytes 3981320 | tf_op jit(solution)/shard_map/ppermute | solution.py:34
  117.6 5.2 %collective-permute-start.17 = (bf16[144,2304]{1,0:T(8,128)(2,1)S(1)}, bf16[144,2304]{1,0:T(8,128)(2,1)S(1)}, u32[]{:S(2)}, u32[]{:S(2)}) collective-permute-start(bf16[144,2304]{1,0:T(8,128)(2,1)S(1)} %get-tuple-element.143.refs_0_), channel_id=1, source_target_pairs={{0,1},{1,0},{2,3},{3,2},{4,5},{5,4},{6,7},{7,6},{8,9},{9,8},{10,11... | collective-permute-start | bytes 1990664 | tf_op jit(solution)/shard_map/ppermute | solution.py:34
  118.1 4.8 %collective-permute-start.18 = (bf16[144,2304]{1,0:T(8,128)(2,1)S(1)}, bf16[144,2304]{1,0:T(8,128)(2,1)S(1)}, u32[]{:S(2)}, u32[]{:S(2)}) collective-permute-start(bf16[144,2304]{1,0:T(8,128)(2,1)S(1)} %collective-permute-done.12.refs_1_), channel_id=1, source_target_pairs={{0,1},{1,0},{2,3},{3,2},{4,5},{5,4},{6,7},{7,6},{8,9},{9,8},{10,11... | collective-permute-start | bytes 1990664 | tf_op jit(solution)/shard_map/ppermute | solution.py:34
  118.4 5.1 %collective-permute-start.19 = (bf16[144,2304]{1,0:T(8,128)(2,1)S(1)}, bf16[144,2304]{1,0:T(8,128)(2,1)S(1)}, u32[]{:S(2)}, u32[]{:S(2)}) collective-permute-start(bf16[144,2304]{1,0:T(8,128)(2,1)S(1)} %collective-permute-done.13.refs_2_), channel_id=1, source_target_pairs={{0,1},{1,0},{2,3},{3,2},{4,5},{5,4},{6,7},{7,6},{8,9},{9,8},{10,11... | collective-permute-start | bytes 1990664 | tf_op jit(solution)/shard_map/ppermute | solution.py:34
  118.6 5.8 %collective-permute-start.20 = (bf16[144,2304]{1,0:T(8,128)(2,1)S(1)}, bf16[144,2304]{1,0:T(8,128)(2,1)S(1)}, u32[]{:S(2)}, u32[]{:S(2)}) collective-permute-start(bf16[144,2304]{1,0:T(8,128)(2,1)S(1)} %collective-permute-done.14.refs_3_), channel_id=1, source_target_pairs={{0,1},{1,0},{2,3},{3,2},{4,5},{5,4},{6,7},{7,6},{8,9},{9,8},{10,11... | collective-permute-start | bytes 1990664 | tf_op jit(solution)/shard_map/ppermute | solution.py:34
  129.1 9.0 %copy-start.6 = (bf16[1152,256]{1,0:T(8,128)(2,1)}, bf16[1152,256]{1,0:T(8,128)(2,1)S(1)}, u32[]{:S(2)}) copy-start(bf16[1152,256]{1,0:T(8,128)(2,1)S(1)} %get-tuple-element.166.refs_2_.refs_3_) | copy-start | bytes 1769476
  129.1 9.0 %copy-start.7 = (bf16[1152,256]{1,0:T(8,128)(2,1)}, bf16[1152,256]{1,0:T(8,128)(2,1)S(1)}, u32[]{:S(2)}) copy-start(bf16[1152,256]{1,0:T(8,128)(2,1)S(1)} %get-tuple-element.167.refs_3_.refs_4_) | copy-start | bytes 1769476
  129.1 12.4 %copy-start.4 = (bf16[1152,256]{1,0:T(8,128)(2,1)}, bf16[1152,256]{1,0:T(8,128)(2,1)S(1)}, u32[]{:S(2)}) copy-start(bf16[1152,256]{1,0:T(8,128)(2,1)S(1)} %get-tuple-element.160.refs_2_.refs_3_) | copy-start | bytes 1769476
  129.1 12.4 %copy-start.5 = (bf16[1152,256]{1,0:T(8,128)(2,1)}, bf16[1152,256]{1,0:T(8,128)(2,1)S(1)}, u32[]{:S(2)}) copy-start(bf16[1152,256]{1,0:T(8,128)(2,1)S(1)} %get-tuple-element.161.refs_3_.refs_4_) | copy-start | bytes 1769476
  132.1 6.0 %collective-permute-start.25 = (bf16[576,2304]{1,0:T(8,128)(2,1)S(1)}, bf16[576,2304]{1,0:T(8,128)(2,1)S(1)}, u32[]{:S(2)}, u32[]{:S(2)}) collective-permute-start(bf16[576,2304]{1,0:T(8,128)(2,1)S(1)} %shard_map.112), channel_id=1, source_target_pairs={{0,1},{1,0},{2,3},{3,2},{4,5},{5,4},{6,7},{7,6},{8,9},{9,8},{10,11... | collective-permute-start | bytes 7962632 | tf_op jit(solution)/shard_map/ppermute | solution.py:34
  134.3 7.1 %collective-permute-start.21 = (bf16[576,2304]{1,0:T(8,128)(2,1)S(1)}, bf16[576,2304]{1,0:T(8,128)(2,1)S(1)}, u32[]{:S(2)}, u32[]{:S(2)}) collective-permute-start(bf16[576,2304]{1,0:T(8,128)(2,1)S(1)} %shard_map.110), channel_id=1, source_target_pairs={{0,1},{1,0},{2,3},{3,2},{4,5},{5,4},{6,7},{7,6},{8,9},{9,8},{10,11... | collective-permute-start | bytes 7962632 | tf_op jit(solution)/shard_map/ppermute | solution.py:34
  136.1 10.1 %collective-permute-start.28 = (bf16[576,1280]{1,0:T(8,128)(2,1)S(1)}, bf16[576,1280]{1,0:T(8,128)(2,1)S(1)}, u32[]{:S(2)}, u32[]{:S(2)}) collective-permute-start(bf16[576,1280]{1,0:T(8,128)(2,1)S(1)} %shard_map.116), channel_id=1, source_target_pairs={{0,1},{1,0},{2,3},{3,2},{4,5},{5,4},{6,7},{7,6},{8,9},{9,8},{10,11... | collective-permute-start | bytes 4423688 | tf_op jit(solution)/shard_map/ppermute | solution.py:34
  137.6 26.6 %collective-permute-start.27 = (bf16[576,1280]{1,0:T(8,128)(2,1)S(1)}, bf16[576,1280]{1,0:T(8,128)(2,1)S(1)}, u32[]{:S(2)}, u32[]{:S(2)}) collective-permute-start(bf16[576,1280]{1,0:T(8,128)(2,1)S(1)} %shard_map.114), channel_id=1, source_target_pairs={{0,1},{1,0},{2,3},{3,2},{4,5},{5,4},{6,7},{7,6},{8,9},{9,8},{10,11... | collective-permute-start | bytes 4423688 | tf_op jit(solution)/shard_map/ppermute | solution.py:34
  140.1 38.2 %collective-permute-start.26 = (bf16[288,2304]{1,0:T(8,128)(2,1)S(1)}, bf16[288,2304]{1,0:T(8,128)(2,1)S(1)}, u32[]{:S(2)}, u32[]{:S(2)}) collective-permute-start(bf16[288,2304]{1,0:T(8,128)(2,1)S(1)} %get-tuple-element.158), channel_id=1, source_target_pairs={{0,2},{1,3},{2,0},{3,1},{4,6},{5,7},{6,4},{7,5},{8,10},{9,11},{10,... | collective-permute-start | bytes 3981320 | tf_op jit(solution)/shard_map/ppermute | solution.py:34
  143.5 10.2 %copy-start.22 = (bf16[144,2304]{1,0:T(8,128)(2,1)}, bf16[144,2304]{1,0:T(8,128)(2,1)S(1)}, u32[]{:S(2)}) copy-start(bf16[144,2304]{1,0:T(8,128)(2,1)S(1)} %get-tuple-element.159.refs_0_) | copy-start | bytes 1990660
  143.5 31.1 %collective-permute-start.22 = (bf16[144,2304]{1,0:T(8,128)(2,1)S(1)}, bf16[144,2304]{1,0:T(8,128)(2,1)S(1)}, u32[]{:S(2)}, u32[]{:S(2)}) collective-permute-start(bf16[144,2304]{1,0:T(8,128)(2,1)S(1)} %get-tuple-element.153), channel_id=1, source_target_pairs={{0,12},{1,13},{2,14},{3,15},{4,0},{5,1},{6,2},{7,3},{8,4},{9,5},{1... | collective-permute-start | bytes 1990664 | tf_op jit(solution)/shard_map/ppermute | solution.py:34
  146.2 28.4 %collective-permute-start.23 = (bf16[144,2304]{1,0:T(8,128)(2,1)S(1)}, bf16[144,2304]{1,0:T(8,128)(2,1)S(1)}, u32[]{:S(2)}, u32[]{:S(2)}) collective-permute-start(bf16[144,2304]{1,0:T(8,128)(2,1)S(1)} %get-tuple-element.154), channel_id=1, source_target_pairs={{0,8},{1,9},{2,10},{3,11},{4,12},{5,13},{6,14},{7,15},{8,0},{9,1},... | collective-permute-start | bytes 1990664 | tf_op jit(solution)/shard_map/ppermute | solution.py:34
  146.2 7.5 %copy-start.34 = (bf16[576,1280]{1,0:T(8,128)(2,1)}, bf16[576,1280]{1,0:T(8,128)(2,1)S(1)}, u32[]{:S(2)}) copy-start(bf16[576,1280]{1,0:T(8,128)(2,1)S(1)} %collective-permute-done.28.refs_2_) | copy-start | bytes 4423684
  146.2 32.1 %collective-permute-start.24 = (bf16[144,2304]{1,0:T(8,128)(2,1)S(1)}, bf16[144,2304]{1,0:T(8,128)(2,1)S(1)}, u32[]{:S(2)}, u32[]{:S(2)}) collective-permute-start(bf16[144,2304]{1,0:T(8,128)(2,1)S(1)} %get-tuple-element.155), channel_id=1, source_target_pairs={{0,4},{1,5},{2,6},{3,7},{4,8},{5,9},{6,10},{7,11},{8,12},{9,13},{1... | collective-permute-start | bytes 1990664 | tf_op jit(solution)/shard_map/ppermute | solution.py:34
  164.2 14.1 %copy-start.48 = (bf16[288,1280]{1,0:T(8,128)(2,1)S(1)}, bf16[288,1280]{1,0:T(8,128)(2,1)}, u32[]{:S(2)}) copy-start(bf16[288,1280]{1,0:T(8,128)(2,1)} %get-tuple-element.183) | copy-start | bytes 2211844
  168.8 15.3 %copy-start.27 = (bf16[144,1280]{1,0:T(8,128)(2,1)}, bf16[144,1280]{1,0:T(8,128)(2,1)S(1)}, u32[]{:S(2)}) copy-start(bf16[144,1280]{1,0:T(8,128)(2,1)S(1)} %get-tuple-element.173.refs_0_) | copy-start | bytes 1105924
  178.3 5.8 %copy-start.35 = (bf16[288,2304]{1,0:T(8,128)(2,1)}, bf16[288,2304]{1,0:T(8,128)(2,1)S(1)}, u32[]{:S(2)}) copy-start(bf16[288,2304]{1,0:T(8,128)(2,1)S(1)} %collective-permute-done.26.refs_1_) | copy-start | bytes 3981316
  178.4 31.1 %collective-permute-start.33 = (bf16[288,1280]{1,0:T(8,128)(2,1)S(1)}, bf16[288,1280]{1,0:T(8,128)(2,1)S(1)}, u32[]{:S(2)}, u32[]{:S(2)}) collective-permute-start(bf16[288,1280]{1,0:T(8,128)(2,1)S(1)} %copy-done.48), channel_id=1, source_target_pairs={{0,2},{1,3},{2,0},{3,1},{4,6},{5,7},{6,4},{7,5},{8,10},{9,11},{10,... | collective-permute-start | bytes 2211848 | tf_op jit(solution)/shard_map/ppermute | solution.py:34
  184.1 25.3 %collective-permute-start.29 = (bf16[128,2304]{1,0:T(8,128)(2,1)}, bf16[128,2304]{1,0:T(8,128)(2,1)S(1)}, u32[]{:S(2)}, u32[]{:S(2)}) collective-permute-start(bf16[128,2304]{1,0:T(8,128)(2,1)} %get-tuple-element.179), channel_id=1, source_target_pairs={{0,2},{1,3},{2,0},{3,1},{4,6},{5,7},{6,4},{7,5},{8,10},{9,11},{10,... | collective-permute-start | bytes 1769480 | tf_op jit(solution)/shard_map/ppermute | solution.py:34
  185.2 11.5 %collective-permute-start.30 = (bf16[144,1280]{1,0:T(8,128)(2,1)S(1)}, bf16[144,1280]{1,0:T(8,128)(2,1)S(1)}, u32[]{:S(2)}, u32[]{:S(2)}) collective-permute-start(bf16[144,1280]{1,0:T(8,128)(2,1)S(1)} %get-tuple-element.180), channel_id=1, source_target_pairs={{0,12},{1,13},{2,14},{3,15},{4,0},{5,1},{6,2},{7,3},{8,4},{9,5},{1... | collective-permute-start | bytes 1105928 | tf_op jit(solution)/shard_map/ppermute | solution.py:34
  185.8 13.1 %collective-permute-start.31 = (bf16[144,1280]{1,0:T(8,128)(2,1)S(1)}, bf16[144,1280]{1,0:T(8,128)(2,1)S(1)}, u32[]{:S(2)}, u32[]{:S(2)}) collective-permute-start(bf16[144,1280]{1,0:T(8,128)(2,1)S(1)} %get-tuple-element.181), channel_id=1, source_target_pairs={{0,8},{1,9},{2,10},{3,11},{4,12},{5,13},{6,14},{7,15},{8,0},{9,1},... | collective-permute-start | bytes 1105928 | tf_op jit(solution)/shard_map/ppermute | solution.py:34
  186.1 18.5 %collective-permute-start.32 = (bf16[144,1280]{1,0:T(8,128)(2,1)S(1)}, bf16[144,1280]{1,0:T(8,128)(2,1)S(1)}, u32[]{:S(2)}, u32[]{:S(2)}) collective-permute-start(bf16[144,1280]{1,0:T(8,128)(2,1)S(1)} %get-tuple-element.182), channel_id=1, source_target_pairs={{0,4},{1,5},{2,6},{3,7},{4,8},{5,9},{6,10},{7,11},{8,12},{9,13},{1... | collective-permute-start | bytes 1105928 | tf_op jit(solution)/shard_map/ppermute | solution.py:34
  196.8 19.6 %copy-start.44 = (bf16[144,1280]{1,0:T(8,128)(2,1)}, bf16[144,1280]{1,0:T(8,128)(2,1)S(1)}, u32[]{:S(2)}) copy-start(bf16[144,1280]{1,0:T(8,128)(2,1)S(1)} %collective-permute-done.30.refs_1_) | copy-start | bytes 1105924
  198.9 17.5 %copy-start.45 = (bf16[144,1280]{1,0:T(8,128)(2,1)}, bf16[144,1280]{1,0:T(8,128)(2,1)S(1)}, u32[]{:S(2)}) copy-start(bf16[144,1280]{1,0:T(8,128)(2,1)S(1)} %collective-permute-done.31.refs_2_) | copy-start | bytes 1105924
  204.6 4.9 %copy-start.46 = (bf16[144,1280]{1,0:T(8,128)(2,1)}, bf16[144,1280]{1,0:T(8,128)(2,1)S(1)}, u32[]{:S(2)}) copy-start(bf16[144,1280]{1,0:T(8,128)(2,1)S(1)} %collective-permute-done.32.refs_3_) | copy-start | bytes 1105924
  209.5 6.9 %copy-start.39 = (bf16[288,1280]{1,0:T(8,128)(2,1)}, bf16[288,1280]{1,0:T(8,128)(2,1)S(1)}, u32[]{:S(2)}) copy-start(bf16[288,1280]{1,0:T(8,128)(2,1)S(1)} %collective-permute-done.33.refs_1_) | copy-start | bytes 2211844
  209.5 28.7 %all-to-all-start.3 = ((bf16[4,72,2304]{2,1,0:T(8,128)(2,1)}), bf16[4,72,2304]{2,1,0:T(8,128)(2,1)S(1)}, u32[]{:S(2)}, u32[]{:S(2)}) async-start(bf16[4,72,2304]{2,1,0:T(8,128)(2,1)} %bitcast.71), calls=%async_computation.3 | async-start | bytes 2654208 | tf_op jit(solution)/shard_map/all_to_all | solution.py:44
  216.4 19.9 %collective-permute-start.35 = (bf16[128,2304]{1,0:T(8,128)(2,1)}, bf16[128,2304]{1,0:T(8,128)(2,1)S(1)}, u32[]{:S(2)}, u32[]{:S(2)}) collective-permute-start(bf16[128,2304]{1,0:T(8,128)(2,1)} %shard_map.125), channel_id=1, source_target_pairs={{0,114},{1,115},{2,112},{3,113},{4,118},{5,119},{6,116},{7,117},{8... | collective-permute-start | bytes 1769480 | tf_op jit(solution)/shard_map/ppermute | solution.py:26
  223.9 8.8 %collective-permute-start.34 = (bf16[128,1280]{1,0:T(8,128)(2,1)}, bf16[128,1280]{1,0:T(8,128)(2,1)S(1)}, u32[]{:S(2)}, u32[]{:S(2)}) collective-permute-start(bf16[128,1280]{1,0:T(8,128)(2,1)} %get-tuple-element.190), channel_id=1, source_target_pairs={{0,2},{1,3},{2,0},{3,1},{4,6},{5,7},{6,4},{7,5},{8,10},{9,11},{10,... | collective-permute-start | bytes 983048 | tf_op jit(solution)/shard_map/ppermute | solution.py:34
  236.3 9.4 %collective-permute-start.37 = (bf16[128,1280]{1,0:T(8,128)(2,1)}, bf16[128,1280]{1,0:T(8,128)(2,1)S(1)}, u32[]{:S(2)}, u32[]{:S(2)}) collective-permute-start(bf16[128,1280]{1,0:T(8,128)(2,1)} %shard_map.123), channel_id=1, source_target_pairs={{0,114},{1,115},{2,112},{3,113},{4,118},{5,119},{6,116},{7,117},{8... | collective-permute-start | bytes 983048 | tf_op jit(solution)/shard_map/ppermute | solution.py:26
  238.2 14.1 %all-to-all-start.2 = ((bf16[4,72,1280]{2,1,0:T(8,128)(2,1)}), bf16[4,72,1280]{2,1,0:T(8,128)(2,1)S(1)}, u32[]{:S(2)}, u32[]{:S(2)}) async-start(bf16[4,72,1280]{2,1,0:T(8,128)(2,1)} %bitcast.22), calls=%async_computation.2 | async-start | bytes 1474560 | tf_op jit(solution)/shard_map/all_to_all | solution.py:44
  245.7 16.4 %collective-permute-start.38 = (bf16[128,2304]{1,0:T(8,128)(2,1)}, bf16[128,2304]{1,0:T(8,128)(2,1)S(1)}, u32[]{:S(2)}, u32[]{:S(2)}) collective-permute-start(bf16[128,2304]{1,0:T(8,128)(2,1)} %shard_map.127), channel_id=1, source_target_pairs={{0,112},{1,113},{2,114},{3,115},{4,116},{5,117},{6,118},{7,119},{8... | collective-permute-start | bytes 1769480 | tf_op jit(solution)/shard_map/ppermute | solution.py:26
  255.5 10.1 %collective-permute-start.36 = (bf16[128,1280]{1,0:T(8,128)(2,1)}, bf16[128,1280]{1,0:T(8,128)(2,1)S(1)}, u32[]{:S(2)}, u32[]{:S(2)}) collective-permute-start(bf16[128,1280]{1,0:T(8,128)(2,1)} %shard_map.126), channel_id=1, source_target_pairs={{0,112},{1,113},{2,114},{3,115},{4,116},{5,117},{6,118},{7,119},{8... | collective-permute-start | bytes 983048 | tf_op jit(solution)/shard_map/ppermute | solution.py:26
  (28 other events, 63.0 us)

commit v2 on v1

--- a/solution.py
+++ b/solution.py
@@ -660,25 +660,25 @@
         (back_b1, back_a1, part_b0, keep_a0, send_a0, grad)
     )
     back_b0 = x_moves(part_b0, -1)
-    back_a0 = ep_move(send_a0, dz=1)
     keep_b1, send_b1 = combine_b(keep_t, send_t, [part_b1[0]] + back_b1)
     cross_b1 = ep_move(send_b1, dz=1)
-    sum_a1 = sum_z(keep_a1, back_a1)
-    cross_b1, back_b0, back_a0, sum_a1 = tie((cross_b1, back_b0, back_a0, sum_a1))
-    own_a1 = x_exchange(sum_a1)
-    up_b1 = section_move(finish_b(at, keep_b1, cross_b1, tok_b1, 0, far_tok1), crossing)
+    back_a0 = ep_move(release(send_a0, cross_b1), dz=1)
+    done_b1 = finish_b(at, keep_b1, cross_b1, tok_b1, 0, far_tok1)
+    up_b1 = section_move(done_b1, crossing)
+    own_a1 = x_exchange(release(sum_z(keep_a1, back_a1), back_b0, done_b1))
+    sum_a0 = sum_z(keep_a0, back_a0)
     keep_b0, send_b0 = combine_b(keep_t, send_t, [part_b0[0]] + back_b0)
     cross_b0 = ep_move(send_b0, dz=1)
-    sum_a0 = sum_z(keep_a0, back_a0)
+    done_a1 = finish_a(place_t, tok1, 0, release(own_a1, send_b0))
+    up_a1 = section_move(release(done_a1, up_b1), swapped)
+    cross_b0 = release(cross_b0, done_a1, sum_a0)
     done_b0 = finish_b(at, keep_b0, cross_b0, tok_b0, 0, far_tok0)
-    done_b0, sum_a0, up_b1 = tie((done_b0, sum_a0, up_b1))
-    up_b0 = section_move(done_b0, crossing)
-    up_a1 = section_move(release(finish_a(place_t, tok1, 0, own_a1), up_b0), swapped)
-    own_a0 = x_exchange(sum_a0)
+    up_b0 = section_move(release(done_b0, up_a1), crossing)
+    own_a0 = x_exchange(release(sum_a0, cross_b0))
     up_a0 = section_move(finish_a(place_t, tok_a0, 0, own_a0), swapped)
     out = place_chunk(up_b1, width, at_b1, None)
+    out = place_chunk(up_a1, width, at_a1, out)
     out = place_chunk(up_b0, width, at_b0, out)
-    out = place_chunk(up_a1, width, at_a1, out)
     out = place_chunk(up_a0, width, at_a0, out)
     return (out[None], grad[None])
 

time: 268 us -> 277 us (1.034)
  starting transfers between devices: 62.4 us -> 80.6 us
  waiting for transfers between devices: 85.6 us -> 73.4 us
  local copies, waits for them, and re-layouts: 17.7 us -> 21.2 us
    ppermute x7, starting transfers between devices: 21.4 us -> 40.6 us  [section_move(): return lax.ppermute(array, ('section', 'ep'), pairs)]
    ppermute x32, waiting for transfers between devices: 70 us -> 55.3 us  [ep_move(): return lax.ppermute(array, 'ep', pairs)]
    all_to_all x4, waiting for transfers between devices: 7.85 us -> 12.7 us  [x_exchange(): lax.all_to_all(blocks, 'ep', 0, 0, axis_index_groups=groups, tiled=True)]
    unnamed x98 -> x96, local copies, waits for them, and re-layouts: 10.1 us -> 13.6 us
  transfers between devices with their start and end apart: 43 -> 43, of which waited for: 21 -> 18; matrix products, arithmetic and copies ran while one was open for 4% -> 3% of each run, Pallas kernels for 34% -> 31%
where the time goes in v2:
time: 277 us; the launch traced here: 276 us
  Pallas kernels  96.1 us (35%)
  starting transfers between devices  80.6 us (29%)
  waiting for transfers between devices  73.4 us (26%)
  local copies, waits for them, and re-layouts  21.2 us (8%)
  other arithmetic  3.13 us (1%)
    pallas_call x23, Pallas kernels, over_columns(): pl.pallas_call(kernel, in_specs=specs, out_specs=[hbm] * n_out + [pl.Bloc...  74.4 us
    ppermute x32, waiting for transfers between devices, ep_move(): return lax.ppermute(array, 'ep', pairs)  55.3 us
    ppermute x7, starting transfers between devices, section_move(): return lax.ppermute(array, ('section', 'ep'), pairs)  40.6 us
    ppermute x32, starting transfers between devices, ep_move(): return lax.ppermute(array, 'ep', pairs)  24.7 us
    pallas_call x11, Pallas kernels, at_once(): pl.pallas_call(kernel, in_specs=specs, out_specs=[whole(shape) for shape,...  16.9 us
    all_to_all x4, starting transfers between devices, x_exchange(): lax.all_to_all(blocks, 'ep', 0, 0, axis_index_groups=groups, tiled=True)  15.3 us
    unnamed x96, local copies, waits for them, and re-layouts  13.6 us
    all_to_all x4, waiting for transfers between devices, x_exchange(): lax.all_to_all(blocks, 'ep', 0, 0, axis_index_groups=groups, tiled=True)  12.7 us
  transfers between devices with their start and end apart: 43, of which 18 were waited for; matrix products, arithmetic and copies ran while one was open for 3% of the time, Pallas kernels for 31%

profile of v2, /device:TPU:0, one launch (start us, length us, event | category | flops | bytes accessed | tf_op | source)
XLA Modules:
  0.0 276.0 jit_solution(12158794769247596688)
XLA Ops:
  1.8 6.6 %collective-permute-start = (bf16[128,1280]{1,0:T(8,128)(2,1)S(1)}, bf16[128,1280]{1,0:T(8,128)(2,1)S(1)}, u32[]{:S(2)}, u32[]{:S(2)}) collective-permute-start(bf16[128,1280]{1,0:T(8,128)(2,1)S(1)} %get-tuple-element.197), channel_id=1, source_target_pairs={{0,114},{1,115},{2,112},{3,113},{4,118},{5,119},{6,116},{7,117},{8... | collective-permute-start | bytes 983048 | tf_op jit(solution)/shard_map/ppermute | solution.py:26
  9.8 1.1 collective-permute-start.2
  11.0 2.4 collective-permute-done.1
  14.0 2.0 shard_map.95
  17.2 2.3 shard_map.96
  19.6 4.3 %all-to-all-start = ((bf16[4,72,1280]{2,1,0:T(8,128)(2,1)}), bf16[4,72,1280]{2,1,0:T(8,128)(2,1)}, u32[]{:S(2)}, u32[]{:S(2)}) async-start(bf16[4,72,1280]{2,1,0:T(8,128)(2,1)} %bitcast.11), calls=%async_computation | async-start | bytes 1474560 | tf_op jit(solution)/shard_map/all_to_all | solution.py:44
  23.9 2.5 slice.41
  26.4 5.8 %collective-permute-start.8 = (bf16[128,4608]{1,0:T(8,128)(2,1)}, bf16[128,4608]{1,0:T(8,128)(2,1)}, u32[]{:S(2)}, u32[]{:S(2)}) collective-permute-start(bf16[128,4608]{1,0:T(8,128)(2,1)} %slice.41), channel_id=1, source_target_pairs={{0,114},{1,115},{2,112},{3,113},{4,118},{5,119},{6,116},{7,117},{8... | collective-permute-start | bytes 3538952 | tf_op jit(solution)/shard_map/ppermute | solution.py:26
  32.2 7.5 %collective-permute-done.3.refs_1_.refs_3_ = bf16[128,1280]{1,0:T(8,128)(2,1)S(1)} collective-permute-done((bf16[128,1280]{1,0:T(8,128)(2,1)S(1)}, bf16[128,1280]{1,0:T(8,128)(2,1)S(1)}, u32[]{:S(2)}, u32[]{:S(2)}) %collective-permute-start.3) | collective-permute-done | bytes 327712 | tf_op jit(solution)/shard_map/ppermute | solution.py:34
  40.4 2.9 %shard_map.97 = (bf16[144,1280]{1,0:T(8,128)(2,1)S(1)}, bf16[144,1280]{1,0:T(8,128)(2,1)}, bf16[144,1280]{1,0:T(8,128)(2,1)}, bf16[144,1280]{1,0:T(8,128)(2,1)S(1)}) custom-call(bf16[128,1280]{1,0:T(8,128)(2,1)} %copy-done.37, bf16[128,1280]{1,0:T(8,128)(2,1)} %copy-done.38, bf16[288,128]{1,0:T(8,128)(2,1)} %get-tuple-element.103.refs_2_, ...), custom_call_target="tpu_custom_call" | custom-call | flops 1 | bytes 1 | tf_op jit(solution)/shard_map/pallas_call | solution.py:203
  44.1 2.4 collective-permute-start.5
  46.5 2.7 collective-permute-start.6
  49.2 1.5 collective-permute-start.7
  50.6 1.3 shard_map.99
  53.8 1.4 copy.16
  57.5 2.8 %shard_map.98 = bf16[288,2304]{1,0:T(8,128)(2,1)} custom-call(bf16[128,4608]{1,0:T(8,128)(2,1)} %collective-permute-done.8.refs_0_, bf16[288,128]{1,0:T(8,128)(2,1)} %get-tuple-element.99.refs_1_, f32[288,128]{1,0:T(8,128)} %get-tuple-element.100.refs_2_), custom_call_target="tpu_custom_call" | custom-call | flops 1 | bytes 1 | tf_op jit(solution)/shard_map/pallas_call | solution.py:203
  61.5 4.0 %all-to-all-start.1 = ((bf16[4,72,2304]{2,1,0:T(8,128)(2,1)}), bf16[4,72,2304]{2,1,0:T(8,128)(2,1)S(1)}, u32[]{:S(2)}, u32[]{:S(2)}) async-start(bf16[4,72,2304]{2,1,0:T(8,128)(2,1)} %bitcast.19), calls=%async_computation.1 | async-start | bytes 2654208 | tf_op jit(solution)/shard_map/all_to_all | solution.py:44
  66.5 3.2 %shard_map.100.refs_0_.refs_2_ = bf16[1152,1280]{1,0:T(8,128)(2,1)} custom-call(bf16[288,1280]{1,0:T(8,128)(2,1)} %bitcast.12.refs_0_, bf16[288,1280]{1,0:T(8,128)(2,1)} %collective-permute-done.4.refs_1_, bf16[144,1280]{1,0:T(8,128)(2,1)} %copy-done.26, bf16[144,1280]{1,0:T(8,128)(2,1)} %collective-permute-done.5.refs_3_, ...), custom_call_target="tpu_custom_call" | custom-call | flops 1 | bytes 1 | tf_op jit(solution)/shard_map/pallas_call | solution.py:203
  69.7 7.7 %collective-permute-done.9.refs_1_.refs_3_ = bf16[128,2304]{1,0:T(8,128)(2,1)} collective-permute-done((bf16[128,2304]{1,0:T(8,128)(2,1)S(1)}, bf16[128,2304]{1,0:T(8,128)(2,1)}, u32[]{:S(2)}, u32[]{:S(2)}) %collective-permute-start.9) | collective-permute-done | bytes 589856 | tf_op jit(solution)/shard_map/ppermute | solution.py:34
  77.4 3.2 %all-to-all-done.1 = bf16[4,72,2304]{2,1,0:T(8,128)(2,1)S(1)} async-done(((bf16[4,72,2304]{2,1,0:T(8,128)(2,1)}), bf16[4,72,2304]{2,1,0:T(8,128)(2,1)S(1)}, u32[]{:S(2)}, u32[]{:S(2)}) %all-to-all-start.1) | async-done | bytes 1327136 | tf_op jit(solution)/shard_map/all_to_all | solution.py:44
  81.3 3.0 %shard_map.101 = (bf16[144,2304]{1,0:T(8,128)(2,1)S(1)}, bf16[144,2304]{1,0:T(8,128)(2,1)S(1)}, bf16[144,2304]{1,0:T(8,128)(2,1)S(1)}, bf16[144,2304]{1,0:T(8,128)(2,1)S(1)}) custom-call(bf16[128,2304]{1,0:T(8,128)(2,1)} %copy-done.31, bf16[128,2304]{1,0:T(8,128)(2,1)} %collective-permute-done.9.refs_1_.refs_3_, ...), custom_call_target="tpu_custom_call" | custom-call | flops 1 | bytes 1 | tf_op jit(solution)/shard_map/pallas_call | solution.py:203
  85.0 2.7 collective-permute-start.13
  88.2 1.6 copy-done.28
  89.8 6.0 %shard_map.102 = (f32[256,7168]{1,0:T(8,128)}, f32[1152,256]{1,0:T(8,128)S(1)}) custom-call(bf16[1152,1280]{1,0:T(8,128)(2,1)} %shard_map.100.refs_0_.refs_2_, bf16[1152,1280]{1,0:T(8,128)(2,1)} %copy-done.28, bf16[1152,1280]{1,0:T(8,128)(2,1)} %shard_map.100.refs_0_.refs_2_, bf16[1152,1280]{1,0:T(8,128)(2,1)} %copy-done.28, bf16[256,7168]{1,0:T(8,128)(2,1)} %bitcast.50, ...), custom_call_target="tpu_custom_call" | custom-call | flops 1 | bytes 1 | tf_op jit(solution)/shard_map/pallas_call | solution.py:203
  95.9 5.6 %shard_map.103 = (f32[256,7168]{1,0:T(8,128)}, f32[1152,256]{1,0:T(8,128)S(1)}) custom-call(bf16[1152,1280]{1,0:T(8,128)(2,1)} %shard_map.100.refs_0_.refs_2_, bf16[1152,1280]{1,0:T(8,128)(2,1)} %copy-done.28, bf16[256,7168]{1,0:T(8,128)(2,1)} %bitcast.51, bf16[2,256,576]{2,1,0:T(8,128)(2,1)} %bitcast.69, ...), custom_call_target="tpu_custom_call", output_to_operand_aliasing={{0}: (4, {})} | custom-call | flops 1 | bytes 1 | tf_op jit(solution)/shard_map/pallas_call | solution.py:203
  101.7 1.6 collective-permute-done.12.refs_1_
  103.3 13.5 %collective-permute-done.13.refs_2_ = bf16[144,2304]{1,0:T(8,128)(2,1)S(1)} collective-permute-done((bf16[144,2304]{1,0:T(8,128)(2,1)S(1)}, bf16[144,2304]{1,0:T(8,128)(2,1)S(1)}, u32[]{:S(2)}, u32[]{:S(2)}) %collective-permute-start.13) | collective-permute-done | bytes 663584 | tf_op jit(solution)/shard_map/ppermute | solution.py:34
  118.9 1.4 shard_map.107.b0_ref
  121.4 1.4 shard_map.104.near_ref
  124.4 1.4 shard_map.108.b1_ref
  127.7 1.4 shard_map.109
  130.1 2.0 shard_map.112
  132.3 2.0 shard_map.110
  134.8 1.3 shard_map.116
  136.3 1.3 shard_map.114
  138.1 2.0 shard_map.113
  140.1 1.3 collective-permute-start.26
  141.5 2.0 shard_map.111
  143.5 2.7 collective-permute-start.22
  147.2 6.6 %shard_map.118.refs_9_ = f32[256,7168]{1,0:T(8,128)} custom-call(bf16[288,2304]{1,0:T(8,128)(2,1)} %bitcast.60, bf16[288,2304]{1,0:T(8,128)(2,1)} %copy-done.9, bf16[288,2304]{1,0:T(8,128)(2,1)} %copy-done.8, bf16[288,2304]{1,0:T(8,128)(2,1)} %copy-done.10, bf16[4,256,288]{2,1,0:T(8,128)(2,1)} %bitcast.68, ...), custom_call_target="tpu_custom_call", output_to_operand_aliasing={{}: (5, {})} | custom-call | flops 1 | bytes 1 | tf_op jit(solution)/shard_map/pallas_call | solution.py:203
  153.7 6.3 %shard_map.119 = f32[256,7168]{1,0:T(8,128)} custom-call(bf16[144,2304]{1,0:T(8,128)(2,1)} %copy-done.11, bf16[144,2304]{1,0:T(8,128)(2,1)} %copy-done.12, bf16[144,2304]{1,0:T(8,128)(2,1)} %copy-done.13, bf16[144,2304]{1,0:T(8,128)(2,1)} %copy-done.14, bf16[144,2304]{1,0:T(8,128)(2,1)} %copy-done.15, ...), custom_call_target="tpu_custom_call", output_to_operand_aliasing={{}: (9, {})} | custom-call | flops 1 | bytes 1 | tf_op jit(solution)/shard_map/pallas_call | solution.py:203
  160.0 4.1 %shard_map.117 = (bf16[288,1280]{1,0:T(8,128)(2,1)}, bf16[288,1280]{1,0:T(8,128)(2,1)}) custom-call(bf16[7168,256]{1,0:T(8,128)(2,1)} %bitcast.34, bf16[7168,256]{1,0:T(8,128)(2,1)} %bitcast.42, bf16[576,1280]{1,0:T(8,128)(2,1)} %copy-done.34, bf16[1152,256]{1,0:T(8,128)(2,1)} %copy-done.6, bf16[1152,256]{1,0:T(8,128)(2,1)} %copy-done.7), custom_call_target="tpu_custom_call" | custom-call | flops 1 | bytes 1 | tf_op jit(solution)/shard_map/pallas_call | solution.py:203
  165.3 3.5 %shard_map.115 = (bf16[144,1280]{1,0:T(8,128)(2,1)S(1)}, bf16[144,1280]{1,0:T(8,128)(2,1)S(1)}, bf16[144,1280]{1,0:T(8,128)(2,1)S(1)}, bf16[144,1280]{1,0:T(8,128)(2,1)S(1)}) custom-call(bf16[7168,256]{1,0:T(8,128)(2,1)} %bitcast.35, bf16[7168,256]{1,0:T(8,128)(2,1)} %bitcast.43, bf16[576,1280]{1,0:T(8,128)(2,1)} %copy-done.33, bf16[1152,256]{1,0:T(8,128)(2,1)} %copy-done.4, ...), custom_call_target="tpu_custom_call" | custom-call | flops 1 | bytes 1 | tf_op jit(solution)/shard_map/pallas_call | solution.py:203
  168.8 5.9 %collective-permute-done.22.refs_1_ = bf16[144,2304]{1,0:T(8,128)(2,1)S(1)} collective-permute-done((bf16[144,2304]{1,0:T(8,128)(2,1)S(1)}, bf16[144,2304]{1,0:T(8,128)(2,1)S(1)}, u32[]{:S(2)}, u32[]{:S(2)}) %collective-permute-start.22) | collective-permute-done | bytes 663584 | tf_op jit(solution)/shard_map/ppermute | solution.py:34
  174.7 3.7 %collective-permute-done.24.refs_3_ = bf16[144,2304]{1,0:T(8,128)(2,1)S(1)} collective-permute-done((bf16[144,2304]{1,0:T(8,128)(2,1)S(1)}, bf16[144,2304]{1,0:T(8,128)(2,1)S(1)}, u32[]{:S(2)}, u32[]{:S(2)}) %collective-permute-start.24) | collective-permute-done | bytes 663584 | tf_op jit(solution)/shard_map/ppermute | solution.py:34
  179.2 4.6 %shard_map.120 = (f32[128,2304]{1,0:T(8,128)}, bf16[128,2304]{1,0:T(8,128)(2,1)}) custom-call(bf16[144,2304]{1,0:T(8,128)(2,1)} %copy-done.22, bf16[144,2304]{1,0:T(8,128)(2,1)} %copy-done.40, bf16[144,2304]{1,0:T(8,128)(2,1)} %copy-done.41, bf16[144,2304]{1,0:T(8,128)(2,1)} %copy-done.42, bf16[4,128,144]{2,1,0:T(8,128)(2,1)} %get-tuple-element.175.refs_4_, ...), custom_call_target="tpu_custom_call" | custom-call | flops 1 | bytes 1 | tf_op jit(solution)/shard_map/pallas_call | solution.py:203
  185.9 1.1 collective-permute-start.33
  187.0 2.7 shard_map.123
  189.7 9.7 %collective-permute-done.29.refs_1_ = bf16[128,2304]{1,0:T(8,128)(2,1)S(1)} collective-permute-done((bf16[128,2304]{1,0:T(8,128)(2,1)}, bf16[128,2304]{1,0:T(8,128)(2,1)S(1)}, u32[]{:S(2)}, u32[]{:S(2)}) %collective-permute-start.29) | collective-permute-done | bytes 589856 | tf_op jit(solution)/shard_map/ppermute | solution.py:34
  200.2 3.3 %shard_map.124 = bf16[128,2304]{1,0:T(8,128)(2,1)} custom-call(f32[128,2304]{1,0:T(8,128)} %get-tuple-element.186.refs_0_, bf16[128,2304]{1,0:T(8,128)(2,1)} %copy-done.44, bf16[128,2304]{1,0:T(8,128)(2,1)} %copy-done.31, bf16[128,2304]{1,0:T(8,128)(2,1)} %collective-permute-done.9.refs_1_.refs_3_, s32[5]{0:T(128)S(1)} %stack.26.at_ref.refs_4_), custom_call_target="tpu_custom_call" | custom-call | flops 1 | bytes 1 | tf_op jit(solution)/shard_map/pallas_call | solution.py:203
  205.4 3.5 %all-to-all-start.2 = ((bf16[4,72,2304]{2,1,0:T(8,128)(2,1)}), bf16[4,72,2304]{2,1,0:T(8,128)(2,1)S(1)}, u32[]{:S(2)}, u32[]{:S(2)}) async-start(bf16[4,72,2304]{2,1,0:T(8,128)(2,1)} %bitcast.22), calls=%async_computation.2 | async-start | bytes 2654208 | tf_op jit(solution)/shard_map/all_to_all | solution.py:44
  210.0 3.8 %collective-permute-start.36 = (bf16[128,2304]{1,0:T(8,128)(2,1)S(1)}, bf16[128,2304]{1,0:T(8,128)(2,1)S(1)}, u32[]{:S(2)}, u32[]{:S(2)}) collective-permute-start(bf16[128,2304]{1,0:T(8,128)(2,1)S(1)} %copy-done.43), channel_id=1, source_target_pairs={{0,114},{1,115},{2,112},{3,113},{4,118},{5,119},{6,116},{7,117},{8... | collective-permute-start | bytes 1769480 | tf_op jit(solution)/shard_map/ppermute | solution.py:26
  213.8 3.6 %shard_map.122 = (f32[128,1280]{1,0:T(8,128)}, bf16[128,1280]{1,0:T(8,128)(2,1)}) custom-call(bf16[144,1280]{1,0:T(8,128)(2,1)} %copy-done.27, bf16[144,1280]{1,0:T(8,128)(2,1)} %copy-done.45, bf16[144,1280]{1,0:T(8,128)(2,1)} %copy-done.46, bf16[144,1280]{1,0:T(8,128)(2,1)} %copy-done.47, bf16[4,128,144]{2,1,0:T(8,128)(2,1)} %get-tuple-element.175.refs_4_, ...), custom_call_target="tpu_custom_call" | custom-call | flops 1 | bytes 1 | tf_op jit(solution)/shard_map/pallas_call | solution.py:203
  217.9 9.5 %all-to-all-done.2 = bf16[4,72,2304]{2,1,0:T(8,128)(2,1)S(1)} async-done(((bf16[4,72,2304]{2,1,0:T(8,128)(2,1)}), bf16[4,72,2304]{2,1,0:T(8,128)(2,1)S(1)}, u32[]{:S(2)}, u32[]{:S(2)}) %all-to-all-start.2) | async-done | bytes 1327136 | tf_op jit(solution)/shard_map/all_to_all | solution.py:44
  228.5 3.0 %shard_map.125 = bf16[128,2304]{1,0:T(8,128)(2,1)} custom-call(bf16[128,4608]{1,0:T(8,128)(2,1)} %collective-permute-done.8.refs_0_, bf16[288,2304]{1,0:T(8,128)(2,1)} %bitcast.71, bf16[128,288]{1,0:T(8,128)(2,1)} %get-tuple-element.189.refs_2_), custom_call_target="tpu_custom_call" | custom-call | flops 1 | bytes 1 | tf_op jit(solution)/shard_map/pallas_call | solution.py:203
  231.4 4.3 %collective-permute-start.37 = (bf16[128,2304]{1,0:T(8,128)(2,1)}, bf16[128,2304]{1,0:T(8,128)(2,1)S(1)}, u32[]{:S(2)}, u32[]{:S(2)}) collective-permute-start(bf16[128,2304]{1,0:T(8,128)(2,1)} %shard_map.125), channel_id=1, source_target_pairs={{0,112},{1,113},{2,114},{3,115},{4,116},{5,117},{6,118},{7,119},{8... | collective-permute-start | bytes 1769480 | tf_op jit(solution)/shard_map/ppermute | solution.py:26
  236.7 2.2 shard_map.121
  238.9 3.5 %all-to-all-start.3 = ((bf16[4,72,1280]{2,1,0:T(8,128)(2,1)}), bf16[4,72,1280]{2,1,0:T(8,128)(2,1)S(1)}, u32[]{:S(2)}, u32[]{:S(2)}) async-start(bf16[4,72,1280]{2,1,0:T(8,128)(2,1)} %bitcast.73), calls=%async_computation.3 | async-start | bytes 1474560 | tf_op jit(solution)/shard_map/all_to_all | solution.py:44
  242.4 2.8 %shard_map.127 = bf16[128,1280]{1,0:T(8,128)(2,1)} custom-call(f32[128,1280]{1,0:T(8,128)} %get-tuple-element.192.refs_0_, bf16[128,1280]{1,0:T(8,128)(2,1)} %collective-permute-done.34.refs_1_, bf16[128,1280]{1,0:T(8,128)(2,1)} %copy-done.37, bf16[128,1280]{1,0:T(8,128)(2,1)} %copy-done.38, s32[5]{0:T(128)S(1)} %stack.26.at_ref.refs_4_), custom_call_target="tpu_custom_call" | custom-call | flops 1 | bytes 1 | tf_op jit(solution)/shard_map/pallas_call | solution.py:203
  245.2 2.8 %collective-permute-done.37.refs_0_ = bf16[128,2304]{1,0:T(8,128)(2,1)S(1)} collective-permute-done((bf16[128,2304]{1,0:T(8,128)(2,1)}, bf16[128,2304]{1,0:T(8,128)(2,1)S(1)}, u32[]{:S(2)}, u32[]{:S(2)}) %collective-permute-start.37) | collective-permute-done | bytes 589856 | tf_op jit(solution)/shard_map/ppermute | solution.py:26
  248.0 10.5 %collective-permute-start.38 = (bf16[128,1280]{1,0:T(8,128)(2,1)}, bf16[128,1280]{1,0:T(8,128)(2,1)S(1)}, u32[]{:S(2)}, u32[]{:S(2)}) collective-permute-start(bf16[128,1280]{1,0:T(8,128)(2,1)} %shard_map.127), channel_id=1, source_target_pairs={{0,114},{1,115},{2,112},{3,113},{4,118},{5,119},{6,116},{7,117},{8... | collective-permute-start | bytes 983048 | tf_op jit(solution)/shard_map/ppermute | solution.py:26
  259.4 2.4 shard_map.126
  261.8 8.4 %collective-permute-start.35 = (bf16[128,1280]{1,0:T(8,128)(2,1)}, bf16[128,1280]{1,0:T(8,128)(2,1)S(1)}, u32[]{:S(2)}, u32[]{:S(2)}) collective-permute-start(bf16[128,1280]{1,0:T(8,128)(2,1)} %shard_map.126), channel_id=1, source_target_pairs={{0,112},{1,113},{2,114},{3,115},{4,116},{5,117},{6,118},{7,119},{8... | collective-permute-start | bytes 983048 | tf_op jit(solution)/shard_map/ppermute | solution.py:26
  272.9 2.2 collective-permute-done.35.refs_0_
  (169 shorter events, 38.5 us)
Async XLA Ops:
  1.8 14.8 %collective-permute-start = (bf16[128,1280]{1,0:T(8,128)(2,1)S(1)}, bf16[128,1280]{1,0:T(8,128)(2,1)S(1)}, u32[]{:S(2)}, u32[]{:S(2)}) collective-permute-start(bf16[128,1280]{1,0:T(8,128)(2,1)S(1)} %get-tuple-element.197), channel_id=1, source_target_pairs={{0,114},{1,115},{2,112},{3,113},{4,118},{5,119},{6,116},{7,117},{8... | collective-permute-start | bytes 983048 | tf_op jit(solution)/shard_map/ppermute | solution.py:26
  9.8 3.6 %collective-permute-start.1 = (f32[4,128]{1,0:T(4,128)S(1)}, f32[4,128]{1,0:T(4,128)S(1)}, u32[]{:S(2)}, u32[]{:S(2)}) collective-permute-start(f32[4,128]{1,0:T(4,128)S(1)} %maximum_bitcast_fusion), channel_id=1, source_target_pairs={{0,2},{1,3},{2,0},{3,1},{4,6},{5,7},{6,4},{7,5},{8,10},{9,11},{10,... | collective-permute-start | bytes 6152 | tf_op jit(solution)/shard_map/ppermute | solution.py:34
  9.8 14.1 %collective-permute-start.2 = (bf16[128,1280]{1,0:T(8,128)(2,1)S(1)}, bf16[128,1280]{1,0:T(8,128)(2,1)S(1)}, u32[]{:S(2)}, u32[]{:S(2)}) collective-permute-start(bf16[128,1280]{1,0:T(8,128)(2,1)S(1)} %get-tuple-element.196), channel_id=1, source_target_pairs={{0,114},{1,115},{2,112},{3,113},{4,118},{5,119},{6,116},{7,117},{8... | collective-permute-start | bytes 983048 | tf_op jit(solution)/shard_map/ppermute | solution.py:26
  19.6 20.1 %all-to-all-start = ((bf16[4,72,1280]{2,1,0:T(8,128)(2,1)}), bf16[4,72,1280]{2,1,0:T(8,128)(2,1)}, u32[]{:S(2)}, u32[]{:S(2)}) async-start(bf16[4,72,1280]{2,1,0:T(8,128)(2,1)} %bitcast.11), calls=%async_computation | async-start | bytes 1474560 | tf_op jit(solution)/shard_map/all_to_all | solution.py:44
  23.9 26.8 %copy-start.23 = (bf16[1,1152,256]{2,1,0:T(8,128)(2,1)S(1)}, bf16[1,1152,256]{2,1,0:T(8,128)(2,1)}, u32[]{:S(2)}) copy-start(bf16[1,1152,256]{2,1,0:T(8,128)(2,1)} %param.11) | copy-start | bytes 1769476
  23.9 26.8 %copy-start.24 = (bf16[1,1152,256]{2,1,0:T(8,128)(2,1)S(1)}, bf16[1,1152,256]{2,1,0:T(8,128)(2,1)}, u32[]{:S(2)}) copy-start(bf16[1,1152,256]{2,1,0:T(8,128)(2,1)} %param.12) | copy-start | bytes 1769476
  23.9 15.9 %copy-start.37 = (bf16[128,1280]{1,0:T(8,128)(2,1)}, bf16[128,1280]{1,0:T(8,128)(2,1)S(1)}, u32[]{:S(2)}) copy-start(bf16[128,1280]{1,0:T(8,128)(2,1)S(1)} %collective-permute-done.2.refs_0_.refs_2_) | copy-start | bytes 983044
  26.4 31.1 %collective-permute-start.8 = (bf16[128,4608]{1,0:T(8,128)(2,1)}, bf16[128,4608]{1,0:T(8,128)(2,1)}, u32[]{:S(2)}, u32[]{:S(2)}) collective-permute-start(bf16[128,4608]{1,0:T(8,128)(2,1)} %slice.41), channel_id=1, source_target_pairs={{0,114},{1,115},{2,112},{3,113},{4,118},{5,119},{6,116},{7,117},{8... | collective-permute-start | bytes 3538952 | tf_op jit(solution)/shard_map/ppermute | solution.py:26
  32.2 7.5 %collective-permute-start.3 = (bf16[128,1280]{1,0:T(8,128)(2,1)S(1)}, bf16[128,1280]{1,0:T(8,128)(2,1)S(1)}, u32[]{:S(2)}, u32[]{:S(2)}) collective-permute-start(bf16[128,1280]{1,0:T(8,128)(2,1)S(1)} %collective-permute-done.2.refs_0_.refs_2_), channel_id=1, source_target_pairs={{0,2},{1,3},{2,0},{3,1},{4,6},{5,7},{6,4},{7,5},{8,10},{9,11},{10,... | collective-permute-start | bytes 983048 | tf_op jit(solution)/shard_map/ppermute | solution.py:34
  39.7 21.8 %collective-permute-start.4 = (bf16[288,1280]{1,0:T(8,128)(2,1)}, bf16[288,1280]{1,0:T(8,128)(2,1)}, u32[]{:S(2)}, u32[]{:S(2)}) collective-permute-start(bf16[288,1280]{1,0:T(8,128)(2,1)} %bitcast.12.refs_0_), channel_id=1, source_target_pairs={{0,2},{1,3},{2,0},{3,1},{4,6},{5,7},{6,4},{7,5},{8,10},{9,11},{10,... | collective-permute-start | bytes 2211848 | tf_op jit(solution)/shard_map/ppermute | solution.py:34
  44.1 17.3 %collective-permute-start.5 = (bf16[144,1280]{1,0:T(8,128)(2,1)}, bf16[144,1280]{1,0:T(8,128)(2,1)}, u32[]{:S(2)}, u32[]{:S(2)}) collective-permute-start(bf16[144,1280]{1,0:T(8,128)(2,1)} %get-tuple-element.107), channel_id=1, source_target_pairs={{0,4},{1,5},{2,6},{3,7},{4,8},{5,9},{6,10},{7,11},{8,12},{9,13},{1... | collective-permute-start | bytes 1105928 | tf_op jit(solution)/shard_map/ppermute | solution.py:34
  46.5 15.0 %collective-permute-start.6 = (bf16[144,1280]{1,0:T(8,128)(2,1)}, bf16[144,1280]{1,0:T(8,128)(2,1)}, u32[]{:S(2)}, u32[]{:S(2)}) collective-permute-start(bf16[144,1280]{1,0:T(8,128)(2,1)} %get-tuple-element.108), channel_id=1, source_target_pairs={{0,8},{1,9},{2,10},{3,11},{4,12},{5,13},{6,14},{7,15},{8,0},{9,1},... | collective-permute-start | bytes 1105928 | tf_op jit(solution)/shard_map/ppermute | solution.py:34
  49.2 12.3 %collective-permute-start.7 = (bf16[144,1280]{1,0:T(8,128)(2,1)S(1)}, bf16[144,1280]{1,0:T(8,128)(2,1)}, u32[]{:S(2)}, u32[]{:S(2)}) collective-permute-start(bf16[144,1280]{1,0:T(8,128)(2,1)S(1)} %get-tuple-element.109), channel_id=1, source_target_pairs={{0,12},{1,13},{2,14},{3,15},{4,0},{5,1},{6,2},{7,3},{8,4},{9,5},{1... | collective-permute-start | bytes 1105928 | tf_op jit(solution)/shard_map/ppermute | solution.py:34
  61.4 8.3 %copy-start.31 = (bf16[128,2304]{1,0:T(8,128)(2,1)}, bf16[128,2304]{1,0:T(8,128)(2,1)S(1)}, u32[]{:S(2)}) copy-start(bf16[128,2304]{1,0:T(8,128)(2,1)S(1)} %slice.54.refs_0_.refs_2_) | copy-start | bytes 1769476
  61.5 19.1 %all-to-all-start.1 = ((bf16[4,72,2304]{2,1,0:T(8,128)(2,1)}), bf16[4,72,2304]{2,1,0:T(8,128)(2,1)S(1)}, u32[]{:S(2)}, u32[]{:S(2)}) async-start(bf16[4,72,2304]{2,1,0:T(8,128)(2,1)} %bitcast.19), calls=%async_computation.1 | async-start | bytes 2654208 | tf_op jit(solution)/shard_map/all_to_all | solution.py:44
  65.4 11.9 %collective-permute-start.9 = (bf16[128,2304]{1,0:T(8,128)(2,1)S(1)}, bf16[128,2304]{1,0:T(8,128)(2,1)}, u32[]{:S(2)}, u32[]{:S(2)}) collective-permute-start(bf16[128,2304]{1,0:T(8,128)(2,1)S(1)} %slice.54.refs_0_.refs_2_), channel_id=1, source_target_pairs={{0,2},{1,3},{2,0},{3,1},{4,6},{5,7},{6,4},{7,5},{8,10},{9,11},{10,... | collective-permute-start | bytes 1769480 | tf_op jit(solution)/shard_map/ppermute | solution.py:34
  80.5 40.9 %copy-start.3 = (bf16[4,72,2304]{2,1,0:T(8,128)(2,1)}, bf16[4,72,2304]{2,1,0:T(8,128)(2,1)S(1)}, u32[]{:S(2)}) copy-start(bf16[4,72,2304]{2,1,0:T(8,128)(2,1)S(1)} %all-to-all-done.1) | copy-start | bytes 3981316
  80.5 7.7 %collective-permute-start.15 = (bf16[1152,1280]{1,0:T(8,128)(2,1)}, bf16[1152,1280]{1,0:T(8,128)(2,1)S(1)}, u32[]{:S(2)}, u32[]{:S(2)}) collective-permute-start(bf16[1152,1280]{1,0:T(8,128)(2,1)} %shard_map.100.refs_0_.refs_2_), channel_id=1, source_target_pairs={{0,1},{1,0},{2,3},{3,2},{4,5},{5,4},{6,7},{7,6},{8,9},{9,8},{10,11... | collective-permute-start | bytes 8847368 | tf_op jit(solution)/shard_map/ppermute | solution.py:34
  80.5 37.0 %collective-permute-start.11 = (bf16[288,2304]{1,0:T(8,128)(2,1)S(1)}, bf16[288,2304]{1,0:T(8,128)(2,1)S(1)}, u32[]{:S(2)}, u32[]{:S(2)}) collective-permute-start(bf16[288,2304]{1,0:T(8,128)(2,1)S(1)} %bitcast.57), channel_id=1, source_target_pairs={{0,2},{1,3},{2,0},{3,1},{4,6},{5,7},{6,4},{7,5},{8,10},{9,11},{10,... | collective-permute-start | bytes 3981320 | tf_op jit(solution)/shard_map/ppermute | solution.py:34
  84.3 34.6 %copy-start.11 = (bf16[144,2304]{1,0:T(8,128)(2,1)}, bf16[144,2304]{1,0:T(8,128)(2,1)S(1)}, u32[]{:S(2)}) copy-start(bf16[144,2304]{1,0:T(8,128)(2,1)S(1)} %get-tuple-element.140.refs_0_) | copy-start | bytes 1990660
  84.3 19.0 %collective-permute-start.12 = (bf16[144,2304]{1,0:T(8,128)(2,1)S(1)}, bf16[144,2304]{1,0:T(8,128)(2,1)S(1)}, u32[]{:S(2)}, u32[]{:S(2)}) collective-permute-start(bf16[144,2304]{1,0:T(8,128)(2,1)S(1)} %get-tuple-element.126), channel_id=1, source_target_pairs={{0,4},{1,5},{2,6},{3,7},{4,8},{5,9},{6,10},{7,11},{8,12},{9,13},{1... | collective-permute-start | bytes 1990664 | tf_op jit(solution)/shard_map/ppermute | solution.py:34
  85.0 31.9 %collective-permute-start.13 = (bf16[144,2304]{1,0:T(8,128)(2,1)S(1)}, bf16[144,2304]{1,0:T(8,128)(2,1)S(1)}, u32[]{:S(2)}, u32[]{:S(2)}) collective-permute-start(bf16[144,2304]{1,0:T(8,128)(2,1)S(1)} %get-tuple-element.127), channel_id=1, source_target_pairs={{0,8},{1,9},{2,10},{3,11},{4,12},{5,13},{6,14},{7,15},{8,0},{9,1},... | collective-permute-start | bytes 1990664 | tf_op jit(solution)/shard_map/ppermute | solution.py:34
  87.7 29.8 %collective-permute-start.14 = (bf16[144,2304]{1,0:T(8,128)(2,1)S(1)}, bf16[144,2304]{1,0:T(8,128)(2,1)S(1)}, u32[]{:S(2)}, u32[]{:S(2)}) collective-permute-start(bf16[144,2304]{1,0:T(8,128)(2,1)S(1)} %get-tuple-element.128), channel_id=1, source_target_pairs={{0,12},{1,13},{2,14},{3,15},{4,0},{5,1},{6,2},{7,3},{8,4},{9,5},{1... | collective-permute-start | bytes 1990664 | tf_op jit(solution)/shard_map/ppermute | solution.py:34
  88.2 30.4 %collective-permute-start.10 = (bf16[288,2304]{1,0:T(8,128)(2,1)S(1)}, bf16[288,2304]{1,0:T(8,128)(2,1)S(1)}, u32[]{:S(2)}, u32[]{:S(2)}) collective-permute-start(bf16[288,2304]{1,0:T(8,128)(2,1)S(1)} %bitcast.58), channel_id=1, source_target_pairs={{0,1},{1,0},{2,3},{3,2},{4,5},{5,4},{6,7},{7,6},{8,9},{9,8},{10,11... | collective-permute-start | bytes 3981320 | tf_op jit(solution)/shard_map/ppermute | solution.py:34
  101.5 17.4 %copy-start.2 = (bf16[1,256,7168]{2,1,0:T(8,128)(2,1)S(1)}, bf16[1,256,7168]{2,1,0:T(8,128)(2,1)}, u32[]{:S(2)}) copy-start(bf16[1,256,7168]{2,1,0:T(8,128)(2,1)} %param.15) | copy-start | bytes 11010052
  103.3 17.0 %copy-start.12 = (bf16[144,2304]{1,0:T(8,128)(2,1)}, bf16[144,2304]{1,0:T(8,128)(2,1)S(1)}, u32[]{:S(2)}) copy-start(bf16[144,2304]{1,0:T(8,128)(2,1)S(1)} %collective-permute-done.12.refs_1_) | copy-start | bytes 1990660
  116.9 3.4 %copy-start.13 = (bf16[144,2304]{1,0:T(8,128)(2,1)}, bf16[144,2304]{1,0:T(8,128)(2,1)S(1)}, u32[]{:S(2)}) copy-start(bf16[144,2304]{1,0:T(8,128)(2,1)S(1)} %collective-permute-done.13.refs_2_) | copy-start | bytes 1990660
  117.5 8.4 %collective-permute-start.16 = (bf16[288,2304]{1,0:T(8,128)(2,1)S(1)}, bf16[288,2304]{1,0:T(8,128)(2,1)S(1)}, u32[]{:S(2)}, u32[]{:S(2)}) collective-permute-start(bf16[288,2304]{1,0:T(8,128)(2,1)S(1)} %collective-permute-done.11.refs_0_.refs_1_), channel_id=1, source_target_pairs={{0,1},{1,0},{2,3},{3,2},{4,5},{5,4},{6,7},{7,6},{8,9},{9,8},{10,11... | collective-permute-start | bytes 3981320 | tf_op jit(solution)/shard_map/ppermute | solution.py:34
  117.6 5.2 %collective-permute-start.17 = (bf16[144,2304]{1,0:T(8,128)(2,1)S(1)}, bf16[144,2304]{1,0:T(8,128)(2,1)S(1)}, u32[]{:S(2)}, u32[]{:S(2)}) collective-permute-start(bf16[144,2304]{1,0:T(8,128)(2,1)S(1)} %get-tuple-element.140.refs_0_), channel_id=1, source_target_pairs={{0,1},{1,0},{2,3},{3,2},{4,5},{5,4},{6,7},{7,6},{8,9},{9,8},{10,11... | collective-permute-start | bytes 1990664 | tf_op jit(solution)/shard_map/ppermute | solution.py:34
  118.1 4.8 %collective-permute-start.18 = (bf16[144,2304]{1,0:T(8,128)(2,1)S(1)}, bf16[144,2304]{1,0:T(8,128)(2,1)S(1)}, u32[]{:S(2)}, u32[]{:S(2)}) collective-permute-start(bf16[144,2304]{1,0:T(8,128)(2,1)S(1)} %collective-permute-done.12.refs_1_), channel_id=1, source_target_pairs={{0,1},{1,0},{2,3},{3,2},{4,5},{5,4},{6,7},{7,6},{8,9},{9,8},{10,11... | collective-permute-start | bytes 1990664 | tf_op jit(solution)/shard_map/ppermute | solution.py:34
  118.4 5.1 %collective-permute-start.19 = (bf16[144,2304]{1,0:T(8,128)(2,1)S(1)}, bf16[144,2304]{1,0:T(8,128)(2,1)S(1)}, u32[]{:S(2)}, u32[]{:S(2)}) collective-permute-start(bf16[144,2304]{1,0:T(8,128)(2,1)S(1)} %collective-permute-done.13.refs_2_), channel_id=1, source_target_pairs={{0,1},{1,0},{2,3},{3,2},{4,5},{5,4},{6,7},{7,6},{8,9},{9,8},{10,11... | collective-permute-start | bytes 1990664 | tf_op jit(solution)/shard_map/ppermute | solution.py:34
  118.6 5.8 %collective-permute-start.20 = (bf16[144,2304]{1,0:T(8,128)(2,1)S(1)}, bf16[144,2304]{1,0:T(8,128)(2,1)S(1)}, u32[]{:S(2)}, u32[]{:S(2)}) collective-permute-start(bf16[144,2304]{1,0:T(8,128)(2,1)S(1)} %collective-permute-done.14.refs_3_), channel_id=1, source_target_pairs={{0,1},{1,0},{2,3},{3,2},{4,5},{5,4},{6,7},{7,6},{8,9},{9,8},{10,11... | collective-permute-start | bytes 1990664 | tf_op jit(solution)/shard_map/ppermute | solution.py:34
  129.1 9.0 %copy-start.6 = (bf16[1152,256]{1,0:T(8,128)(2,1)}, bf16[1152,256]{1,0:T(8,128)(2,1)S(1)}, u32[]{:S(2)}) copy-start(bf16[1152,256]{1,0:T(8,128)(2,1)S(1)} %get-tuple-element.163.refs_2_.refs_3_) | copy-start | bytes 1769476
  129.1 9.0 %copy-start.7 = (bf16[1152,256]{1,0:T(8,128)(2,1)}, bf16[1152,256]{1,0:T(8,128)(2,1)S(1)}, u32[]{:S(2)}) copy-start(bf16[1152,256]{1,0:T(8,128)(2,1)S(1)} %get-tuple-element.164.refs_3_.refs_4_) | copy-start | bytes 1769476
  129.1 12.4 %copy-start.4 = (bf16[1152,256]{1,0:T(8,128)(2,1)}, bf16[1152,256]{1,0:T(8,128)(2,1)S(1)}, u32[]{:S(2)}) copy-start(bf16[1152,256]{1,0:T(8,128)(2,1)S(1)} %get-tuple-element.157.refs_2_.refs_3_) | copy-start | bytes 1769476
  129.1 12.4 %copy-start.5 = (bf16[1152,256]{1,0:T(8,128)(2,1)}, bf16[1152,256]{1,0:T(8,128)(2,1)S(1)}, u32[]{:S(2)}) copy-start(bf16[1152,256]{1,0:T(8,128)(2,1)S(1)} %get-tuple-element.158.refs_3_.refs_4_) | copy-start | bytes 1769476
  132.1 6.0 %collective-permute-start.25 = (bf16[576,2304]{1,0:T(8,128)(2,1)S(1)}, bf16[576,2304]{1,0:T(8,128)(2,1)S(1)}, u32[]{:S(2)}, u32[]{:S(2)}) collective-permute-start(bf16[576,2304]{1,0:T(8,128)(2,1)S(1)} %shard_map.112), channel_id=1, source_target_pairs={{0,1},{1,0},{2,3},{3,2},{4,5},{5,4},{6,7},{7,6},{8,9},{9,8},{10,11... | collective-permute-start | bytes 7962632 | tf_op jit(solution)/shard_map/ppermute | solution.py:34
  134.3 7.1 %collective-permute-start.21 = (bf16[576,2304]{1,0:T(8,128)(2,1)S(1)}, bf16[576,2304]{1,0:T(8,128)(2,1)S(1)}, u32[]{:S(2)}, u32[]{:S(2)}) collective-permute-start(bf16[576,2304]{1,0:T(8,128)(2,1)S(1)} %shard_map.110), channel_id=1, source_target_pairs={{0,1},{1,0},{2,3},{3,2},{4,5},{5,4},{6,7},{7,6},{8,9},{9,8},{10,11... | collective-permute-start | bytes 7962632 | tf_op jit(solution)/shard_map/ppermute | solution.py:34
  136.1 10.1 %collective-permute-start.28 = (bf16[576,1280]{1,0:T(8,128)(2,1)S(1)}, bf16[576,1280]{1,0:T(8,128)(2,1)S(1)}, u32[]{:S(2)}, u32[]{:S(2)}) collective-permute-start(bf16[576,1280]{1,0:T(8,128)(2,1)S(1)} %shard_map.116), channel_id=1, source_target_pairs={{0,1},{1,0},{2,3},{3,2},{4,5},{5,4},{6,7},{7,6},{8,9},{9,8},{10,11... | collective-permute-start | bytes 4423688 | tf_op jit(solution)/shard_map/ppermute | solution.py:34
  137.6 26.5 %collective-permute-start.27 = (bf16[576,1280]{1,0:T(8,128)(2,1)S(1)}, bf16[576,1280]{1,0:T(8,128)(2,1)S(1)}, u32[]{:S(2)}, u32[]{:S(2)}) collective-permute-start(bf16[576,1280]{1,0:T(8,128)(2,1)S(1)} %shard_map.114), channel_id=1, source_target_pairs={{0,1},{1,0},{2,3},{3,2},{4,5},{5,4},{6,7},{7,6},{8,9},{9,8},{10,11... | collective-permute-start | bytes 4423688 | tf_op jit(solution)/shard_map/ppermute | solution.py:34
  140.1 3.4 %copy-start.19 = (bf16[288,2304]{1,0:T(8,128)(2,1)}, bf16[288,2304]{1,0:T(8,128)(2,1)S(1)}, u32[]{:S(2)}) copy-start(bf16[288,2304]{1,0:T(8,128)(2,1)S(1)} %get-tuple-element.184.refs_0_) | copy-start | bytes 3981316
  140.1 38.2 %collective-permute-start.26 = (bf16[288,2304]{1,0:T(8,128)(2,1)S(1)}, bf16[288,2304]{1,0:T(8,128)(2,1)S(1)}, u32[]{:S(2)}, u32[]{:S(2)}) collective-permute-start(bf16[288,2304]{1,0:T(8,128)(2,1)S(1)} %get-tuple-element.155), channel_id=1, source_target_pairs={{0,2},{1,3},{2,0},{3,1},{4,6},{5,7},{6,4},{7,5},{8,10},{9,11},{10,... | collective-permute-start | bytes 3981320 | tf_op jit(solution)/shard_map/ppermute | solution.py:34
  143.5 10.2 %copy-start.22 = (bf16[144,2304]{1,0:T(8,128)(2,1)}, bf16[144,2304]{1,0:T(8,128)(2,1)S(1)}, u32[]{:S(2)}) copy-start(bf16[144,2304]{1,0:T(8,128)(2,1)S(1)} %get-tuple-element.156.refs_0_) | copy-start | bytes 1990660
  143.5 31.1 %collective-permute-start.22 = (bf16[144,2304]{1,0:T(8,128)(2,1)S(1)}, bf16[144,2304]{1,0:T(8,128)(2,1)S(1)}, u32[]{:S(2)}, u32[]{:S(2)}) collective-permute-start(bf16[144,2304]{1,0:T(8,128)(2,1)S(1)} %get-tuple-element.150), channel_id=1, source_target_pairs={{0,12},{1,13},{2,14},{3,15},{4,0},{5,1},{6,2},{7,3},{8,4},{9,5},{1... | collective-permute-start | bytes 1990664 | tf_op jit(solution)/shard_map/ppermute | solution.py:34
  146.2 28.5 %collective-permute-start.23 = (bf16[144,2304]{1,0:T(8,128)(2,1)S(1)}, bf16[144,2304]{1,0:T(8,128)(2,1)S(1)}, u32[]{:S(2)}, u32[]{:S(2)}) collective-permute-start(bf16[144,2304]{1,0:T(8,128)(2,1)S(1)} %get-tuple-element.151), channel_id=1, source_target_pairs={{0,8},{1,9},{2,10},{3,11},{4,12},{5,13},{6,14},{7,15},{8,0},{9,1},... | collective-permute-start | bytes 1990664 | tf_op jit(solution)/shard_map/ppermute | solution.py:34
  146.2 7.5 %copy-start.34 = (bf16[576,1280]{1,0:T(8,128)(2,1)}, bf16[576,1280]{1,0:T(8,128)(2,1)S(1)}, u32[]{:S(2)}) copy-start(bf16[576,1280]{1,0:T(8,128)(2,1)S(1)} %collective-permute-done.28.refs_2_) | copy-start | bytes 4423684
  146.2 32.1 %collective-permute-start.24 = (bf16[144,2304]{1,0:T(8,128)(2,1)S(1)}, bf16[144,2304]{1,0:T(8,128)(2,1)S(1)}, u32[]{:S(2)}, u32[]{:S(2)}) collective-permute-start(bf16[144,2304]{1,0:T(8,128)(2,1)S(1)} %get-tuple-element.152), channel_id=1, source_target_pairs={{0,4},{1,5},{2,6},{3,7},{4,8},{5,9},{6,10},{7,11},{8,12},{9,13},{1... | collective-permute-start | bytes 1990664 | tf_op jit(solution)/shard_map/ppermute | solution.py:34
  168.8 15.1 %copy-start.27 = (bf16[144,1280]{1,0:T(8,128)(2,1)}, bf16[144,1280]{1,0:T(8,128)(2,1)S(1)}, u32[]{:S(2)}) copy-start(bf16[144,1280]{1,0:T(8,128)(2,1)S(1)} %get-tuple-element.179.refs_0_) | copy-start | bytes 1105924
  174.7 3.7 %copy-start.40 = (bf16[144,2304]{1,0:T(8,128)(2,1)}, bf16[144,2304]{1,0:T(8,128)(2,1)S(1)}, u32[]{:S(2)}) copy-start(bf16[144,2304]{1,0:T(8,128)(2,1)S(1)} %collective-permute-done.22.refs_1_) | copy-start | bytes 1990660
  174.7 3.7 %copy-start.41 = (bf16[144,2304]{1,0:T(8,128)(2,1)}, bf16[144,2304]{1,0:T(8,128)(2,1)S(1)}, u32[]{:S(2)}) copy-start(bf16[144,2304]{1,0:T(8,128)(2,1)S(1)} %collective-permute-done.23.refs_2_) | copy-start | bytes 1990660
  178.3 5.5 %copy-start.35 = (bf16[288,2304]{1,0:T(8,128)(2,1)}, bf16[288,2304]{1,0:T(8,128)(2,1)S(1)}, u32[]{:S(2)}) copy-start(bf16[288,2304]{1,0:T(8,128)(2,1)S(1)} %collective-permute-done.26.refs_1_) | copy-start | bytes 3981316
  183.9 15.5 %collective-permute-start.29 = (bf16[128,2304]{1,0:T(8,128)(2,1)}, bf16[128,2304]{1,0:T(8,128)(2,1)S(1)}, u32[]{:S(2)}, u32[]{:S(2)}) collective-permute-start(bf16[128,2304]{1,0:T(8,128)(2,1)} %get-tuple-element.177), channel_id=1, source_target_pairs={{0,2},{1,3},{2,0},{3,1},{4,6},{5,7},{6,4},{7,5},{8,10},{9,11},{10,... | collective-permute-start | bytes 1769480 | tf_op jit(solution)/shard_map/ppermute | solution.py:34
  185.0 18.6 %collective-permute-start.31 = (bf16[144,1280]{1,0:T(8,128)(2,1)S(1)}, bf16[144,1280]{1,0:T(8,128)(2,1)S(1)}, u32[]{:S(2)}, u32[]{:S(2)}) collective-permute-start(bf16[144,1280]{1,0:T(8,128)(2,1)S(1)} %get-tuple-element.180), channel_id=1, source_target_pairs={{0,12},{1,13},{2,14},{3,15},{4,0},{5,1},{6,2},{7,3},{8,4},{9,5},{1... | collective-permute-start | bytes 1105928 | tf_op jit(solution)/shard_map/ppermute | solution.py:34
  185.6 18.0 %collective-permute-start.32 = (bf16[144,1280]{1,0:T(8,128)(2,1)S(1)}, bf16[144,1280]{1,0:T(8,128)(2,1)S(1)}, u32[]{:S(2)}, u32[]{:S(2)}) collective-permute-start(bf16[144,1280]{1,0:T(8,128)(2,1)S(1)} %get-tuple-element.181), channel_id=1, source_target_pairs={{0,8},{1,9},{2,10},{3,11},{4,12},{5,13},{6,14},{7,15},{8,0},{9,1},... | collective-permute-start | bytes 1105928 | tf_op jit(solution)/shard_map/ppermute | solution.py:34
  185.9 18.7 %collective-permute-start.33 = (bf16[144,1280]{1,0:T(8,128)(2,1)S(1)}, bf16[144,1280]{1,0:T(8,128)(2,1)S(1)}, u32[]{:S(2)}, u32[]{:S(2)}) collective-permute-start(bf16[144,1280]{1,0:T(8,128)(2,1)S(1)} %get-tuple-element.182), channel_id=1, source_target_pairs={{0,4},{1,5},{2,6},{3,7},{4,8},{5,9},{6,10},{7,11},{8,12},{9,13},{1... | collective-permute-start | bytes 1105928 | tf_op jit(solution)/shard_map/ppermute | solution.py:34
  203.5 6.5 %copy-start.43 = (bf16[128,2304]{1,0:T(8,128)(2,1)S(1)}, bf16[128,2304]{1,0:T(8,128)(2,1)}, u32[]{:S(2)}) copy-start(bf16[128,2304]{1,0:T(8,128)(2,1)} %shard_map.124) | copy-start | bytes 1769476
  205.4 22.1 %all-to-all-start.2 = ((bf16[4,72,2304]{2,1,0:T(8,128)(2,1)}), bf16[4,72,2304]{2,1,0:T(8,128)(2,1)S(1)}, u32[]{:S(2)}, u32[]{:S(2)}) async-start(bf16[4,72,2304]{2,1,0:T(8,128)(2,1)} %bitcast.22), calls=%async_computation.2 | async-start | bytes 2654208 | tf_op jit(solution)/shard_map/all_to_all | solution.py:44
  208.9 26.9 %collective-permute-start.30 = (bf16[288,1280]{1,0:T(8,128)(2,1)}, bf16[288,1280]{1,0:T(8,128)(2,1)S(1)}, u32[]{:S(2)}, u32[]{:S(2)}) collective-permute-start(bf16[288,1280]{1,0:T(8,128)(2,1)} %get-tuple-element.178), channel_id=1, source_target_pairs={{0,2},{1,3},{2,0},{3,1},{4,6},{5,7},{6,4},{7,5},{8,10},{9,11},{10,... | collective-permute-start | bytes 2211848 | tf_op jit(solution)/shard_map/ppermute | solution.py:34
  210.0 21.4 %collective-permute-start.36 = (bf16[128,2304]{1,0:T(8,128)(2,1)S(1)}, bf16[128,2304]{1,0:T(8,128)(2,1)S(1)}, u32[]{:S(2)}, u32[]{:S(2)}) collective-permute-start(bf16[128,2304]{1,0:T(8,128)(2,1)S(1)} %copy-done.43), channel_id=1, source_target_pairs={{0,114},{1,115},{2,112},{3,113},{4,118},{5,119},{6,116},{7,117},{8... | collective-permute-start | bytes 1769480 | tf_op jit(solution)/shard_map/ppermute | solution.py:26
  217.4 21.5 %collective-permute-start.34 = (bf16[128,1280]{1,0:T(8,128)(2,1)}, bf16[128,1280]{1,0:T(8,128)(2,1)}, u32[]{:S(2)}, u32[]{:S(2)}) collective-permute-start(bf16[128,1280]{1,0:T(8,128)(2,1)} %get-tuple-element.183), channel_id=1, source_target_pairs={{0,2},{1,3},{2,0},{3,1},{4,6},{5,7},{6,4},{7,5},{8,10},{9,11},{10,... | collective-permute-start | bytes 983048 | tf_op jit(solution)/shard_map/ppermute | solution.py:34
  231.4 16.6 %collective-permute-start.37 = (bf16[128,2304]{1,0:T(8,128)(2,1)}, bf16[128,2304]{1,0:T(8,128)(2,1)S(1)}, u32[]{:S(2)}, u32[]{:S(2)}) collective-permute-start(bf16[128,2304]{1,0:T(8,128)(2,1)} %shard_map.125), channel_id=1, source_target_pairs={{0,112},{1,113},{2,114},{3,115},{4,116},{5,117},{6,118},{7,119},{8... | collective-permute-start | bytes 1769480 | tf_op jit(solution)/shard_map/ppermute | solution.py:26
  238.9 19.6 %all-to-all-start.3 = ((bf16[4,72,1280]{2,1,0:T(8,128)(2,1)}), bf16[4,72,1280]{2,1,0:T(8,128)(2,1)S(1)}, u32[]{:S(2)}, u32[]{:S(2)}) async-start(bf16[4,72,1280]{2,1,0:T(8,128)(2,1)} %bitcast.73), calls=%async_computation.3 | async-start | bytes 1474560 | tf_op jit(solution)/shard_map/all_to_all | solution.py:44
  248.0 24.0 %collective-permute-start.38 = (bf16[128,1280]{1,0:T(8,128)(2,1)}, bf16[128,1280]{1,0:T(8,128)(2,1)S(1)}, u32[]{:S(2)}, u32[]{:S(2)}) collective-permute-start(bf16[128,1280]{1,0:T(8,128)(2,1)} %shard_map.127), channel_id=1, source_target_pairs={{0,114},{1,115},{2,112},{3,113},{4,118},{5,119},{6,116},{7,117},{8... | collective-permute-start | bytes 983048 | tf_op jit(solution)/shard_map/ppermute | solution.py:26
  261.8 13.3 %collective-permute-start.35 = (bf16[128,1280]{1,0:T(8,128)(2,1)}, bf16[128,1280]{1,0:T(8,128)(2,1)S(1)}, u32[]{:S(2)}, u32[]{:S(2)}) collective-permute-start(bf16[128,1280]{1,0:T(8,128)(2,1)} %shard_map.126), channel_id=1, source_target_pairs={{0,112},{1,113},{2,114},{3,115},{4,116},{5,117},{6,118},{7,119},{8... | collective-permute-start | bytes 983048 | tf_op jit(solution)/shard_map/ppermute | solution.py:26
  (27 other events, 43.1 us)

commit v3 on v1

--- a/solution.py
+++ b/solution.py
@@ -664,10 +664,11 @@
     keep_b1, send_b1 = combine_b(keep_t, send_t, [part_b1[0]] + back_b1)
     cross_b1 = ep_move(send_b1, dz=1)
     sum_a1 = sum_z(keep_a1, back_a1)
-    cross_b1, back_b0, back_a0, sum_a1 = tie((cross_b1, back_b0, back_a0, sum_a1))
-    own_a1 = x_exchange(sum_a1)
-    up_b1 = section_move(finish_b(at, keep_b1, cross_b1, tok_b1, 0, far_tok1), crossing)
     keep_b0, send_b0 = combine_b(keep_t, send_t, [part_b0[0]] + back_b0)
+    cross_b1, send_b0, back_a0, sum_a1 = tie((cross_b1, send_b0, back_a0, sum_a1))
+    done_b1 = finish_b(at, keep_b1, cross_b1, tok_b1, 0, far_tok1)
+    up_b1 = section_move(done_b1, crossing)
+    own_a1 = x_exchange(release(sum_a1, done_b1))
     cross_b0 = ep_move(send_b0, dz=1)
     sum_a0 = sum_z(keep_a0, back_a0)
     done_b0 = finish_b(at, keep_b0, cross_b0, tok_b0, 0, far_tok0)

time: 268 us -> 270 us (level)
  waiting for transfers between devices: 85.6 us -> 81.4 us
  starting transfers between devices: 62.4 us -> 66.5 us
    ppermute x7, starting transfers between devices: 21.4 us -> 25.6 us  [section_move(): return lax.ppermute(array, ('section', 'ep'), pairs)]
    ppermute x32, waiting for transfers between devices: 70 us -> 65.9 us  [ep_move(): return lax.ppermute(array, 'ep', pairs)]
    unnamed x98 -> x102, local copies, waits for them, and re-layouts: 10.1 us -> 11.6 us
  transfers between devices with their start and end apart: 43 -> 43, of which waited for: 21 -> 21; matrix products, arithmetic and copies ran while one was open for 4% -> 4% of each run, Pallas kernels for 34% -> 33%
where the time goes in v3:
time: 270 us; the launch traced here: 268 us
  Pallas kernels  96.1 us (36%)
  waiting for transfers between devices  81.4 us (30%)
  starting transfers between devices  66.5 us (25%)
  local copies, waits for them, and re-layouts  19.2 us (7%)
  other arithmetic  3.11 us (1%)
    pallas_call x23, Pallas kernels, over_columns(): pl.pallas_call(kernel, in_specs=specs, out_specs=[hbm] * n_out + [pl.Bloc...  74.4 us
    ppermute x32, waiting for transfers between devices, ep_move(): return lax.ppermute(array, 'ep', pairs)  65.9 us
    ppermute x7, starting transfers between devices, section_move(): return lax.ppermute(array, ('section', 'ep'), pairs)  25.6 us
    ppermute x32, starting transfers between devices, ep_move(): return lax.ppermute(array, 'ep', pairs)  24.5 us
    pallas_call x11, Pallas kernels, at_once(): pl.pallas_call(kernel, in_specs=specs, out_specs=[whole(shape) for shape,...  17 us
    all_to_all x4, starting transfers between devices, x_exchange(): lax.all_to_all(blocks, 'ep', 0, 0, axis_index_groups=groups, tiled=True)  16.4 us
    unnamed x102, local copies, waits for them, and re-layouts  11.6 us
    all_to_all x4, waiting for transfers between devices, x_exchange(): lax.all_to_all(blocks, 'ep', 0, 0, axis_index_groups=groups, tiled=True)  7.83 us
  transfers between devices with their start and end apart: 43, of which 21 were waited for; matrix products, arithmetic and copies ran while one was open for 4% of the time, Pallas kernels for 33%

profile of v3, /device:TPU:0, one launch (start us, length us, event | category | flops | bytes accessed | tf_op | source)
XLA Modules:
  0.0 267.9 jit_solution(13230920241993689048)
XLA Ops:
  1.8 6.6 %collective-permute-start = (bf16[128,1280]{1,0:T(8,128)(2,1)S(1)}, bf16[128,1280]{1,0:T(8,128)(2,1)S(1)}, u32[]{:S(2)}, u32[]{:S(2)}) collective-permute-start(bf16[128,1280]{1,0:T(8,128)(2,1)S(1)} %get-tuple-element.201), channel_id=1, source_target_pairs={{0,114},{1,115},{2,112},{3,113},{4,118},{5,119},{6,116},{7,117},{8... | collective-permute-start | bytes 983048 | tf_op jit(solution)/shard_map/ppermute | solution.py:26
  11.0 2.4 collective-permute-done.1
  14.0 2.0 shard_map.95
  17.2 2.3 shard_map.96
  19.6 4.3 %all-to-all-start = ((bf16[4,72,1280]{2,1,0:T(8,128)(2,1)}), bf16[4,72,1280]{2,1,0:T(8,128)(2,1)}, u32[]{:S(2)}, u32[]{:S(2)}) async-start(bf16[4,72,1280]{2,1,0:T(8,128)(2,1)} %bitcast.11), calls=%async_computation | async-start | bytes 1474560 | tf_op jit(solution)/shard_map/all_to_all | solution.py:44
  23.9 2.5 slice.41
  26.4 5.8 %collective-permute-start.8 = (bf16[128,4608]{1,0:T(8,128)(2,1)}, bf16[128,4608]{1,0:T(8,128)(2,1)}, u32[]{:S(2)}, u32[]{:S(2)}) collective-permute-start(bf16[128,4608]{1,0:T(8,128)(2,1)} %slice.41), channel_id=1, source_target_pairs={{0,114},{1,115},{2,112},{3,113},{4,118},{5,119},{6,116},{7,117},{8... | collective-permute-start | bytes 3538952 | tf_op jit(solution)/shard_map/ppermute | solution.py:26
  32.2 7.5 %collective-permute-done.3.refs_1_.refs_3_ = bf16[128,1280]{1,0:T(8,128)(2,1)S(1)} collective-permute-done((bf16[128,1280]{1,0:T(8,128)(2,1)S(1)}, bf16[128,1280]{1,0:T(8,128)(2,1)S(1)}, u32[]{:S(2)}, u32[]{:S(2)}) %collective-permute-start.3) | collective-permute-done | bytes 327712 | tf_op jit(solution)/shard_map/ppermute | solution.py:34
  40.4 2.9 %shard_map.97 = (bf16[144,1280]{1,0:T(8,128)(2,1)S(1)}, bf16[144,1280]{1,0:T(8,128)(2,1)}, bf16[144,1280]{1,0:T(8,128)(2,1)}, bf16[144,1280]{1,0:T(8,128)(2,1)S(1)}) custom-call(bf16[128,1280]{1,0:T(8,128)(2,1)} %copy-done.37, bf16[128,1280]{1,0:T(8,128)(2,1)} %copy-done.38, bf16[288,128]{1,0:T(8,128)(2,1)} %get-tuple-element.105.refs_2_, ...), custom_call_target="tpu_custom_call" | custom-call | flops 1 | bytes 1 | tf_op jit(solution)/shard_map/pallas_call | solution.py:203
  44.1 2.3 collective-permute-start.5
  46.4 2.7 collective-permute-start.6
  49.1 1.5 collective-permute-start.7
  50.6 1.3 shard_map.99
  53.8 1.4 copy.16
  57.5 2.8 %shard_map.98 = bf16[288,2304]{1,0:T(8,128)(2,1)} custom-call(bf16[128,4608]{1,0:T(8,128)(2,1)} %collective-permute-done.8.refs_0_, bf16[288,128]{1,0:T(8,128)(2,1)} %get-tuple-element.101.refs_1_, f32[288,128]{1,0:T(8,128)} %get-tuple-element.102.refs_2_), custom_call_target="tpu_custom_call" | custom-call | flops 1 | bytes 1 | tf_op jit(solution)/shard_map/pallas_call | solution.py:203
  61.5 4.0 %all-to-all-start.1 = ((bf16[4,72,2304]{2,1,0:T(8,128)(2,1)}), bf16[4,72,2304]{2,1,0:T(8,128)(2,1)S(1)}, u32[]{:S(2)}, u32[]{:S(2)}) async-start(bf16[4,72,2304]{2,1,0:T(8,128)(2,1)} %bitcast.19), calls=%async_computation.1 | async-start | bytes 2654208 | tf_op jit(solution)/shard_map/all_to_all | solution.py:44
  66.5 3.2 %shard_map.100.refs_0_.refs_2_ = bf16[1152,1280]{1,0:T(8,128)(2,1)} custom-call(bf16[288,1280]{1,0:T(8,128)(2,1)} %bitcast.12.refs_0_, bf16[288,1280]{1,0:T(8,128)(2,1)} %collective-permute-done.4.refs_1_, bf16[144,1280]{1,0:T(8,128)(2,1)} %copy-done.26, bf16[144,1280]{1,0:T(8,128)(2,1)} %collective-permute-done.5.refs_3_, ...), custom_call_target="tpu_custom_call" | custom-call | flops 1 | bytes 1 | tf_op jit(solution)/shard_map/pallas_call | solution.py:203
  69.7 7.7 %collective-permute-done.9.refs_1_.refs_3_ = bf16[128,2304]{1,0:T(8,128)(2,1)} collective-permute-done((bf16[128,2304]{1,0:T(8,128)(2,1)S(1)}, bf16[128,2304]{1,0:T(8,128)(2,1)}, u32[]{:S(2)}, u32[]{:S(2)}) %collective-permute-start.9) | collective-permute-done | bytes 589856 | tf_op jit(solution)/shard_map/ppermute | solution.py:34
  77.4 3.2 %all-to-all-done.1 = bf16[4,72,2304]{2,1,0:T(8,128)(2,1)S(1)} async-done(((bf16[4,72,2304]{2,1,0:T(8,128)(2,1)}), bf16[4,72,2304]{2,1,0:T(8,128)(2,1)S(1)}, u32[]{:S(2)}, u32[]{:S(2)}) %all-to-all-start.1) | async-done | bytes 1327136 | tf_op jit(solution)/shard_map/all_to_all | solution.py:44
  81.3 3.0 %shard_map.101 = (bf16[144,2304]{1,0:T(8,128)(2,1)S(1)}, bf16[144,2304]{1,0:T(8,128)(2,1)S(1)}, bf16[144,2304]{1,0:T(8,128)(2,1)S(1)}, bf16[144,2304]{1,0:T(8,128)(2,1)S(1)}) custom-call(bf16[128,2304]{1,0:T(8,128)(2,1)} %copy-done.31, bf16[128,2304]{1,0:T(8,128)(2,1)} %collective-permute-done.9.refs_1_.refs_3_, ...), custom_call_target="tpu_custom_call" | custom-call | flops 1 | bytes 1 | tf_op jit(solution)/shard_map/pallas_call | solution.py:203
  85.0 2.7 %collective-permute-start.13 = (bf16[144,2304]{1,0:T(8,128)(2,1)S(1)}, bf16[144,2304]{1,0:T(8,128)(2,1)S(1)}, u32[]{:S(2)}, u32[]{:S(2)}) collective-permute-start(bf16[144,2304]{1,0:T(8,128)(2,1)S(1)} %get-tuple-element.129), channel_id=1, source_target_pairs={{0,8},{1,9},{2,10},{3,11},{4,12},{5,13},{6,14},{7,15},{8,0},{9,1},... | collective-permute-start | bytes 1990664 | tf_op jit(solution)/shard_map/ppermute | solution.py:34
  88.2 1.6 copy-done.28
  89.8 6.0 %shard_map.102 = (f32[256,7168]{1,0:T(8,128)}, f32[1152,256]{1,0:T(8,128)S(1)}) custom-call(bf16[1152,1280]{1,0:T(8,128)(2,1)} %shard_map.100.refs_0_.refs_2_, bf16[1152,1280]{1,0:T(8,128)(2,1)} %copy-done.28, bf16[1152,1280]{1,0:T(8,128)(2,1)} %shard_map.100.refs_0_.refs_2_, bf16[1152,1280]{1,0:T(8,128)(2,1)} %copy-done.28, bf16[256,7168]{1,0:T(8,128)(2,1)} %bitcast.50, ...), custom_call_target="tpu_custom_call" | custom-call | flops 1 | bytes 1 | tf_op jit(solution)/shard_map/pallas_call | solution.py:203
  95.9 5.6 %shard_map.103 = (f32[256,7168]{1,0:T(8,128)}, f32[1152,256]{1,0:T(8,128)S(1)}) custom-call(bf16[1152,1280]{1,0:T(8,128)(2,1)} %shard_map.100.refs_0_.refs_2_, bf16[1152,1280]{1,0:T(8,128)(2,1)} %copy-done.28, bf16[256,7168]{1,0:T(8,128)(2,1)} %bitcast.51, bf16[2,256,576]{2,1,0:T(8,128)(2,1)} %bitcast.69, ...), custom_call_target="tpu_custom_call", output_to_operand_aliasing={{0}: (4, {})} | custom-call | flops 1 | bytes 1 | tf_op jit(solution)/shard_map/pallas_call | solution.py:203
  101.7 1.7 collective-permute-done.12.refs_1_
  103.4 13.5 %collective-permute-done.13.refs_2_ = bf16[144,2304]{1,0:T(8,128)(2,1)S(1)} collective-permute-done((bf16[144,2304]{1,0:T(8,128)(2,1)S(1)}, bf16[144,2304]{1,0:T(8,128)(2,1)S(1)}, u32[]{:S(2)}, u32[]{:S(2)}) %collective-permute-start.13) | collective-permute-done | bytes 663584 | tf_op jit(solution)/shard_map/ppermute | solution.py:34
  118.9 1.4 shard_map.107.b0_ref
  121.4 1.4 shard_map.104.near_ref
  124.5 1.4 shard_map.108.b1_ref
  127.7 1.4 shard_map.109
  130.1 2.0 shard_map.112
  132.4 2.0 shard_map.110
  134.8 1.3 shard_map.116
  136.3 1.3 shard_map.114
  138.1 2.0 shard_map.113
  140.1 1.4 collective-permute-start.26
  141.5 2.0 shard_map.111
  143.6 2.7 %collective-permute-start.22 = (bf16[144,2304]{1,0:T(8,128)(2,1)S(1)}, bf16[144,2304]{1,0:T(8,128)(2,1)S(1)}, u32[]{:S(2)}, u32[]{:S(2)}) collective-permute-start(bf16[144,2304]{1,0:T(8,128)(2,1)S(1)} %get-tuple-element.152), channel_id=1, source_target_pairs={{0,12},{1,13},{2,14},{3,15},{4,0},{5,1},{6,2},{7,3},{8,4},{9,5},{1... | collective-permute-start | bytes 1990664 | tf_op jit(solution)/shard_map/ppermute | solution.py:34
  147.2 6.6 %shard_map.118.refs_9_ = f32[256,7168]{1,0:T(8,128)} custom-call(bf16[288,2304]{1,0:T(8,128)(2,1)} %bitcast.60, bf16[288,2304]{1,0:T(8,128)(2,1)} %copy-done.9, bf16[288,2304]{1,0:T(8,128)(2,1)} %copy-done.8, bf16[288,2304]{1,0:T(8,128)(2,1)} %copy-done.10, bf16[4,256,288]{2,1,0:T(8,128)(2,1)} %bitcast.68, ...), custom_call_target="tpu_custom_call", output_to_operand_aliasing={{}: (5, {})} | custom-call | flops 1 | bytes 1 | tf_op jit(solution)/shard_map/pallas_call | solution.py:203
  153.8 6.3 %shard_map.119 = f32[256,7168]{1,0:T(8,128)} custom-call(bf16[144,2304]{1,0:T(8,128)(2,1)} %copy-done.11, bf16[144,2304]{1,0:T(8,128)(2,1)} %copy-done.12, bf16[144,2304]{1,0:T(8,128)(2,1)} %copy-done.13, bf16[144,2304]{1,0:T(8,128)(2,1)} %copy-done.14, bf16[144,2304]{1,0:T(8,128)(2,1)} %copy-done.15, ...), custom_call_target="tpu_custom_call", output_to_operand_aliasing={{}: (9, {})} | custom-call | flops 1 | bytes 1 | tf_op jit(solution)/shard_map/pallas_call | solution.py:203
  160.1 4.2 %shard_map.117 = (bf16[288,1280]{1,0:T(8,128)(2,1)}, bf16[288,1280]{1,0:T(8,128)(2,1)}) custom-call(bf16[7168,256]{1,0:T(8,128)(2,1)} %bitcast.34, bf16[7168,256]{1,0:T(8,128)(2,1)} %bitcast.42, bf16[576,1280]{1,0:T(8,128)(2,1)} %copy-done.34, bf16[1152,256]{1,0:T(8,128)(2,1)} %copy-done.6, bf16[1152,256]{1,0:T(8,128)(2,1)} %copy-done.7), custom_call_target="tpu_custom_call" | custom-call | flops 1 | bytes 1 | tf_op jit(solution)/shard_map/pallas_call | solution.py:203
  165.4 3.5 %shard_map.115 = (bf16[144,1280]{1,0:T(8,128)(2,1)S(1)}, bf16[144,1280]{1,0:T(8,128)(2,1)S(1)}, bf16[144,1280]{1,0:T(8,128)(2,1)S(1)}, bf16[144,1280]{1,0:T(8,128)(2,1)S(1)}) custom-call(bf16[7168,256]{1,0:T(8,128)(2,1)} %bitcast.35, bf16[7168,256]{1,0:T(8,128)(2,1)} %bitcast.43, bf16[576,1280]{1,0:T(8,128)(2,1)} %copy-done.33, bf16[1152,256]{1,0:T(8,128)(2,1)} %copy-done.4, ...), custom_call_target="tpu_custom_call" | custom-call | flops 1 | bytes 1 | tf_op jit(solution)/shard_map/pallas_call | solution.py:203
  168.9 5.8 %collective-permute-done.22.refs_1_ = bf16[144,2304]{1,0:T(8,128)(2,1)S(1)} collective-permute-done((bf16[144,2304]{1,0:T(8,128)(2,1)S(1)}, bf16[144,2304]{1,0:T(8,128)(2,1)S(1)}, u32[]{:S(2)}, u32[]{:S(2)}) %collective-permute-start.22) | collective-permute-done | bytes 663584 | tf_op jit(solution)/shard_map/ppermute | solution.py:34
  174.7 3.7 %collective-permute-done.24.refs_3_ = bf16[144,2304]{1,0:T(8,128)(2,1)S(1)} collective-permute-done((bf16[144,2304]{1,0:T(8,128)(2,1)S(1)}, bf16[144,2304]{1,0:T(8,128)(2,1)S(1)}, u32[]{:S(2)}, u32[]{:S(2)}) %collective-permute-start.24) | collective-permute-done | bytes 663584 | tf_op jit(solution)/shard_map/ppermute | solution.py:34
  179.5 4.7 %shard_map.121 = (f32[128,2304]{1,0:T(8,128)}, bf16[128,2304]{1,0:T(8,128)(2,1)}) custom-call(bf16[144,2304]{1,0:T(8,128)(2,1)} %copy-done.22, bf16[144,2304]{1,0:T(8,128)(2,1)} %copy-done.40, bf16[144,2304]{1,0:T(8,128)(2,1)} %copy-done.41, bf16[144,2304]{1,0:T(8,128)(2,1)} %copy-done.42, bf16[4,128,144]{2,1,0:T(8,128)(2,1)} %get-tuple-element.176.refs_4_, ...), custom_call_target="tpu_custom_call" | custom-call | flops 1 | bytes 1 | tf_op jit(solution)/shard_map/pallas_call | solution.py:203
  187.3 2.7 %shard_map.122 = bf16[288,2304]{1,0:T(8,128)(2,1)} custom-call(bf16[288,2304]{1,0:T(8,128)(2,1)} %copy-done.19, bf16[288,2304]{1,0:T(8,128)(2,1)} %copy-done.35), custom_call_target="tpu_custom_call" | custom-call | flops 1 | bytes 1 | tf_op jit(solution)/shard_map/pallas_call | solution.py:203
  190.0 6.8 %collective-permute-done.29.refs_1_ = bf16[144,1280]{1,0:T(8,128)(2,1)S(1)} collective-permute-done((bf16[144,1280]{1,0:T(8,128)(2,1)S(1)}, bf16[144,1280]{1,0:T(8,128)(2,1)S(1)}, u32[]{:S(2)}, u32[]{:S(2)}) %collective-permute-start.29) | collective-permute-done | bytes 368672 | tf_op jit(solution)/shard_map/ppermute | solution.py:34
  196.8 2.2 collective-permute-done.30.refs_2_
  199.0 5.7 %collective-permute-done.31.refs_3_ = bf16[144,1280]{1,0:T(8,128)(2,1)S(1)} collective-permute-done((bf16[144,1280]{1,0:T(8,128)(2,1)S(1)}, bf16[144,1280]{1,0:T(8,128)(2,1)S(1)}, u32[]{:S(2)}, u32[]{:S(2)}) %collective-permute-start.31) | collective-permute-done | bytes 368672 | tf_op jit(solution)/shard_map/ppermute | solution.py:34
  205.4 3.6 %shard_map.120 = (f32[128,1280]{1,0:T(8,128)}, bf16[128,1280]{1,0:T(8,128)(2,1)}) custom-call(bf16[144,1280]{1,0:T(8,128)(2,1)} %copy-done.27, bf16[144,1280]{1,0:T(8,128)(2,1)} %copy-done.45, bf16[144,1280]{1,0:T(8,128)(2,1)} %copy-done.46, bf16[144,1280]{1,0:T(8,128)(2,1)} %copy-done.47, bf16[4,128,144]{2,1,0:T(8,128)(2,1)} %get-tuple-element.176.refs_4_, ...), custom_call_target="tpu_custom_call" | custom-call | flops 1 | bytes 1 | tf_op jit(solution)/shard_map/pallas_call | solution.py:203
  210.3 3.3 %shard_map.125 = bf16[128,2304]{1,0:T(8,128)(2,1)} custom-call(f32[128,2304]{1,0:T(8,128)} %get-tuple-element.190.refs_0_, bf16[128,2304]{1,0:T(8,128)(2,1)} %copy-done.43, bf16[128,2304]{1,0:T(8,128)(2,1)} %copy-done.31, bf16[128,2304]{1,0:T(8,128)(2,1)} %collective-permute-done.9.refs_1_.refs_3_, s32[5]{0:T(128)S(1)} %stack.26.at_ref.refs_4_), custom_call_target="tpu_custom_call" | custom-call | flops 1 | bytes 1 | tf_op jit(solution)/shard_map/pallas_call | solution.py:203
  213.7 3.7 %all-to-all-start.3 = ((bf16[4,72,2304]{2,1,0:T(8,128)(2,1)}), bf16[4,72,2304]{2,1,0:T(8,128)(2,1)S(1)}, u32[]{:S(2)}, u32[]{:S(2)}) async-start(bf16[4,72,2304]{2,1,0:T(8,128)(2,1)} %bitcast.24), calls=%async_computation.3 | async-start | bytes 2654208 | tf_op jit(solution)/shard_map/all_to_all | solution.py:44
  217.4 3.9 %collective-permute-start.35 = (bf16[128,2304]{1,0:T(8,128)(2,1)S(1)}, bf16[128,2304]{1,0:T(8,128)(2,1)S(1)}, u32[]{:S(2)}, u32[]{:S(2)}) collective-permute-start(bf16[128,2304]{1,0:T(8,128)(2,1)S(1)} %copy-done.44), channel_id=1, source_target_pairs={{0,114},{1,115},{2,112},{3,113},{4,118},{5,119},{6,116},{7,117},{8... | collective-permute-start | bytes 1769480 | tf_op jit(solution)/shard_map/ppermute | solution.py:26
  221.7 2.2 shard_map.124
  223.9 6.2 %collective-permute-done.34.refs_1_ = bf16[128,1280]{1,0:T(8,128)(2,1)S(1)} collective-permute-done((bf16[128,1280]{1,0:T(8,128)(2,1)S(1)}, bf16[128,1280]{1,0:T(8,128)(2,1)S(1)}, u32[]{:S(2)}, u32[]{:S(2)}) %collective-permute-start.34) | collective-permute-done | bytes 327712 | tf_op jit(solution)/shard_map/ppermute | solution.py:34
  230.8 2.8 %shard_map.123 = bf16[128,1280]{1,0:T(8,128)(2,1)} custom-call(f32[128,1280]{1,0:T(8,128)} %get-tuple-element.178.refs_0_, bf16[128,1280]{1,0:T(8,128)(2,1)} %copy-done.48, bf16[128,1280]{1,0:T(8,128)(2,1)} %copy-done.37, bf16[128,1280]{1,0:T(8,128)(2,1)} %copy-done.38, s32[5]{0:T(128)S(1)} %stack.26.at_ref.refs_4_), custom_call_target="tpu_custom_call" | custom-call | flops 1 | bytes 1 | tf_op jit(solution)/shard_map/pallas_call | solution.py:203
  233.6 5.6 %collective-permute-start.37 = (bf16[128,1280]{1,0:T(8,128)(2,1)}, bf16[128,1280]{1,0:T(8,128)(2,1)S(1)}, u32[]{:S(2)}, u32[]{:S(2)}) collective-permute-start(bf16[128,1280]{1,0:T(8,128)(2,1)} %shard_map.123), channel_id=1, source_target_pairs={{0,114},{1,115},{2,112},{3,113},{4,118},{5,119},{6,116},{7,117},{8... | collective-permute-start | bytes 983048 | tf_op jit(solution)/shard_map/ppermute | solution.py:26
  239.3 4.4 %all-to-all-start.2 = ((bf16[4,72,1280]{2,1,0:T(8,128)(2,1)}), bf16[4,72,1280]{2,1,0:T(8,128)(2,1)S(1)}, u32[]{:S(2)}, u32[]{:S(2)}) async-start(bf16[4,72,1280]{2,1,0:T(8,128)(2,1)} %bitcast.22), calls=%async_computation.2 | async-start | bytes 1474560 | tf_op jit(solution)/shard_map/all_to_all | solution.py:44
  243.7 3.0 %shard_map.127 = bf16[128,2304]{1,0:T(8,128)(2,1)} custom-call(bf16[128,4608]{1,0:T(8,128)(2,1)} %collective-permute-done.8.refs_0_, bf16[288,2304]{1,0:T(8,128)(2,1)} %bitcast.71, bf16[128,288]{1,0:T(8,128)(2,1)} %get-tuple-element.193.refs_2_), custom_call_target="tpu_custom_call" | custom-call | flops 1 | bytes 1 | tf_op jit(solution)/shard_map/pallas_call | solution.py:203
  246.7 2.3 collective-permute-start.38
  249.0 4.6 %all-to-all-done.2 = bf16[4,72,1280]{2,1,0:T(8,128)(2,1)S(1)} async-done(((bf16[4,72,1280]{2,1,0:T(8,128)(2,1)}), bf16[4,72,1280]{2,1,0:T(8,128)(2,1)S(1)}, u32[]{:S(2)}, u32[]{:S(2)}) %all-to-all-start.2) | async-done | bytes 737312 | tf_op jit(solution)/shard_map/all_to_all | solution.py:44
  254.5 2.4 shard_map.126
  258.9 4.3 %collective-permute-done.38.refs_0_ = bf16[128,2304]{1,0:T(8,128)(2,1)S(1)} collective-permute-done((bf16[128,2304]{1,0:T(8,128)(2,1)}, bf16[128,2304]{1,0:T(8,128)(2,1)S(1)}, u32[]{:S(2)}, u32[]{:S(2)}) %collective-permute-start.38) | collective-permute-done | bytes 589856 | tf_op jit(solution)/shard_map/ppermute | solution.py:26
  264.2 2.8 %collective-permute-done.36.refs_0_ = bf16[128,1280]{1,0:T(8,128)(2,1)S(1)} collective-permute-done((bf16[128,1280]{1,0:T(8,128)(2,1)}, bf16[128,1280]{1,0:T(8,128)(2,1)S(1)}, u32[]{:S(2)}, u32[]{:S(2)}) %collective-permute-start.36) | collective-permute-done | bytes 327712 | tf_op jit(solution)/shard_map/ppermute | solution.py:26
  (175 shorter events, 38.4 us)
Async XLA Ops:
  1.8 14.8 %collective-permute-start = (bf16[128,1280]{1,0:T(8,128)(2,1)S(1)}, bf16[128,1280]{1,0:T(8,128)(2,1)S(1)}, u32[]{:S(2)}, u32[]{:S(2)}) collective-permute-start(bf16[128,1280]{1,0:T(8,128)(2,1)S(1)} %get-tuple-element.201), channel_id=1, source_target_pairs={{0,114},{1,115},{2,112},{3,113},{4,118},{5,119},{6,116},{7,117},{8... | collective-permute-start | bytes 983048 | tf_op jit(solution)/shard_map/ppermute | solution.py:26
  9.8 3.6 %collective-permute-start.1 = (f32[4,128]{1,0:T(4,128)S(1)}, f32[4,128]{1,0:T(4,128)S(1)}, u32[]{:S(2)}, u32[]{:S(2)}) collective-permute-start(f32[4,128]{1,0:T(4,128)S(1)} %maximum_bitcast_fusion), channel_id=1, source_target_pairs={{0,2},{1,3},{2,0},{3,1},{4,6},{5,7},{6,4},{7,5},{8,10},{9,11},{10,... | collective-permute-start | bytes 6152 | tf_op jit(solution)/shard_map/ppermute | solution.py:34
  9.8 14.1 %collective-permute-start.2 = (bf16[128,1280]{1,0:T(8,128)(2,1)S(1)}, bf16[128,1280]{1,0:T(8,128)(2,1)S(1)}, u32[]{:S(2)}, u32[]{:S(2)}) collective-permute-start(bf16[128,1280]{1,0:T(8,128)(2,1)S(1)} %get-tuple-element.200), channel_id=1, source_target_pairs={{0,114},{1,115},{2,112},{3,113},{4,118},{5,119},{6,116},{7,117},{8... | collective-permute-start | bytes 983048 | tf_op jit(solution)/shard_map/ppermute | solution.py:26
  19.6 20.1 %all-to-all-start = ((bf16[4,72,1280]{2,1,0:T(8,128)(2,1)}), bf16[4,72,1280]{2,1,0:T(8,128)(2,1)}, u32[]{:S(2)}, u32[]{:S(2)}) async-start(bf16[4,72,1280]{2,1,0:T(8,128)(2,1)} %bitcast.11), calls=%async_computation | async-start | bytes 1474560 | tf_op jit(solution)/shard_map/all_to_all | solution.py:44
  23.9 26.7 %copy-start.23 = (bf16[1,1152,256]{2,1,0:T(8,128)(2,1)S(1)}, bf16[1,1152,256]{2,1,0:T(8,128)(2,1)}, u32[]{:S(2)}) copy-start(bf16[1,1152,256]{2,1,0:T(8,128)(2,1)} %param.11) | copy-start | bytes 1769476
  23.9 26.7 %copy-start.24 = (bf16[1,1152,256]{2,1,0:T(8,128)(2,1)S(1)}, bf16[1,1152,256]{2,1,0:T(8,128)(2,1)}, u32[]{:S(2)}) copy-start(bf16[1,1152,256]{2,1,0:T(8,128)(2,1)} %param.12) | copy-start | bytes 1769476
  23.9 15.9 %copy-start.37 = (bf16[128,1280]{1,0:T(8,128)(2,1)}, bf16[128,1280]{1,0:T(8,128)(2,1)S(1)}, u32[]{:S(2)}) copy-start(bf16[128,1280]{1,0:T(8,128)(2,1)S(1)} %collective-permute-done.2.refs_0_.refs_2_) | copy-start | bytes 983044
  26.4 31.1 %collective-permute-start.8 = (bf16[128,4608]{1,0:T(8,128)(2,1)}, bf16[128,4608]{1,0:T(8,128)(2,1)}, u32[]{:S(2)}, u32[]{:S(2)}) collective-permute-start(bf16[128,4608]{1,0:T(8,128)(2,1)} %slice.41), channel_id=1, source_target_pairs={{0,114},{1,115},{2,112},{3,113},{4,118},{5,119},{6,116},{7,117},{8... | collective-permute-start | bytes 3538952 | tf_op jit(solution)/shard_map/ppermute | solution.py:26
  32.2 7.5 %collective-permute-start.3 = (bf16[128,1280]{1,0:T(8,128)(2,1)S(1)}, bf16[128,1280]{1,0:T(8,128)(2,1)S(1)}, u32[]{:S(2)}, u32[]{:S(2)}) collective-permute-start(bf16[128,1280]{1,0:T(8,128)(2,1)S(1)} %collective-permute-done.2.refs_0_.refs_2_), channel_id=1, source_target_pairs={{0,2},{1,3},{2,0},{3,1},{4,6},{5,7},{6,4},{7,5},{8,10},{9,11},{10,... | collective-permute-start | bytes 983048 | tf_op jit(solution)/shard_map/ppermute | solution.py:34
  39.7 21.8 %collective-permute-start.4 = (bf16[288,1280]{1,0:T(8,128)(2,1)}, bf16[288,1280]{1,0:T(8,128)(2,1)}, u32[]{:S(2)}, u32[]{:S(2)}) collective-permute-start(bf16[288,1280]{1,0:T(8,128)(2,1)} %bitcast.12.refs_0_), channel_id=1, source_target_pairs={{0,2},{1,3},{2,0},{3,1},{4,6},{5,7},{6,4},{7,5},{8,10},{9,11},{10,... | collective-permute-start | bytes 2211848 | tf_op jit(solution)/shard_map/ppermute | solution.py:34
  44.1 17.3 %collective-permute-start.5 = (bf16[144,1280]{1,0:T(8,128)(2,1)}, bf16[144,1280]{1,0:T(8,128)(2,1)}, u32[]{:S(2)}, u32[]{:S(2)}) collective-permute-start(bf16[144,1280]{1,0:T(8,128)(2,1)} %get-tuple-element.109), channel_id=1, source_target_pairs={{0,4},{1,5},{2,6},{3,7},{4,8},{5,9},{6,10},{7,11},{8,12},{9,13},{1... | collective-permute-start | bytes 1105928 | tf_op jit(solution)/shard_map/ppermute | solution.py:34
  46.4 15.0 %collective-permute-start.6 = (bf16[144,1280]{1,0:T(8,128)(2,1)}, bf16[144,1280]{1,0:T(8,128)(2,1)}, u32[]{:S(2)}, u32[]{:S(2)}) collective-permute-start(bf16[144,1280]{1,0:T(8,128)(2,1)} %get-tuple-element.110), channel_id=1, source_target_pairs={{0,8},{1,9},{2,10},{3,11},{4,12},{5,13},{6,14},{7,15},{8,0},{9,1},... | collective-permute-start | bytes 1105928 | tf_op jit(solution)/shard_map/ppermute | solution.py:34
  49.1 12.4 %collective-permute-start.7 = (bf16[144,1280]{1,0:T(8,128)(2,1)S(1)}, bf16[144,1280]{1,0:T(8,128)(2,1)}, u32[]{:S(2)}, u32[]{:S(2)}) collective-permute-start(bf16[144,1280]{1,0:T(8,128)(2,1)S(1)} %get-tuple-element.111), channel_id=1, source_target_pairs={{0,12},{1,13},{2,14},{3,15},{4,0},{5,1},{6,2},{7,3},{8,4},{9,5},{1... | collective-permute-start | bytes 1105928 | tf_op jit(solution)/shard_map/ppermute | solution.py:34
  61.4 8.3 %copy-start.31 = (bf16[128,2304]{1,0:T(8,128)(2,1)}, bf16[128,2304]{1,0:T(8,128)(2,1)S(1)}, u32[]{:S(2)}) copy-start(bf16[128,2304]{1,0:T(8,128)(2,1)S(1)} %slice.54.refs_0_.refs_2_) | copy-start | bytes 1769476
  61.5 19.1 %all-to-all-start.1 = ((bf16[4,72,2304]{2,1,0:T(8,128)(2,1)}), bf16[4,72,2304]{2,1,0:T(8,128)(2,1)S(1)}, u32[]{:S(2)}, u32[]{:S(2)}) async-start(bf16[4,72,2304]{2,1,0:T(8,128)(2,1)} %bitcast.19), calls=%async_computation.1 | async-start | bytes 2654208 | tf_op jit(solution)/shard_map/all_to_all | solution.py:44
  65.4 12.0 %collective-permute-start.9 = (bf16[128,2304]{1,0:T(8,128)(2,1)S(1)}, bf16[128,2304]{1,0:T(8,128)(2,1)}, u32[]{:S(2)}, u32[]{:S(2)}) collective-permute-start(bf16[128,2304]{1,0:T(8,128)(2,1)S(1)} %slice.54.refs_0_.refs_2_), channel_id=1, source_target_pairs={{0,2},{1,3},{2,0},{3,1},{4,6},{5,7},{6,4},{7,5},{8,10},{9,11},{10,... | collective-permute-start | bytes 1769480 | tf_op jit(solution)/shard_map/ppermute | solution.py:34
  80.6 40.8 %copy-start.3 = (bf16[4,72,2304]{2,1,0:T(8,128)(2,1)}, bf16[4,72,2304]{2,1,0:T(8,128)(2,1)S(1)}, u32[]{:S(2)}) copy-start(bf16[4,72,2304]{2,1,0:T(8,128)(2,1)S(1)} %all-to-all-done.1) | copy-start | bytes 3981316
  80.6 7.6 %collective-permute-start.15 = (bf16[1152,1280]{1,0:T(8,128)(2,1)}, bf16[1152,1280]{1,0:T(8,128)(2,1)S(1)}, u32[]{:S(2)}, u32[]{:S(2)}) collective-permute-start(bf16[1152,1280]{1,0:T(8,128)(2,1)} %shard_map.100.refs_0_.refs_2_), channel_id=1, source_target_pairs={{0,1},{1,0},{2,3},{3,2},{4,5},{5,4},{6,7},{7,6},{8,9},{9,8},{10,11... | collective-permute-start | bytes 8847368 | tf_op jit(solution)/shard_map/ppermute | solution.py:34
  80.6 36.9 %collective-permute-start.11 = (bf16[288,2304]{1,0:T(8,128)(2,1)S(1)}, bf16[288,2304]{1,0:T(8,128)(2,1)S(1)}, u32[]{:S(2)}, u32[]{:S(2)}) collective-permute-start(bf16[288,2304]{1,0:T(8,128)(2,1)S(1)} %bitcast.57), channel_id=1, source_target_pairs={{0,2},{1,3},{2,0},{3,1},{4,6},{5,7},{6,4},{7,5},{8,10},{9,11},{10,... | collective-permute-start | bytes 3981320 | tf_op jit(solution)/shard_map/ppermute | solution.py:34
  84.3 34.6 %copy-start.11 = (bf16[144,2304]{1,0:T(8,128)(2,1)}, bf16[144,2304]{1,0:T(8,128)(2,1)S(1)}, u32[]{:S(2)}) copy-start(bf16[144,2304]{1,0:T(8,128)(2,1)S(1)} %get-tuple-element.142.refs_0_) | copy-start | bytes 1990660
  84.4 19.0 %collective-permute-start.12 = (bf16[144,2304]{1,0:T(8,128)(2,1)S(1)}, bf16[144,2304]{1,0:T(8,128)(2,1)S(1)}, u32[]{:S(2)}, u32[]{:S(2)}) collective-permute-start(bf16[144,2304]{1,0:T(8,128)(2,1)S(1)} %get-tuple-element.128), channel_id=1, source_target_pairs={{0,4},{1,5},{2,6},{3,7},{4,8},{5,9},{6,10},{7,11},{8,12},{9,13},{1... | collective-permute-start | bytes 1990664 | tf_op jit(solution)/shard_map/ppermute | solution.py:34
  85.0 31.9 %collective-permute-start.13 = (bf16[144,2304]{1,0:T(8,128)(2,1)S(1)}, bf16[144,2304]{1,0:T(8,128)(2,1)S(1)}, u32[]{:S(2)}, u32[]{:S(2)}) collective-permute-start(bf16[144,2304]{1,0:T(8,128)(2,1)S(1)} %get-tuple-element.129), channel_id=1, source_target_pairs={{0,8},{1,9},{2,10},{3,11},{4,12},{5,13},{6,14},{7,15},{8,0},{9,1},... | collective-permute-start | bytes 1990664 | tf_op jit(solution)/shard_map/ppermute | solution.py:34
  87.7 29.8 %collective-permute-start.14 = (bf16[144,2304]{1,0:T(8,128)(2,1)S(1)}, bf16[144,2304]{1,0:T(8,128)(2,1)S(1)}, u32[]{:S(2)}, u32[]{:S(2)}) collective-permute-start(bf16[144,2304]{1,0:T(8,128)(2,1)S(1)} %get-tuple-element.130), channel_id=1, source_target_pairs={{0,12},{1,13},{2,14},{3,15},{4,0},{5,1},{6,2},{7,3},{8,4},{9,5},{1... | collective-permute-start | bytes 1990664 | tf_op jit(solution)/shard_map/ppermute | solution.py:34
  88.2 30.4 %collective-permute-start.10 = (bf16[288,2304]{1,0:T(8,128)(2,1)S(1)}, bf16[288,2304]{1,0:T(8,128)(2,1)S(1)}, u32[]{:S(2)}, u32[]{:S(2)}) collective-permute-start(bf16[288,2304]{1,0:T(8,128)(2,1)S(1)} %bitcast.58), channel_id=1, source_target_pairs={{0,1},{1,0},{2,3},{3,2},{4,5},{5,4},{6,7},{7,6},{8,9},{9,8},{10,11... | collective-permute-start | bytes 3981320 | tf_op jit(solution)/shard_map/ppermute | solution.py:34
  101.5 17.4 %copy-start.2 = (bf16[1,256,7168]{2,1,0:T(8,128)(2,1)S(1)}, bf16[1,256,7168]{2,1,0:T(8,128)(2,1)}, u32[]{:S(2)}) copy-start(bf16[1,256,7168]{2,1,0:T(8,128)(2,1)} %param.15) | copy-start | bytes 11010052
  103.4 17.0 %copy-start.12 = (bf16[144,2304]{1,0:T(8,128)(2,1)}, bf16[144,2304]{1,0:T(8,128)(2,1)S(1)}, u32[]{:S(2)}) copy-start(bf16[144,2304]{1,0:T(8,128)(2,1)S(1)} %collective-permute-done.12.refs_1_) | copy-start | bytes 1990660
  117.5 8.4 %collective-permute-start.16 = (bf16[288,2304]{1,0:T(8,128)(2,1)S(1)}, bf16[288,2304]{1,0:T(8,128)(2,1)S(1)}, u32[]{:S(2)}, u32[]{:S(2)}) collective-permute-start(bf16[288,2304]{1,0:T(8,128)(2,1)S(1)} %collective-permute-done.11.refs_0_.refs_1_), channel_id=1, source_target_pairs={{0,1},{1,0},{2,3},{3,2},{4,5},{5,4},{6,7},{7,6},{8,9},{9,8},{10,11... | collective-permute-start | bytes 3981320 | tf_op jit(solution)/shard_map/ppermute | solution.py:34
  117.6 5.2 %collective-permute-start.17 = (bf16[144,2304]{1,0:T(8,128)(2,1)S(1)}, bf16[144,2304]{1,0:T(8,128)(2,1)S(1)}, u32[]{:S(2)}, u32[]{:S(2)}) collective-permute-start(bf16[144,2304]{1,0:T(8,128)(2,1)S(1)} %get-tuple-element.142.refs_0_), channel_id=1, source_target_pairs={{0,1},{1,0},{2,3},{3,2},{4,5},{5,4},{6,7},{7,6},{8,9},{9,8},{10,11... | collective-permute-start | bytes 1990664 | tf_op jit(solution)/shard_map/ppermute | solution.py:34
  118.1 4.8 %collective-permute-start.18 = (bf16[144,2304]{1,0:T(8,128)(2,1)S(1)}, bf16[144,2304]{1,0:T(8,128)(2,1)S(1)}, u32[]{:S(2)}, u32[]{:S(2)}) collective-permute-start(bf16[144,2304]{1,0:T(8,128)(2,1)S(1)} %collective-permute-done.12.refs_1_), channel_id=1, source_target_pairs={{0,1},{1,0},{2,3},{3,2},{4,5},{5,4},{6,7},{7,6},{8,9},{9,8},{10,11... | collective-permute-start | bytes 1990664 | tf_op jit(solution)/shard_map/ppermute | solution.py:34
  118.4 5.1 %collective-permute-start.19 = (bf16[144,2304]{1,0:T(8,128)(2,1)S(1)}, bf16[144,2304]{1,0:T(8,128)(2,1)S(1)}, u32[]{:S(2)}, u32[]{:S(2)}) collective-permute-start(bf16[144,2304]{1,0:T(8,128)(2,1)S(1)} %collective-permute-done.13.refs_2_), channel_id=1, source_target_pairs={{0,1},{1,0},{2,3},{3,2},{4,5},{5,4},{6,7},{7,6},{8,9},{9,8},{10,11... | collective-permute-start | bytes 1990664 | tf_op jit(solution)/shard_map/ppermute | solution.py:34
  118.6 5.8 %collective-permute-start.20 = (bf16[144,2304]{1,0:T(8,128)(2,1)S(1)}, bf16[144,2304]{1,0:T(8,128)(2,1)S(1)}, u32[]{:S(2)}, u32[]{:S(2)}) collective-permute-start(bf16[144,2304]{1,0:T(8,128)(2,1)S(1)} %collective-permute-done.14.refs_3_), channel_id=1, source_target_pairs={{0,1},{1,0},{2,3},{3,2},{4,5},{5,4},{6,7},{7,6},{8,9},{9,8},{10,11... | collective-permute-start | bytes 1990664 | tf_op jit(solution)/shard_map/ppermute | solution.py:34
  129.1 9.0 %copy-start.6 = (bf16[1152,256]{1,0:T(8,128)(2,1)}, bf16[1152,256]{1,0:T(8,128)(2,1)S(1)}, u32[]{:S(2)}) copy-start(bf16[1152,256]{1,0:T(8,128)(2,1)S(1)} %get-tuple-element.165.refs_2_.refs_3_) | copy-start | bytes 1769476
  129.1 9.0 %copy-start.7 = (bf16[1152,256]{1,0:T(8,128)(2,1)}, bf16[1152,256]{1,0:T(8,128)(2,1)S(1)}, u32[]{:S(2)}) copy-start(bf16[1152,256]{1,0:T(8,128)(2,1)S(1)} %get-tuple-element.166.refs_3_.refs_4_) | copy-start | bytes 1769476
  129.1 12.4 %copy-start.4 = (bf16[1152,256]{1,0:T(8,128)(2,1)}, bf16[1152,256]{1,0:T(8,128)(2,1)S(1)}, u32[]{:S(2)}) copy-start(bf16[1152,256]{1,0:T(8,128)(2,1)S(1)} %get-tuple-element.159.refs_2_.refs_3_) | copy-start | bytes 1769476
  129.1 12.4 %copy-start.5 = (bf16[1152,256]{1,0:T(8,128)(2,1)}, bf16[1152,256]{1,0:T(8,128)(2,1)S(1)}, u32[]{:S(2)}) copy-start(bf16[1152,256]{1,0:T(8,128)(2,1)S(1)} %get-tuple-element.160.refs_3_.refs_4_) | copy-start | bytes 1769476
  132.1 6.0 %collective-permute-start.25 = (bf16[576,2304]{1,0:T(8,128)(2,1)S(1)}, bf16[576,2304]{1,0:T(8,128)(2,1)S(1)}, u32[]{:S(2)}, u32[]{:S(2)}) collective-permute-start(bf16[576,2304]{1,0:T(8,128)(2,1)S(1)} %shard_map.112), channel_id=1, source_target_pairs={{0,1},{1,0},{2,3},{3,2},{4,5},{5,4},{6,7},{7,6},{8,9},{9,8},{10,11... | collective-permute-start | bytes 7962632 | tf_op jit(solution)/shard_map/ppermute | solution.py:34
  134.4 7.2 %collective-permute-start.21 = (bf16[576,2304]{1,0:T(8,128)(2,1)S(1)}, bf16[576,2304]{1,0:T(8,128)(2,1)S(1)}, u32[]{:S(2)}, u32[]{:S(2)}) collective-permute-start(bf16[576,2304]{1,0:T(8,128)(2,1)S(1)} %shard_map.110), channel_id=1, source_target_pairs={{0,1},{1,0},{2,3},{3,2},{4,5},{5,4},{6,7},{7,6},{8,9},{9,8},{10,11... | collective-permute-start | bytes 7962632 | tf_op jit(solution)/shard_map/ppermute | solution.py:34
  136.1 10.1 %collective-permute-start.28 = (bf16[576,1280]{1,0:T(8,128)(2,1)S(1)}, bf16[576,1280]{1,0:T(8,128)(2,1)S(1)}, u32[]{:S(2)}, u32[]{:S(2)}) collective-permute-start(bf16[576,1280]{1,0:T(8,128)(2,1)S(1)} %shard_map.116), channel_id=1, source_target_pairs={{0,1},{1,0},{2,3},{3,2},{4,5},{5,4},{6,7},{7,6},{8,9},{9,8},{10,11... | collective-permute-start | bytes 4423688 | tf_op jit(solution)/shard_map/ppermute | solution.py:34
  137.6 26.6 %collective-permute-start.27 = (bf16[576,1280]{1,0:T(8,128)(2,1)S(1)}, bf16[576,1280]{1,0:T(8,128)(2,1)S(1)}, u32[]{:S(2)}, u32[]{:S(2)}) collective-permute-start(bf16[576,1280]{1,0:T(8,128)(2,1)S(1)} %shard_map.114), channel_id=1, source_target_pairs={{0,1},{1,0},{2,3},{3,2},{4,5},{5,4},{6,7},{7,6},{8,9},{9,8},{10,11... | collective-permute-start | bytes 4423688 | tf_op jit(solution)/shard_map/ppermute | solution.py:34
  140.1 38.2 %collective-permute-start.26 = (bf16[288,2304]{1,0:T(8,128)(2,1)S(1)}, bf16[288,2304]{1,0:T(8,128)(2,1)S(1)}, u32[]{:S(2)}, u32[]{:S(2)}) collective-permute-start(bf16[288,2304]{1,0:T(8,128)(2,1)S(1)} %get-tuple-element.157), channel_id=1, source_target_pairs={{0,2},{1,3},{2,0},{3,1},{4,6},{5,7},{6,4},{7,5},{8,10},{9,11},{10,... | collective-permute-start | bytes 3981320 | tf_op jit(solution)/shard_map/ppermute | solution.py:34
  143.6 10.2 %copy-start.22 = (bf16[144,2304]{1,0:T(8,128)(2,1)}, bf16[144,2304]{1,0:T(8,128)(2,1)S(1)}, u32[]{:S(2)}) copy-start(bf16[144,2304]{1,0:T(8,128)(2,1)S(1)} %get-tuple-element.158.refs_0_) | copy-start | bytes 1990660
  143.6 31.1 %collective-permute-start.22 = (bf16[144,2304]{1,0:T(8,128)(2,1)S(1)}, bf16[144,2304]{1,0:T(8,128)(2,1)S(1)}, u32[]{:S(2)}, u32[]{:S(2)}) collective-permute-start(bf16[144,2304]{1,0:T(8,128)(2,1)S(1)} %get-tuple-element.152), channel_id=1, source_target_pairs={{0,12},{1,13},{2,14},{3,15},{4,0},{5,1},{6,2},{7,3},{8,4},{9,5},{1... | collective-permute-start | bytes 1990664 | tf_op jit(solution)/shard_map/ppermute | solution.py:34
  146.3 28.5 %collective-permute-start.23 = (bf16[144,2304]{1,0:T(8,128)(2,1)S(1)}, bf16[144,2304]{1,0:T(8,128)(2,1)S(1)}, u32[]{:S(2)}, u32[]{:S(2)}) collective-permute-start(bf16[144,2304]{1,0:T(8,128)(2,1)S(1)} %get-tuple-element.153), channel_id=1, source_target_pairs={{0,8},{1,9},{2,10},{3,11},{4,12},{5,13},{6,14},{7,15},{8,0},{9,1},... | collective-permute-start | bytes 1990664 | tf_op jit(solution)/shard_map/ppermute | solution.py:34
  146.3 7.5 %copy-start.34 = (bf16[576,1280]{1,0:T(8,128)(2,1)}, bf16[576,1280]{1,0:T(8,128)(2,1)S(1)}, u32[]{:S(2)}) copy-start(bf16[576,1280]{1,0:T(8,128)(2,1)S(1)} %collective-permute-done.28.refs_2_) | copy-start | bytes 4423684
  146.3 32.1 %collective-permute-start.24 = (bf16[144,2304]{1,0:T(8,128)(2,1)S(1)}, bf16[144,2304]{1,0:T(8,128)(2,1)S(1)}, u32[]{:S(2)}, u32[]{:S(2)}) collective-permute-start(bf16[144,2304]{1,0:T(8,128)(2,1)S(1)} %get-tuple-element.154), channel_id=1, source_target_pairs={{0,4},{1,5},{2,6},{3,7},{4,8},{5,9},{6,10},{7,11},{8,12},{9,13},{1... | collective-permute-start | bytes 1990664 | tf_op jit(solution)/shard_map/ppermute | solution.py:34
  164.2 14.2 %copy-start.49 = (bf16[288,1280]{1,0:T(8,128)(2,1)S(1)}, bf16[288,1280]{1,0:T(8,128)(2,1)}, u32[]{:S(2)}) copy-start(bf16[288,1280]{1,0:T(8,128)(2,1)} %get-tuple-element.184) | copy-start | bytes 2211844
  168.9 15.3 %copy-start.27 = (bf16[144,1280]{1,0:T(8,128)(2,1)}, bf16[144,1280]{1,0:T(8,128)(2,1)S(1)}, u32[]{:S(2)}) copy-start(bf16[144,1280]{1,0:T(8,128)(2,1)S(1)} %get-tuple-element.172.refs_0_) | copy-start | bytes 1105924
  174.7 4.8 %copy-start.40 = (bf16[144,2304]{1,0:T(8,128)(2,1)}, bf16[144,2304]{1,0:T(8,128)(2,1)S(1)}, u32[]{:S(2)}) copy-start(bf16[144,2304]{1,0:T(8,128)(2,1)S(1)} %collective-permute-done.22.refs_1_) | copy-start | bytes 1990660
  178.4 5.8 %copy-start.35 = (bf16[288,2304]{1,0:T(8,128)(2,1)}, bf16[288,2304]{1,0:T(8,128)(2,1)S(1)}, u32[]{:S(2)}) copy-start(bf16[288,2304]{1,0:T(8,128)(2,1)S(1)} %collective-permute-done.26.refs_1_) | copy-start | bytes 3981316
  178.4 31.1 %collective-permute-start.33 = (bf16[288,1280]{1,0:T(8,128)(2,1)S(1)}, bf16[288,1280]{1,0:T(8,128)(2,1)S(1)}, u32[]{:S(2)}, u32[]{:S(2)}) collective-permute-start(bf16[288,1280]{1,0:T(8,128)(2,1)S(1)} %copy-done.49), channel_id=1, source_target_pairs={{0,2},{1,3},{2,0},{3,1},{4,6},{5,7},{6,4},{7,5},{8,10},{9,11},{10,... | collective-permute-start | bytes 2211848 | tf_op jit(solution)/shard_map/ppermute | solution.py:34
  184.2 25.3 %collective-permute-start.32 = (bf16[128,2304]{1,0:T(8,128)(2,1)}, bf16[128,2304]{1,0:T(8,128)(2,1)S(1)}, u32[]{:S(2)}, u32[]{:S(2)}) collective-permute-start(bf16[128,2304]{1,0:T(8,128)(2,1)} %get-tuple-element.182), channel_id=1, source_target_pairs={{0,2},{1,3},{2,0},{3,1},{4,6},{5,7},{6,4},{7,5},{8,10},{9,11},{10,... | collective-permute-start | bytes 1769480 | tf_op jit(solution)/shard_map/ppermute | solution.py:34
  185.3 11.5 %collective-permute-start.29 = (bf16[144,1280]{1,0:T(8,128)(2,1)S(1)}, bf16[144,1280]{1,0:T(8,128)(2,1)S(1)}, u32[]{:S(2)}, u32[]{:S(2)}) collective-permute-start(bf16[144,1280]{1,0:T(8,128)(2,1)S(1)} %get-tuple-element.173), channel_id=1, source_target_pairs={{0,12},{1,13},{2,14},{3,15},{4,0},{5,1},{6,2},{7,3},{8,4},{9,5},{1... | collective-permute-start | bytes 1105928 | tf_op jit(solution)/shard_map/ppermute | solution.py:34
  185.9 13.1 %collective-permute-start.30 = (bf16[144,1280]{1,0:T(8,128)(2,1)S(1)}, bf16[144,1280]{1,0:T(8,128)(2,1)S(1)}, u32[]{:S(2)}, u32[]{:S(2)}) collective-permute-start(bf16[144,1280]{1,0:T(8,128)(2,1)S(1)} %get-tuple-element.174), channel_id=1, source_target_pairs={{0,8},{1,9},{2,10},{3,11},{4,12},{5,13},{6,14},{7,15},{8,0},{9,1},... | collective-permute-start | bytes 1105928 | tf_op jit(solution)/shard_map/ppermute | solution.py:34
  186.2 18.5 %collective-permute-start.31 = (bf16[144,1280]{1,0:T(8,128)(2,1)S(1)}, bf16[144,1280]{1,0:T(8,128)(2,1)S(1)}, u32[]{:S(2)}, u32[]{:S(2)}) collective-permute-start(bf16[144,1280]{1,0:T(8,128)(2,1)S(1)} %get-tuple-element.175), channel_id=1, source_target_pairs={{0,4},{1,5},{2,6},{3,7},{4,8},{5,9},{6,10},{7,11},{8,12},{9,13},{1... | collective-permute-start | bytes 1105928 | tf_op jit(solution)/shard_map/ppermute | solution.py:34
  196.8 7.8 %copy-start.45 = (bf16[144,1280]{1,0:T(8,128)(2,1)}, bf16[144,1280]{1,0:T(8,128)(2,1)S(1)}, u32[]{:S(2)}) copy-start(bf16[144,1280]{1,0:T(8,128)(2,1)S(1)} %collective-permute-done.29.refs_1_) | copy-start | bytes 1105924
  199.0 5.7 %copy-start.46 = (bf16[144,1280]{1,0:T(8,128)(2,1)}, bf16[144,1280]{1,0:T(8,128)(2,1)S(1)}, u32[]{:S(2)}) copy-start(bf16[144,1280]{1,0:T(8,128)(2,1)S(1)} %collective-permute-done.30.refs_2_) | copy-start | bytes 1105924
  213.7 7.6 %copy-start.50 = (bf16[128,1280]{1,0:T(8,128)(2,1)S(1)}, bf16[128,1280]{1,0:T(8,128)(2,1)}, u32[]{:S(2)}) copy-start(bf16[128,1280]{1,0:T(8,128)(2,1)} %get-tuple-element.187) | copy-start | bytes 983044
  213.7 25.6 %all-to-all-start.3 = ((bf16[4,72,2304]{2,1,0:T(8,128)(2,1)}), bf16[4,72,2304]{2,1,0:T(8,128)(2,1)S(1)}, u32[]{:S(2)}, u32[]{:S(2)}) async-start(bf16[4,72,2304]{2,1,0:T(8,128)(2,1)} %bitcast.24), calls=%async_computation.3 | async-start | bytes 2654208 | tf_op jit(solution)/shard_map/all_to_all | solution.py:44
  217.4 16.3 %collective-permute-start.35 = (bf16[128,2304]{1,0:T(8,128)(2,1)S(1)}, bf16[128,2304]{1,0:T(8,128)(2,1)S(1)}, u32[]{:S(2)}, u32[]{:S(2)}) collective-permute-start(bf16[128,2304]{1,0:T(8,128)(2,1)S(1)} %copy-done.44), channel_id=1, source_target_pairs={{0,114},{1,115},{2,112},{3,113},{4,118},{5,119},{6,116},{7,117},{8... | collective-permute-start | bytes 1769480 | tf_op jit(solution)/shard_map/ppermute | solution.py:26
  221.2 8.8 %collective-permute-start.34 = (bf16[128,1280]{1,0:T(8,128)(2,1)S(1)}, bf16[128,1280]{1,0:T(8,128)(2,1)S(1)}, u32[]{:S(2)}, u32[]{:S(2)}) collective-permute-start(bf16[128,1280]{1,0:T(8,128)(2,1)S(1)} %copy-done.50), channel_id=1, source_target_pairs={{0,2},{1,3},{2,0},{3,1},{4,6},{5,7},{6,4},{7,5},{8,10},{9,11},{10,... | collective-permute-start | bytes 983048 | tf_op jit(solution)/shard_map/ppermute | solution.py:34
  233.6 13.0 %collective-permute-start.37 = (bf16[128,1280]{1,0:T(8,128)(2,1)}, bf16[128,1280]{1,0:T(8,128)(2,1)S(1)}, u32[]{:S(2)}, u32[]{:S(2)}) collective-permute-start(bf16[128,1280]{1,0:T(8,128)(2,1)} %shard_map.123), channel_id=1, source_target_pairs={{0,114},{1,115},{2,112},{3,113},{4,118},{5,119},{6,116},{7,117},{8... | collective-permute-start | bytes 983048 | tf_op jit(solution)/shard_map/ppermute | solution.py:26
  239.3 14.4 %all-to-all-start.2 = ((bf16[4,72,1280]{2,1,0:T(8,128)(2,1)}), bf16[4,72,1280]{2,1,0:T(8,128)(2,1)S(1)}, u32[]{:S(2)}, u32[]{:S(2)}) async-start(bf16[4,72,1280]{2,1,0:T(8,128)(2,1)} %bitcast.22), calls=%async_computation.2 | async-start | bytes 1474560 | tf_op jit(solution)/shard_map/all_to_all | solution.py:44
  246.7 16.5 %collective-permute-start.38 = (bf16[128,2304]{1,0:T(8,128)(2,1)}, bf16[128,2304]{1,0:T(8,128)(2,1)S(1)}, u32[]{:S(2)}, u32[]{:S(2)}) collective-permute-start(bf16[128,2304]{1,0:T(8,128)(2,1)} %shard_map.127), channel_id=1, source_target_pairs={{0,112},{1,113},{2,114},{3,115},{4,116},{5,117},{6,118},{7,119},{8... | collective-permute-start | bytes 1769480 | tf_op jit(solution)/shard_map/ppermute | solution.py:26
  256.9 10.0 %collective-permute-start.36 = (bf16[128,1280]{1,0:T(8,128)(2,1)}, bf16[128,1280]{1,0:T(8,128)(2,1)S(1)}, u32[]{:S(2)}, u32[]{:S(2)}) collective-permute-start(bf16[128,1280]{1,0:T(8,128)(2,1)} %shard_map.126), channel_id=1, source_target_pairs={{0,112},{1,113},{2,114},{3,115},{4,116},{5,117},{6,118},{7,119},{8... | collective-permute-start | bytes 983048 | tf_op jit(solution)/shard_map/ppermute | solution.py:26
  (30 other events, 64.0 us)
